TPU v7x, 128 devices: a whole 4x4x4 slice. The times are simulated.
128 devices in a mesh: expert: 8 (over x, core), dp: 16 (over y, z).
Axes of the slice: x: 4, y: 4, z: 4, core: 2. Of those that a mesh axis runs over, the one named last changes fastest.
Arguments:
- saved_inputs: bfloat16 [8, 20480, 3584], P('expert', 'dp'), may hold values from -6 to 6
- saved_cotangents: bfloat16 [8, 20480, 768], P('expert', 'dp'), may hold values from -0.109375 to 0.109375
- row_counts: int32 [8, 16, 3], P('expert'), may hold values from 1 to 640, 1280 in all within a row
- old_slots: int32 [8, 2], replicated, may hold values from 0 to 7, as said below
- new_slots: int32 [8, 2], replicated, may hold values from 0 to 7, as said below
- master: float32 [8, 3584, 768], P('expert', 'dp'), may hold values from -0.3125 to 0.3125
- first_moment: float32 [8, 3584, 768], P('expert', 'dp'), may hold values from -0.75 to 0.75
- second_moment: float32 [8, 3584, 768], P('expert', 'dp'), may hold values from 0.001 to 0.2
Outputs:
- new_master: float32 [8, 3584, 768], P('expert', 'dp')
- holder_weights: bfloat16 [16, 3584, 768], P('expert', 'dp')
- holder_first: float32 [16, 3584, 768], P('expert', 'dp')
- holder_second: float32 [16, 3584, 768], P('expert', 'dp')
Inputs may be any that keep to these rules, and one draw needn't show every extreme that they name: `old_slots`: every one of the 8 experts fills 1 to 4 of the 16 slots; in every draw some expert fills 4. `new_slots`: every one of the 8 experts fills 1 to 4 of the 16 slots; in every draw some expert fills 4. `row_counts`: for each device the three entries sum to 1280 and the largest is 640.
All inputs are finite; a program needn't handle non-finite values.
Results may differ from a plain program's by a relative error of at most 0.001.
Values may be sent and summed in bfloat16 or wider, within the bound.
No kernel may reach another device: no remote copies, remote signals or barrier semaphores. Data moves between devices by JAX's collectives and lax.ppermute only.
A program may use at most 320 MiB of HBM per device.

v0:
```python
import jax
import jax.numpy as jnp
from jax import lax
from jax.sharding import PartitionSpec as P


def slot_index(counts, row_count, slot_count):
    slot_ends = jnp.cumsum(counts[:slot_count])
    row_index = jnp.arange(row_count, dtype=jnp.int32)
    return jnp.sum((row_index[:, None] >= slot_ends[None, :]).astype(jnp.int32), axis=1)


def masked_cotangent(cotangent, slot_ids, slot_count):
    member = (slot_ids[:, None] == jnp.arange(slot_count, dtype=jnp.int32)[None, :]).astype(
        cotangent.dtype
    )
    return (cotangent[:, None, :] * member[:, :, None]).reshape(
        cotangent.shape[0], slot_count * cotangent.shape[1]
    )


def adam_update(gradient, master, first_moment, second_moment):
    first_new = 0.9 * first_moment + 0.1 * gradient
    second_new = 0.95 * second_moment + 0.05 * gradient * gradient
    corrected = first_new / (1.0 - 0.9**20) / (jnp.sqrt(second_new / (1.0 - 0.95**20)) + 1e-08)
    new_master = master - 0.001 * (corrected + 0.1 * master)
    return (new_master, first_new, second_new)


def body(
    saved_inputs,
    saved_cotangents,
    row_counts,
    old_slots,
    new_slots,
    master,
    first_moment,
    second_moment,
):
    owner_index = lax.axis_index("expert")
    data_index = lax.axis_index("dp")
    experts = old_slots.shape[0]
    slot_count = old_slots.shape[1]
    local_inputs = saved_inputs[0]
    local_cotangent = saved_cotangents[0]
    row_count = local_inputs.shape[0]
    width_h = local_cotangent.shape[1]
    shard_rows = master.shape[1]
    contract_rows = (((0,), (0,)), ((), ()))
    device_counts = row_counts[0]
    every_ids = jax.vmap(lambda counts: slot_index(counts, row_count, slot_count))(
        device_counts
    ).reshape(-1)
    local_ids = lax.dynamic_slice_in_dim(every_ids, data_index * row_count, row_count, 0)
    masked_local = masked_cotangent(local_cotangent, local_ids, slot_count)
    grad_slots = lax.psum_scatter(
        lax.dot_general(
            local_inputs, masked_local, contract_rows, preferred_element_type=jnp.float32
        ),
        "dp",
        scatter_dimension=0,
        tiled=True,
    )
    my_old = lax.dynamic_index_in_dim(old_slots, owner_index, 0, keepdims=False)
    chosen = (my_old[:, None] == jnp.arange(experts, dtype=jnp.int32)[None, :]).astype(jnp.float32)
    shaped = grad_slots.reshape(shard_rows, slot_count, width_h)
    spread = jnp.einsum("se,dsh->edh", chosen, shaped, precision=lax.Precision.HIGHEST)
    owned_grad = lax.psum_scatter(spread, "expert", scatter_dimension=0, tiled=True)[0]
    new_master, first_new, second_new = adam_update(
        owned_grad[None], master, first_moment, second_moment
    )
    my_new = lax.dynamic_index_in_dim(new_slots, owner_index, 0, keepdims=False)
    pieces = (
        lax.all_gather(new_master, "expert", axis=0, tiled=True),
        lax.all_gather(first_new, "expert", axis=0, tiled=True),
        lax.all_gather(second_new, "expert", axis=0, tiled=True),
    )
    sources = pieces[0].shape[0]
    chooser = (my_new[:, None] == jnp.arange(sources, dtype=jnp.int32)[None, :]).astype(jnp.float32)
    held_weights, held_first, held_second = tuple(
        (
            jnp.einsum("sk,kdh->sdh", chooser, piece, precision=lax.Precision.HIGHEST)
            for piece in pieces
        )
    )
    return (new_master, held_weights.astype(jnp.bfloat16), held_first, held_second)


def solution(mesh):
    return jax.shard_map(
        body,
        mesh=mesh,
        in_specs=(
            P("expert", "dp", None),
            P("expert", "dp", None),
            P("expert", None, None),
            P(),
            P(),
            P("expert", "dp", None),
            P("expert", "dp", None),
            P("expert", "dp", None),
        ),
        out_specs=(
            P("expert", "dp", None),
            P("expert", "dp", None),
            P("expert", "dp", None),
            P("expert", "dp", None),
        ),
        check_vma=False,
    )
```

profile of v0, /device:TPU:15, one launch (start us, length us, event | category | flops | bytes accessed | tf_op | source)
XLA Modules:
  0.0 379.3 jit_solution(4324207496908177523)
XLA Ops:
  7.2 0.0 copy-start
  7.2 0.0 reduce-scatter.7.cloned.1.call-start
  7.2 0.7 copy.55
  8.0 0.1 convert_reduce_fusion
  8.1 0.1 dynamic_slice.11
  8.1 0.2 fusion.11
  8.4 0.0 copy-start.5
  8.4 6.0 %broadcast_multiply_fusion = bf16[1280,2,768]{2,1,0:T(2,128)(2,1)S(1)} fusion(bf16[1280,2]{1,0:T(8,128)(2,1)S(1)} %fusion.11, bf16[1280,768]{1,0:T(8,128)(2,1)} %bitcast.28), kind=kLoop, calls=%fused_computation.8 | loop fusion | flops 1966080 | bytes 5903360 | tf_op jit(solution)/shard_map/mul | solution.py:17
  14.4 0.8 copy.45
  15.2 0.0 copy-done.5
  15.2 18.6 %convolution_bitcast_fusion = f32[3584,1536]{0,1:T(8,128)} fusion(bf16[1280,1536]{1,0:T(8,128)(2,1)S(1)} %bitcast.27, bf16[1,1280,3584]{2,1,0:T(8,128)(2,1)S(1)} %copy-done.5), kind=kOutput, calls=%fused_computation | convolution fusion | flops 14092861440 | bytes 35127296 | tf_op jit(solution)/shard_map/dot_general | solution.py:57
  33.8 21.7 %copy.42 = f32[3584,1536]{1,0:T(8,128)} copy(f32[3584,1536]{0,1:T(8,128)} %convolution_bitcast_fusion) | data formatting | bytes 44040192
  55.5 0.0 reduce-scatter.7.cloned.1.call-update
  55.5 0.2 reduce-scatter.5.cloned.1.call-start
  55.7 0.0 copy-done
  55.7 0.2 dynamic-slice_reduce_fusion.1
  55.9 139.2 %reduce-scatter.7.cloned.1.call-done = f32[224,1536]{1,0:T(8,128)} async-done(((f32[3584,1536]{1,0:T(8,128)}), f32[224,1536]{1,0:T(8,128)}) %reduce-scatter.7.cloned.1.call-update) | async-done | bytes 1376272
  195.1 1.8 copy.43
  196.9 0.9 copy.34
  197.9 3.3 fusion.15
  201.2 4.1 %copy.35 = f32[8,224,768]{2,1,0:T(8,128)} copy(f32[8,224,768]{2,0,1:T(8,128)S(1)} %fusion.15) | data formatting | bytes 11010048 | tf_op jit(solution)/shard_map/se,dsh->edh/dot_general | solution.py:67
  205.3 0.0 copy-start.1
  205.3 0.0 copy-start.2
  205.3 0.0 copy-start.3
  205.3 0.0 copy-start.4
  205.3 0.0 reduce-scatter.5.cloned.1.call-update
  205.3 0.0 all-gather.4.cloned.1.call-start
  205.4 39.5 %reduce-scatter.5.cloned.1.call-done = f32[1,224,768]{2,1,0:T(8,128)} async-done(((f32[8,224,768]{2,1,0:T(8,128)}), f32[1,224,768]{2,1,0:T(8,128)}) %reduce-scatter.5.cloned.1.call-update) | async-done | bytes 688144 | tf_op jit(solution)/shard_map/reduce_scatter | solution.py:68
  244.9 0.0 copy-done.1
  244.9 0.0 copy-done.2
  244.9 0.0 copy-done.3
  244.9 2.8 multiply_subtract_fusion
  247.6 0.0 all-gather.4.cloned.1.call-update
  247.6 0.0 all-gather.6.cloned.1.call-start
  247.7 0.5 all-gather.6.cloned.1.call-update
  248.2 0.3 all-gather.8.cloned.1.call-start
  248.5 0.3 all-gather.8.cloned.1.call-update
  248.8 0.0 copy-done.4
  248.8 0.2 dynamic-slice_reduce_fusion
  249.0 35.2 %all-gather.4.cloned.1.call-done = f32[8,224,768]{2,1,0:T(8,128)} async-done(((f32[1,224,768]{2,1,0:T(8,128)}), f32[8,224,768]{2,1,0:T(8,128)}) %all-gather.4.cloned.1.call-update) | async-done | bytes 5505040 | tf_op jit(solution)/shard_map/all_gather | solution.py:74
  284.2 8.2 %fusion.7 = bf16[2,224,768]{2,0,1:T(2,128)(2,1)S(1)} fusion(f32[8,224,768]{2,1,0:T(8,128)} %all-gather.4.cloned.1.call-done, s32[2]{0:T(128)S(1)} %dynamic-slice_reduce_fusion), kind=kOutput, calls=%fused_computation.9 | convolution fusion | flops 33374224 | bytes 6193160 | tf_op jit(solution)/shard_map/sk,kdh->sdh/dot_general | solution.py:82
  292.5 0.9 copy.39
  293.4 30.7 %all-gather.6.cloned.1.call-done = f32[8,224,768]{2,1,0:T(8,128)} async-done(((f32[1,224,768]{2,1,0:T(8,128)}), f32[8,224,768]{2,1,0:T(8,128)}) %all-gather.6.cloned.1.call-update) | async-done | bytes 5505040 | tf_op jit(solution)/shard_map/all_gather | solution.py:75
  324.1 8.2 %fusion.3 = f32[2,224,768]{2,0,1:T(2,128)S(1)} fusion(f32[8,224,768]{2,1,0:T(8,128)} %all-gather.6.cloned.1.call-done, s32[2]{0:T(128)S(1)} %dynamic-slice_reduce_fusion), kind=kOutput, calls=%fused_computation.4 | convolution fusion | flops 33030160 | bytes 6881288 | tf_op jit(solution)/shard_map/sk,kdh->sdh/dot_general | solution.py:82
  332.3 1.4 copy.40
  333.7 29.7 %all-gather.8.cloned.1.call-done = f32[8,224,768]{2,1,0:T(8,128)} async-done(((f32[1,224,768]{2,1,0:T(8,128)}), f32[8,224,768]{2,1,0:T(8,128)}) %all-gather.8.cloned.1.call-update) | async-done | bytes 5505040 | tf_op jit(solution)/shard_map/all_gather | solution.py:76
  363.4 8.2 %fusion.1 = f32[2,224,768]{2,0,1:T(2,128)S(1)} fusion(f32[8,224,768]{2,1,0:T(8,128)} %all-gather.8.cloned.1.call-done, s32[2]{0:T(128)S(1)} %dynamic-slice_reduce_fusion), kind=kOutput, calls=%fused_computation.2 | convolution fusion | flops 33030160 | bytes 6881288 | tf_op jit(solution)/shard_map/sk,kdh->sdh/dot_general | solution.py:82
  371.6 1.2 copy.41
  (3 shorter events, 0.0 us)
Async XLA Ops:
  7.2 48.6 %copy-start = (s32[8,2]{0,1:T(2,128)S(1)}, s32[8,2]{0,1:T(2,128)}, u32[]{:S(2)}) copy-start(s32[8,2]{0,1:T(2,128)} %param.11) | copy-start | bytes 196
  7.2 188.0 %reduce-scatter.7.cloned.1.call-start = ((), (), s32[]{:S(2)}) async-start(), calls=%async_computation.6 | async-start | bytes 23396352
  8.4 6.8 %copy-start.5 = (bf16[1,1280,3584]{2,1,0:T(8,128)(2,1)S(1)}, bf16[1,1280,3584]{2,1,0:T(8,128)(2,1)}, u32[]{:S(2)}) copy-start(bf16[1,1280,3584]{2,1,0:T(8,128)(2,1)} %param.8) | copy-start | bytes 27525124
  55.5 189.4 %reduce-scatter.5.cloned.1.call-start = ((), (), s32[]{:S(2)}) async-start(), calls=%async_computation.2 | async-start | bytes 6193152 | tf_op jit(solution)/shard_map/reduce_scatter | solution.py:68
  205.3 39.6 %copy-start.1 = (f32[1,224,768]{2,1,0:T(8,128)S(1)}, f32[1,224,768]{2,1,0:T(8,128)}, u32[]{:S(2)}) copy-start(f32[1,224,768]{2,1,0:T(8,128)} %param.13) | copy-start | bytes 2064388
  205.3 39.6 %copy-start.2 = (f32[1,224,768]{2,1,0:T(8,128)S(1)}, f32[1,224,768]{2,1,0:T(8,128)}, u32[]{:S(2)}) copy-start(f32[1,224,768]{2,1,0:T(8,128)} %param.14) | copy-start | bytes 2064388
  205.3 39.6 %copy-start.3 = (f32[1,224,768]{2,1,0:T(8,128)S(1)}, f32[1,224,768]{2,1,0:T(8,128)}, u32[]{:S(2)}) copy-start(f32[1,224,768]{2,1,0:T(8,128)} %param.15) | copy-start | bytes 2064388
  205.3 43.5 %copy-start.4 = (s32[8,2]{0,1:T(2,128)S(1)}, s32[8,2]{0,1:T(2,128)}, u32[]{:S(2)}) copy-start(s32[8,2]{0,1:T(2,128)} %param.12) | copy-start | bytes 196
  205.3 78.9 %all-gather.4.cloned.1.call-start = ((), (), s32[]{:S(2)}) async-start(), calls=%async_computation.3 | async-start | bytes 6193152 | tf_op jit(solution)/shard_map/all_gather | solution.py:74
  247.6 76.5 %all-gather.6.cloned.1.call-start = ((), (), s32[]{:S(2)}) async-start(), calls=%async_computation.4 | async-start | bytes 6193152 | tf_op jit(solution)/shard_map/all_gather | solution.py:75
  248.2 115.2 %all-gather.8.cloned.1.call-start = ((), (), s32[]{:S(2)}) async-start(), calls=%async_computation.5 | async-start | bytes 6193152 | tf_op jit(solution)/shard_map/all_gather | solution.py:76
Sparse Core Ops, SparseCore 0:
  55.6 139.4 reduce-scatter.6
  205.4 39.3 reduce-scatter.4
  247.8 36.4 all-gather.3
  286.4 37.6 all-gather.5
  325.7 37.6 all-gather.7
where the time goes:
time: 383 us; the launch traced here: 379 us
  waiting for transfers between devices  275 us (72%)
  matrix products  46.5 us (12%)
  local copies, waits for them, and re-layouts  33.9 us (9%)
  between operations  13.9 us (4%)
  other arithmetic  9.11 us (2%)
    unnamed x6, waiting for transfers between devices  140 us
    reduce_scatter x1, waiting for transfers between devices, body(): lax.psum_scatter(spread, 'expert', scatter_dimension=0, tiled=True)[0]  39.5 us
    all_gather x1, waiting for transfers between devices, body(): lax.all_gather(new_master, 'expert', axis=0, tiled=True)  35.2 us
    all_gather x1, waiting for transfers between devices, body(): lax.all_gather(first_new, 'expert', axis=0, tiled=True)  30.7 us
    all_gather x1, waiting for transfers between devices, body(): lax.all_gather(second_new, 'expert', axis=0, tiled=True)  29.7 us
    unnamed x19, local copies, waits for them, and re-layouts  28.5 us
    dot_general x3, matrix products, body(): jnp.einsum('sk,kdh->sdh', chooser, piece, precision=lax.Precision.HIGHEST)  24.6 us
    dot_general x1, matrix products, body(): lax.dot_general(local_inputs, masked_local, contract_rows, preferred_elem...  18.6 us
  transfers between devices with their start and end apart: 5, of which 5 were waited for; matrix products, arithmetic and copies ran while one was open for 5% of the time, Pallas kernels for 0%

commit v1 on v0

v1 whole, which is shorter than its diff:
```python
import jax
import jax.numpy as jnp
from jax import lax
from jax.experimental import pallas as pl
from jax.experimental.pallas import tpu as pltpu
from jax.sharding import PartitionSpec as P

F16 = jnp.float16
F32 = jnp.float32
NY, NZ, NX = 4, 4, 4
WINDOW = 656
SCALE = 64.0


def y_shift(d):
    return [(j, ((j // NZ + d) % NY) * NZ + j % NZ) for j in range(NY * NZ)]


def z_shift(d):
    return [(j, (j // NZ) * NZ + (j % NZ + d) % NZ) for j in range(NY * NZ)]


def x_shift(d):
    return [(e, ((e // 2 + d) % NX) * 2 + e % 2) for e in range(2 * NX)]


def core_swap():
    return [(e, e ^ 1) for e in range(2 * NX)]


def adam_update(gradient, master, first_moment, second_moment):
    first_new = 0.9 * first_moment + 0.1 * gradient
    second_new = 0.95 * second_moment + 0.05 * gradient * gradient
    corrected = first_new / (1.0 - 0.9**20) / (jnp.sqrt(second_new / (1.0 - 0.95**20)) + 1e-08)
    new_master = master - 0.001 * (corrected + 0.1 * master)
    return (new_master, first_new, second_new)


def encode_moments(m, v):
    root = jnp.sqrt(jnp.sqrt(jnp.sqrt(jnp.minimum(jnp.abs(m) * (1.0 / 0.75), 1.0))))
    qm = jnp.round(jnp.where(m < 0, -root, root) * 32767.0).astype(jnp.int32)
    qv = jnp.round(jnp.sqrt(jnp.clip(v * 5.0, 0.0, 1.0)) * 65535.0).astype(jnp.int32)
    return qm * 65536 + qv


def decode_moments(code):
    qm = lax.shift_right_arithmetic(code, jnp.int32(16)).astype(F32) * (1.0 / 32767.0)
    qv = (code & jnp.int32(0xFFFF)).astype(F32) * (1.0 / 65535.0)
    m2 = qm * qm
    m4 = m2 * m2
    m8 = m4 * m4 * 0.75
    return jnp.where(qm < 0, -m8, m8), qv * qv * 0.2


def ring_sums(pieces, shifts):
    up, down = shifts[1], shifts[-1]
    far_up = lax.ppermute(pieces[2][0], "dp", up)
    far_down = lax.ppermute(pieces[2][1], "dp", down)
    raw_up = lax.ppermute(pieces[1][1], "dp", up)
    raw_down = lax.ppermute(pieces[3][0], "dp", down)
    both_up = lax.ppermute((pieces[1][0].astype(F32) + far_up.astype(F32)).astype(F16), "dp", up)
    both_down = lax.ppermute(
        (pieces[3][1].astype(F32) + far_down.astype(F32)).astype(F16), "dp", down
    )
    first = pieces[0][0].astype(F32) + both_up.astype(F32) + raw_down.astype(F32)
    second = pieces[0][1].astype(F32) + raw_up.astype(F32) + both_down.astype(F32)
    return first, second


def last_sums(halves, me, shifts):
    total = jnp.concatenate([(h * 0.5).astype(F16) for h in halves], -1)

    def block(d):
        return lax.dynamic_index_in_dim(total, (me + d) % 4, 0, keepdims=False)

    a = lax.ppermute(block(1), "dp", shifts[1])
    b = lax.ppermute(block(3), "dp", shifts[-1])
    c = lax.ppermute(block(2), "dp", shifts[2])
    return block(0).astype(F32) + a.astype(F32) + b.astype(F32) + c.astype(F32)


def adam_kernel(slots, grad, w, m, v, w0, w1, c0, c1, master_out, hw, hf, hs):
    new_master, _, _ = adam_update(grad[0], w[...], m[...], v[...])
    master_out[...] = new_master
    for s, (wr, cr) in enumerate(((w0, c0), (w1, c1))):
        m_s, v_s = decode_moments(cr[0])
        nw, nf, ns = adam_update(grad[1 + s], wr[0], m_s, v_s)
        hw[s] = nw.astype(jnp.bfloat16)
        hf[s] = nf
        hs[s] = ns


def finish(slots, grads, w, m, v, all_w, all_codes):
    rows, cols = w.shape
    step = 32

    def plain(i, slots):
        return (i, 0)

    def lead(i, slots):
        return (0, i, 0)

    def held(s):
        return pl.BlockSpec((1, step, cols), lambda i, slots: (slots[s], i, 0))

    flat = pl.BlockSpec((step, cols), plain)
    pair = pl.BlockSpec((2, step, cols), lead)
    return pl.pallas_call(
        adam_kernel,
        grid_spec=pltpu.PrefetchScalarGridSpec(
            num_scalar_prefetch=1,
            grid=(rows // step,),
            in_specs=[pl.BlockSpec((3, step, cols), lead), flat, flat, flat]
            + [held(0), held(1), held(0), held(1)],
            out_specs=[flat, pair, pair, pair],
        ),
        out_shape=[
            jax.ShapeDtypeStruct((rows, cols), F32),
            jax.ShapeDtypeStruct((2, rows, cols), jnp.bfloat16),
            jax.ShapeDtypeStruct((2, rows, cols), F32),
            jax.ShapeDtypeStruct((2, rows, cols), F32),
        ],
        compiler_params=pltpu.CompilerParams(vmem_limit_bytes=32 << 20),
        cost_estimate=pl.CostEstimate(
            flops=60 * rows * cols, bytes_accessed=60 * rows * cols, transcendentals=6 * rows * cols
        ),
    )(slots, grads, w, m, v, all_w, all_w, all_codes, all_codes)


def body(
    saved_inputs,
    saved_cotangents,
    row_counts,
    old_slots,
    new_slots,
    master,
    first_moment,
    second_moment,
):
    expert_index = lax.axis_index("expert")
    data_index = lax.axis_index("dp")
    y, z = data_index // NZ, data_index % NZ
    x, core = expert_index // 2, expert_index % 2
    inputs = saved_inputs[0]
    cot = saved_cotangents[0]
    rows, width_d = inputs.shape
    width_h = cot.shape[1]
    half_h = width_h // 2
    shard = master.shape[1]
    block = width_d // NY
    contract = (((0,), (0,)), ((), ()))
    ys = {d: y_shift(d) for d in (1, 2, -1)}
    zs = {d: z_shift(d) for d in (1, 2, -1)}

    offsets = jnp.array([0, 3, 1, 2], jnp.int32)
    ids = old_slots.reshape(NX, 2, 2)[(x + offsets) % NX]
    ids = jnp.where(core == 0, ids, ids[:, ::-1]).transpose(1, 0, 2).reshape(16)
    mine_new = lax.dynamic_index_in_dim(new_slots, expert_index, 0, keepdims=False)
    targets = jnp.concatenate([expert_index[None].astype(jnp.int32), mine_new])
    table = jnp.where(ids[:, None] == targets[None, :], 0.125, 0.0).astype(F32)

    counts = lax.dynamic_index_in_dim(row_counts[0], data_index, 0, keepdims=False)
    c0, c1 = counts[0], counts[1]
    half = rows // 2

    def scaled(cs, lo, hi):
        index = lax.broadcasted_iota(jnp.int32, (cs.shape[0], 1), 0)
        return jnp.where((index >= lo) & (index < hi), cs * jnp.bfloat16(SCALE), jnp.bfloat16(0))

    def dot(xs, cs):
        return lax.dot_general(xs, cs, contract, preferred_element_type=F32).astype(F16)

    cot0 = scaled(cot[:half], 0, c0)
    a_pieces = {}
    for d in (2, 1, 3, 0):
        xs = lax.dynamic_slice(inputs, (0, ((y + d) % NY) * block), (half, block))
        a_pieces[d] = [
            dot(xs, cot0[:, h * half_h : (h + 1) * half_h]).reshape(NZ, shard, half_h) for h in (0, 1)
        ]
    start = jnp.minimum((c0 // 16) * 16, rows - WINDOW)
    window = lax.dynamic_slice_in_dim(inputs, start, WINDOW, 0)
    cot1 = scaled(lax.dynamic_slice_in_dim(cot, start, WINDOW, 0), c0 - start, c0 + c1 - start)
    b_all = [
        dot(window, cot1[:, h * half_h : (h + 1) * half_h]).reshape(NY, NZ, shard, half_h)
        for h in (0, 1)
    ]
    b_pieces = {
        d: [lax.dynamic_index_in_dim(b, (z + d) % NZ, 1, keepdims=False) for b in b_all]
        for d in (2, 1, 3, 0)
    }

    all_master = lax.all_gather(master[0], "expert", axis=0, tiled=False)
    all_codes = lax.all_gather(
        encode_moments(first_moment[0], second_moment[0]), "expert", axis=0, tiled=False
    )

    sum_a = ring_sums(a_pieces, ys)
    sum_b = ring_sums(b_pieces, zs)
    grad_a = last_sums(sum_a, z, zs)
    grad_b = last_sums(sum_b, y, ys)

    back = 8.0 * 2.0 / SCALE
    mine = [(grad_a * back).astype(F16), (grad_b * back).astype(F16)]
    left = [lax.ppermute(v, "expert", x_shift(1)) for v in mine]
    right = [lax.ppermute(v, "expert", x_shift(-1)) for v in mine]
    far = [lax.ppermute(left[0], "expert", x_shift(1)), lax.ppermute(right[1], "expert", x_shift(-1))]
    same = mine + left + right + far
    other = [lax.ppermute(v, "expert", core_swap()) for v in same]

    grads = 0.0
    for k, g in enumerate(same + other):
        grads = grads + table[k][:, None, None] * g.astype(F32)[None]
    new_master, held_w, held_first, held_second = finish(
        mine_new, grads, master[0], first_moment[0], second_moment[0], all_master, all_codes
    )
    return new_master[None], held_w, held_first, held_second


def solution(mesh):
    return jax.shard_map(
        body,
        mesh=mesh,
        in_specs=(
            P("expert", "dp", None),
            P("expert", "dp", None),
            P("expert", None, None),
            P(),
            P(),
            P("expert", "dp", None),
            P("expert", "dp", None),
            P("expert", "dp", None),
        ),
        out_specs=(
            P("expert", "dp", None),
            P("expert", "dp", None),
            P("expert", "dp", None),
            P("expert", "dp", None),
        ),
        check_vma=False,
    )
```

time: 383 us -> 178 us (0.46)
  waiting for transfers between devices: 275 us -> 40.5 us
  starting transfers between devices: 0.6 us -> 46.7 us
  local copies, waits for them, and re-layouts: 33.9 us -> 11.1 us
  matrix products: 46.5 us -> 29.5 us
  other arithmetic: 9.11 us -> 22.9 us
  between operations: 13.9 us -> 19.2 us
  Pallas kernels: 0 us -> 5.12 us
    unnamed x6 -> x2, waiting for transfers between devices: 140 us -> 0.71 us
    all_gather x3 -> x2, waiting for transfers between devices: 95.6 us -> 0.04 us  [the longest x1 0.02 us: body(): lax.all_gather(encode_moments(first_moment[0], second_moment[0]), 'expert...]
    ppermute x0 -> x32, starting transfers between devices: none -> 46.6 us  [the longest x8 18.9 us: body(): other = [lax.ppermute(v, 'expert', core_swap()) for v in same]]
    ppermute x0 -> x32, waiting for transfers between devices: none -> 39.7 us  [the longest x2 14 us: ring_sums(): lax.ppermute((pieces[3][1].astype(F32) + far_down.astype(F32)).astype(F16...]
    reduce_scatter x1 -> x0, waiting for transfers between devices: 39.5 us -> none  [body(): lax.psum_scatter(spread, 'expert', scatter_dimension=0, tiled=True)[0]]
    unnamed x19 -> x46, local copies, waits for them, and re-layouts: 28.5 us -> 7.6 us
    dot_general x5 -> x10, matrix products: 46.5 us -> 29.5 us  [dot(): lax.dot_general(xs, cs, contract, preferred_element_type=F32).astype(F16)]
    convert_element_type x1 -> x24, other arithmetic: 0.24 us -> 14.5 us  [the longest x16 5.24 us: body(): grads = grads + table[k][:, None, None] * g.astype(F32)[None]]
  transfers between devices with their start and end apart: 5 -> 34, of which waited for: 5 -> 7; matrix products, arithmetic and copies ran while one was open for 5% -> 30% of each run, Pallas kernels for 0% -> 0%
where the time goes in v1:
time: 178 us; the launch traced here: 175 us
  starting transfers between devices  46.7 us (26%)
  waiting for transfers between devices  40.5 us (23%)
  matrix products  29.5 us (17%)
  other arithmetic  22.9 us (13%)
  between operations  19.2 us (11%)
  local copies, waits for them, and re-layouts  11.1 us (6%)
  Pallas kernels  5.12 us (3%)
    dot_general x10, matrix products, dot(): lax.dot_general(xs, cs, contract, preferred_element_type=F32).astype(F16)  29.5 us
    ppermute x8, starting transfers between devices, body(): other = [lax.ppermute(v, 'expert', core_swap()) for v in same]  18.9 us
    ppermute x2, waiting for transfers between devices, ring_sums(): lax.ppermute((pieces[3][1].astype(F32) + far_down.astype(F32)).astype(F16...  14 us
    ppermute x2, waiting for transfers between devices, ring_sums(): far_up = lax.ppermute(pieces[2][0], 'dp', up)  8.28 us
    unnamed x46, local copies, waits for them, and re-layouts  7.6 us
    ppermute x2, waiting for transfers between devices, ring_sums(): raw_up = lax.ppermute(pieces[1][1], 'dp', up)  7.32 us
    ppermute x2, starting transfers between devices, last_sums(): c = lax.ppermute(block(2), 'dp', shifts[2])  5.4 us
    convert_element_type x16, other arithmetic, body(): grads = grads + table[k][:, None, None] * g.astype(F32)[None]  5.24 us
  transfers between devices with their start and end apart: 34, of which 7 were waited for; matrix products, arithmetic and copies ran while one was open for 30% of the time, Pallas kernels for 0%

profile of v1, /device:TPU:15, one launch (start us, length us, event | category | flops | bytes accessed | tf_op | source)
XLA Modules:
  0.0 175.1 jit_solution(7581204703753433048)
XLA Ops:
  7.2 3.3 %fusion.40 = s32[1,224,768]{2,1,0:T(8,128)} fusion(f32[1,224,768]{2,1,0:T(8,128)} %param.16, f32[1,224,768]{2,1,0:T(8,128)} %param.15), kind=kLoop, calls=%fused_computation.79 | loop fusion | flops 2752512 | bytes 2064384 | tf_op jit(solution)/shard_map/add | solution.py:43
  12.8 3.4 %convolution_convert_fusion.2 = f16[896,384]{1,0:T(8,128)(2,1)} fusion(bf16[1,1280,3584]{2,1,0:T(8,128)(2,1)} %param.9, s32[]{:T(128)S(6)} %select_n.185, bf16[640,768]{1,0:T(8,128)(2,1)S(1)} %bitcast_select_fusion.1), kind=kOutput, calls=%fused_computation.48 | convolution fusion | flops 440745984 | bytes 2326532 | tf_op jit(solution)/shard_map/dot_general | solution.py:171
  16.3 3.0 %convolution_convert_fusion.4 = f16[896,384]{1,0:T(8,128)(2,1)} fusion(bf16[1,1280,3584]{2,1,0:T(8,128)(2,1)} %param.9, s32[]{:T(128)S(6)} %select_n.183, bf16[640,768]{1,0:T(8,128)(2,1)S(1)} %bitcast_select_fusion.1), kind=kOutput, calls=%fused_computation.50 | convolution fusion | flops 440745984 | bytes 2326532 | tf_op jit(solution)/shard_map/dot_general | solution.py:171
  19.3 1.3 collective-permute-start.3
  20.6 3.0 %convolution_convert_fusion.7 = f16[896,384]{1,0:T(8,128)(2,1)} fusion(bf16[1,1280,3584]{2,1,0:T(8,128)(2,1)} %param.9, s32[]{:T(128)S(6)} %select_n.185, bf16[640,768]{1,0:T(8,128)(2,1)S(1)} %bitcast_select_fusion.1), kind=kOutput, calls=%fused_computation.53 | convolution fusion | flops 440745984 | bytes 2326532 | tf_op jit(solution)/shard_map/dot_general | solution.py:171
  23.5 1.3 collective-permute-start
  24.9 3.0 %convolution_convert_fusion.6 = f16[896,384]{1,0:T(8,128)(2,1)} fusion(bf16[1,1280,3584]{2,1,0:T(8,128)(2,1)} %param.9, s32[]{:T(128)S(6)} %select_n.187, bf16[640,768]{1,0:T(8,128)(2,1)S(1)} %bitcast_select_fusion.1), kind=kOutput, calls=%fused_computation.52 | convolution fusion | flops 440745984 | bytes 2326532 | tf_op jit(solution)/shard_map/dot_general | solution.py:171
  33.1 5.9 %convolution_convert_fusion = f16[3584,384]{1,0:T(8,128)(2,1)S(1)} fusion(bf16[1,1280,3584]{2,1,0:T(8,128)(2,1)} %param.9, s32[]{:T(128)S(6)} %select_n.198, bf16[656,768]{1,0:T(8,128)(2,1)S(1)} %bitcast_select_fusion), kind=kOutput, calls=%fused_computation.1 | convolution fusion | flops 1807024128 | bytes 7958532 | tf_op jit(solution)/shard_map/dot_general | solution.py:171
  39.0 1.6 dynamic-slice_bitcast_fusion.1
  40.6 3.7 %collective-permute-start.13 = (f16[4,224,384]{2,1,0:T(8,128)(2,1)}, f16[4,224,384]{2,1,0:T(8,128)(2,1)}, u32[]{:S(2)}, u32[]{:S(2)}) collective-permute-start(f16[4,224,384]{2,1,0:T(8,128)(2,1)} %get-tuple-element.17), channel_id=1, source_target_pairs={{0,3},{1,0},{2,1},{3,2},{4,7},{5,4},{6,5},{7,6},{8,11},{9,8},{10,9... | collective-permute-start | bytes 2064392 | tf_op jit(solution)/shard_map/ppermute | solution.py:58
  44.3 1.7 convolution_convert_fusion.3
  46.1 3.3 %convolution_convert_fusion.1 = f16[3584,384]{1,0:T(8,128)(2,1)S(1)} fusion(bf16[1,1280,3584]{2,1,0:T(8,128)(2,1)S(1)} %bitcast.152, s32[]{:T(128)S(6)} %select_n.198, bf16[656,768]{1,0:T(8,128)(2,1)S(1)} %bitcast_select_fusion), kind=kOutput, calls=%fused_computation.2 | convolution fusion | flops 1807024128 | bytes 7958532 | tf_op jit(solution)/shard_map/dot_general | solution.py:171
  49.4 1.8 %convolution_convert_fusion.8 = f16[896,384]{1,0:T(8,128)(2,1)} fusion(bf16[1,1280,3584]{2,1,0:T(8,128)(2,1)S(1)} %bitcast.152, s32[]{:T(128)S(6)} %select_n.183, bf16[640,768]{1,0:T(8,128)(2,1)S(1)} %copy-done.13), kind=kOutput, calls=%fused_computation.54 | convolution fusion | flops 440745984 | bytes 2326532 | tf_op jit(solution)/shard_map/dot_general | solution.py:171
  51.2 2.2 %convolution_convert_fusion.5 = f16[896,384]{1,0:T(8,128)(2,1)S(1)} fusion(bf16[1,1280,3584]{2,1,0:T(8,128)(2,1)} %param.9, s32[]{:T(128)S(6)} %select_n.179, bf16[640,768]{1,0:T(8,128)(2,1)} %copy-done.12), kind=kOutput, calls=%fused_computation.51 | convolution fusion | flops 440745984 | bytes 2326532 | tf_op jit(solution)/shard_map/dot_general | solution.py:171
  53.5 2.2 %convolution_convert_fusion.9 = f16[896,384]{1,0:T(8,128)(2,1)S(1)} fusion(bf16[1,1280,3584]{2,1,0:T(8,128)(2,1)} %param.9, s32[]{:T(128)S(6)} %select_n.179, bf16[640,768]{1,0:T(8,128)(2,1)} %copy-done.12), kind=kOutput, calls=%fused_computation.55 | convolution fusion | flops 440745984 | bytes 2326532 | tf_op jit(solution)/shard_map/dot_general | solution.py:171
  56.9 1.5 fusion.12
  58.4 2.8 %collective-permute-start.5 = (f16[4,224,384]{2,1,0:T(8,128)(2,1)S(1)}, f16[4,224,384]{2,1,0:T(8,128)(2,1)S(1)}, u32[]{:S(2)}, u32[]{:S(2)}) collective-permute-start(f16[4,224,384]{2,1,0:T(8,128)(2,1)S(1)} %fusion.12), channel_id=1, source_target_pairs={{0,12},{1,13},{2,14},{3,15},{4,0},{5,1},{6,2},{7,3},{8,4},{9,5},{1... | collective-permute-start | bytes 2064392 | tf_op jit(solution)/shard_map/ppermute | solution.py:62
  61.1 1.4 fusion.16
  62.7 1.4 fusion.4
  64.0 8.3 %collective-permute-done.9 = f16[4,224,384]{2,1,0:T(8,128)(2,1)S(1)} collective-permute-done((f16[4,224,384]{2,1,0:T(8,128)(2,1)S(1)}, f16[4,224,384]{2,1,0:T(8,128)(2,1)S(1)}, u32[]{:S(2)}, u32[]{:S(2)}) %collective-permute-start.9) | collective-permute-done | bytes 688160 | tf_op jit(solution)/shard_map/ppermute | solution.py:57
  72.6 2.7 %collective-permute-start.11 = (f16[4,224,384]{2,1,0:T(8,128)(2,1)S(1)}, f16[4,224,384]{2,1,0:T(8,128)(2,1)S(1)}, u32[]{:S(2)}, u32[]{:S(2)}) collective-permute-start(f16[4,224,384]{2,1,0:T(8,128)(2,1)S(1)} %get-tuple-element.19), channel_id=1, source_target_pairs={{0,3},{1,0},{2,1},{3,2},{4,7},{5,4},{6,5},{7,6},{8,11},{9,8},{10,9... | collective-permute-start | bytes 2064392 | tf_op jit(solution)/shard_map/ppermute | solution.py:60
  75.3 1.1 collective-permute-start.14
  76.4 1.5 fusion.15
  78.4 1.5 fusion.19
  80.2 7.3 %collective-permute-done.12 = f16[4,224,384]{2,1,0:T(8,128)(2,1)S(1)} collective-permute-done((f16[4,224,384]{2,1,0:T(8,128)(2,1)S(1)}, f16[4,224,384]{2,1,0:T(8,128)(2,1)S(1)}, u32[]{:S(2)}, u32[]{:S(2)}) %collective-permute-start.12) | collective-permute-done | bytes 688160 | tf_op jit(solution)/shard_map/ppermute | solution.py:59
  87.5 14.0 %collective-permute-done.14 = f16[4,224,384]{2,1,0:T(8,128)(2,1)S(1)} collective-permute-done((f16[4,224,384]{2,1,0:T(8,128)(2,1)S(1)}, f16[4,224,384]{2,1,0:T(8,128)(2,1)S(1)}, u32[]{:S(2)}, u32[]{:S(2)}) %collective-permute-start.14) | collective-permute-done | bytes 688160 | tf_op jit(solution)/shard_map/ppermute | solution.py:62
  101.5 2.2 %collective-permute-start.8 = (f16[224,768]{1,0:T(8,128)(2,1)S(1)}, f16[224,768]{1,0:T(8,128)(2,1)}, u32[]{:S(2)}, u32[]{:S(2)}) collective-permute-start(f16[224,768]{1,0:T(8,128)(2,1)S(1)} %get-tuple-element.22), channel_id=1, source_target_pairs={{0,2},{1,3},{2,0},{3,1},{4,6},{5,7},{6,4},{7,5},{8,10},{9,11},{10,... | collective-permute-start | bytes 1032200 | tf_op jit(solution)/shard_map/ppermute | solution.py:78
  104.1 1.5 fusion.11
  105.6 1.1 fusion.56
  106.7 2.9 %collective-permute-start.15 = (f16[224,768]{1,0:T(8,128)(2,1)}, f16[224,768]{1,0:T(8,128)(2,1)}, u32[]{:S(2)}, u32[]{:S(2)}) collective-permute-start(f16[224,768]{1,0:T(8,128)(2,1)} %get-tuple-element.23), channel_id=1, source_target_pairs={{0,4},{1,5},{2,6},{3,7},{4,8},{5,9},{6,10},{7,11},{8,12},{9,13},{1... | collective-permute-start | bytes 1032200 | tf_op jit(solution)/shard_map/ppermute | solution.py:76
  109.9 2.2 %collective-permute-done.6 = f16[224,768]{1,0:T(8,128)(2,1)} collective-permute-done((f16[224,768]{1,0:T(8,128)(2,1)S(1)}, f16[224,768]{1,0:T(8,128)(2,1)}, u32[]{:S(2)}, u32[]{:S(2)}) %collective-permute-start.6) | collective-permute-done | bytes 344096 | tf_op jit(solution)/shard_map/ppermute | solution.py:76
  112.1 3.2 %collective-permute-start.17 = (f16[224,768]{1,0:T(8,128)(2,1)}, f16[224,768]{1,0:T(8,128)(2,1)}, u32[]{:S(2)}, u32[]{:S(2)}) collective-permute-start(f16[224,768]{1,0:T(8,128)(2,1)} %get-tuple-element.25), channel_id=1, source_target_pairs={{0,8},{1,9},{2,10},{3,11},{4,12},{5,13},{6,14},{7,15},{8,0},{9,1},... | collective-permute-start | bytes 1032200 | tf_op jit(solution)/shard_map/ppermute | solution.py:78
  115.4 2.3 %fusion.88 = (f32[224,768]{1,0:T(8,128)}, f16[224,768]{1,0:T(8,128)(2,1)S(1)}) fusion(f16[224,768]{1,0:T(8,128)(2,1)} %collective-permute-done.8, f16[224,768]{1,0:T(8,128)(2,1)} %collective-permute-done.7, f16[224,768]{1,0:T(8,128)(2,1)} %collective-permute-done.6, s32[]{:T(128)S(6)} %select_n.190, f16[4,224,384]{2,1,0:T(8,128)(2,1)S(1)} %fusion.15, ...), kind=kLoop, calls=%fused_computation.163 | loop fusion | flops 1892352 | bytes 3440644 | tf_op jit(solution)/shard_map/convert_element_type | solution.py:212
  117.7 1.5 collective-permute-start.20
  119.1 9.7 %collective-permute-start.24 = (f16[224,768]{1,0:T(8,128)(2,1)S(1)}, f16[224,768]{1,0:T(8,128)(2,1)S(1)}, u32[]{:S(2)}, u32[]{:S(2)}) collective-permute-start(f16[224,768]{1,0:T(8,128)(2,1)S(1)} %get-tuple-element.13), channel_id=1, source_target_pairs={{0,16},{16,0},{32,48},{48,32},{64,80},{80,64},{96,112},{112,96},{1... | collective-permute-start | bytes 1032200 | tf_op jit(solution)/shard_map/ppermute | solution.py:208
  128.8 2.3 %fusion.90 = (f32[224,768]{1,0:T(8,128)}, f16[224,768]{1,0:T(8,128)(2,1)S(1)}) fusion(f16[224,768]{1,0:T(8,128)(2,1)} %collective-permute-done.17, f16[224,768]{1,0:T(8,128)(2,1)} %collective-permute-done.16, f16[224,768]{1,0:T(8,128)(2,1)} %collective-permute-done.15, s32[]{:T(128)S(6)} %select_n.200, f16[4,224,384]{2,1,0:T(8,128)(2,1)S(1)} %fusion.7, ...), kind=kLoop, calls=%fused_computation.164 | loop fusion | flops 1892352 | bytes 3440644 | tf_op jit(solution)/shard_map/convert_element_type | solution.py:212
  131.5 2.3 %collective-permute-start.19 = (f16[224,768]{1,0:T(8,128)(2,1)S(1)}, f16[224,768]{1,0:T(8,128)(2,1)S(1)}, u32[]{:S(2)}, u32[]{:S(2)}) collective-permute-start(f16[224,768]{1,0:T(8,128)(2,1)S(1)} %get-tuple-element.15), channel_id=1, source_target_pairs={{0,32},{16,48},{32,64},{48,80},{64,96},{80,112},{96,0},{112,16},{1... | collective-permute-start | bytes 1032200 | tf_op jit(solution)/shard_map/ppermute | solution.py:204
  133.9 1.8 %collective-permute-start.25 = (f16[224,768]{1,0:T(8,128)(2,1)S(1)}, f16[224,768]{1,0:T(8,128)(2,1)S(1)}, u32[]{:S(2)}, u32[]{:S(2)}) collective-permute-start(f16[224,768]{1,0:T(8,128)(2,1)S(1)} %get-tuple-element.15), channel_id=1, source_target_pairs={{0,16},{16,0},{32,48},{48,32},{64,80},{80,64},{96,112},{112,96},{1... | collective-permute-start | bytes 1032200 | tf_op jit(solution)/shard_map/ppermute | solution.py:208
  135.8 5.0 %collective-permute-done.21 = f16[224,768]{1,0:T(8,128)(2,1)S(1)} collective-permute-done((f16[224,768]{1,0:T(8,128)(2,1)S(1)}, f16[224,768]{1,0:T(8,128)(2,1)S(1)}, u32[]{:S(2)}, u32[]{:S(2)}) %collective-permute-start.21) | collective-permute-done | bytes 344096 | tf_op jit(solution)/shard_map/ppermute | solution.py:205
  142.7 1.8 %collective-permute-start.29 = (f16[224,768]{1,0:T(8,128)(2,1)S(1)}, f16[224,768]{1,0:T(8,128)(2,1)S(1)}, u32[]{:S(2)}, u32[]{:S(2)}) collective-permute-start(f16[224,768]{1,0:T(8,128)(2,1)S(1)} %collective-permute-done.21), channel_id=1, source_target_pairs={{0,16},{16,0},{32,48},{48,32},{64,80},{80,64},{96,112},{112,96},{1... | collective-permute-start | bytes 1032200 | tf_op jit(solution)/shard_map/ppermute | solution.py:208
  144.6 2.5 %collective-permute-done.22 = f16[224,768]{1,0:T(8,128)(2,1)S(1)} collective-permute-done((f16[224,768]{1,0:T(8,128)(2,1)S(1)}, f16[224,768]{1,0:T(8,128)(2,1)S(1)}, u32[]{:S(2)}, u32[]{:S(2)}) %collective-permute-start.22) | collective-permute-done | bytes 344096 | tf_op jit(solution)/shard_map/ppermute | solution.py:206
  147.1 2.4 %collective-permute-start.27 = (f16[224,768]{1,0:T(8,128)(2,1)S(1)}, f16[224,768]{1,0:T(8,128)(2,1)S(1)}, u32[]{:S(2)}, u32[]{:S(2)}) collective-permute-start(f16[224,768]{1,0:T(8,128)(2,1)S(1)} %collective-permute-done.19), channel_id=1, source_target_pairs={{0,16},{16,0},{32,48},{48,32},{64,80},{80,64},{96,112},{112,96},{1... | collective-permute-start | bytes 1032200 | tf_op jit(solution)/shard_map/ppermute | solution.py:208
  149.5 3.0 %collective-permute-start.31 = (f16[224,768]{1,0:T(8,128)(2,1)S(1)}, f16[224,768]{1,0:T(8,128)(2,1)S(1)}, u32[]{:S(2)}, u32[]{:S(2)}) collective-permute-start(f16[224,768]{1,0:T(8,128)(2,1)S(1)} %collective-permute-done.23), channel_id=1, source_target_pairs={{0,16},{16,0},{32,48},{48,32},{64,80},{80,64},{96,112},{112,96},{1... | collective-permute-start | bytes 1032200 | tf_op jit(solution)/shard_map/ppermute | solution.py:208
  154.5 2.4 %multiply_add_fusion.grad = f32[3,224,768]{2,1,0:T(8,128)S(1)} fusion(f32[224,768]{1,0:T(8,128)S(1)} %convert_element_type.303, f32[3]{0:T(128)S(1)} %get-tuple-element.27, f32[224,768]{1,0:T(8,128)S(1)} %convert_element_type.302, f32[3]{0:T(128)S(1)} %get-tuple-element.28, f32[224,768]{1,0:T(8,128)S(1)} %convert_element_type.301, ...), kind=kLoop, calls=%fused_computation.7 | loop fusion | flops 15998976 | bytes 13074624 | tf_op jit(solution)/shard_map/add | solution.py:212
  156.9 2.6 %copy-done.1 = s32[8,224,768]{2,1,0:T(8,128)S(1)} copy-done((s32[8,224,768]{2,1,0:T(8,128)S(1)}, s32[8,224,768]{2,1,0:T(8,128)}, u32[]{:S(2)}) %copy-start.1) | copy-done | bytes 5505048
  159.5 2.6 %copy-done.2 = f32[8,224,768]{2,1,0:T(8,128)S(1)} copy-done((f32[8,224,768]{2,1,0:T(8,128)S(1)}, f32[8,224,768]{2,1,0:T(8,128)}, u32[]{:S(2)}) %copy-start.2) | copy-done | bytes 5505048
  162.0 1.1 copy-done.5
  163.1 5.1 %shard_map.120 = (f32[224,768]{1,0:T(8,128)}, bf16[2,224,768]{2,1,0:T(8,128)(2,1)}, f32[2,224,768]{2,1,0:T(8,128)}, f32[2,224,768]{2,1,0:T(8,128)}) custom-call(s32[2]{0:T(128)S(1)} %fusion.86.slots, f32[3,224,768]{2,1,0:T(8,128)S(1)} %multiply_add_fusion.grad, f32[224,768]{1,0:T(8,128)S(1)} %bitcast.137, f32[224,768]{1,0:T(8,128)S(1)} %bitcast.138, ...), custom_call_target="tpu_custom_call" | custom-call | flops 10321920 | bytes 10321920 | tf_op jit(solution)/shard_map/pallas_call | solution.py:108
  (127 shorter events, 10.6 us)
Async XLA Ops:
  7.2 135.3 %copy-start = (s32[8,2]{0,1:T(2,128)S(1)}, s32[8,2]{0,1:T(2,128)}, u32[]{:S(2)}) copy-start(s32[8,2]{0,1:T(2,128)} %param.13) | copy-start | bytes 196
  7.2 4.1 %copy-start.18 = (s32[1,16,3]{1,0,2:T(1,128)S(1)}, s32[1,16,3]{1,0,2:T(1,128)}, u32[]{:S(2)}) copy-start(s32[1,16,3]{1,0,2:T(1,128)} %param.11) | copy-start | bytes 580
  7.2 5.4 %copy-start.11 = (bf16[1,1280,768]{2,1,0:T(8,128)(2,1)S(1)}, bf16[1,1280,768]{2,1,0:T(8,128)(2,1)}, u32[]{:S(2)}) copy-start(bf16[1,1280,768]{2,1,0:T(8,128)(2,1)} %param.10) | copy-start | bytes 5898244
  7.2 149.6 %all-gather.5.cloned.1.call-start = ((), (), s32[]{:S(2)}) async-start(), calls=%async_computation.1 | async-start | bytes 6193152 | tf_op jit(solution)/shard_map/all_gather | solution.py:193
  10.5 146.3 %all-gather.3.cloned.1.call-start = ((), (), s32[]{:S(2)}) async-start(), calls=%async_computation | async-start | bytes 6193152 | tf_op jit(solution)/shard_map/all_gather | solution.py:192
  12.8 31.5 %copy-start.12 = (bf16[640,768]{1,0:T(8,128)(2,1)}, bf16[640,768]{1,0:T(8,128)(2,1)S(1)}, u32[]{:S(2)}) copy-start(bf16[640,768]{1,0:T(8,128)(2,1)S(1)} %bitcast_select_fusion.1) | copy-start | bytes 2949124
  16.1 40.0 %collective-permute-start.4 = (f16[4,224,384]{2,1,0:T(8,128)(2,1)}, f16[4,224,384]{2,1,0:T(8,128)(2,1)}, u32[]{:S(2)}, u32[]{:S(2)}) collective-permute-start(f16[4,224,384]{2,1,0:T(8,128)(2,1)} %bitcast.17), channel_id=1, source_target_pairs={{0,12},{1,13},{2,14},{3,15},{4,0},{5,1},{6,2},{7,3},{8,4},{9,5},{1... | collective-permute-start | bytes 2064392 | tf_op jit(solution)/shard_map/ppermute | solution.py:58
  19.3 53.3 %collective-permute-start.3 = (f16[4,224,384]{2,1,0:T(8,128)(2,1)}, f16[4,224,384]{2,1,0:T(8,128)(2,1)}, u32[]{:S(2)}, u32[]{:S(2)}) collective-permute-start(f16[4,224,384]{2,1,0:T(8,128)(2,1)} %bitcast.15), channel_id=1, source_target_pairs={{0,4},{1,5},{2,6},{3,7},{4,8},{5,9},{6,10},{7,11},{8,12},{9,13},{1... | collective-permute-start | bytes 2064392 | tf_op jit(solution)/shard_map/ppermute | solution.py:59
  23.5 34.8 %collective-permute-start = (f16[4,224,384]{2,1,0:T(8,128)(2,1)}, f16[4,224,384]{2,1,0:T(8,128)(2,1)}, u32[]{:S(2)}, u32[]{:S(2)}) collective-permute-start(f16[4,224,384]{2,1,0:T(8,128)(2,1)} %bitcast.11), channel_id=1, source_target_pairs={{0,4},{1,5},{2,6},{3,7},{4,8},{5,9},{6,10},{7,11},{8,12},{9,13},{1... | collective-permute-start | bytes 2064392 | tf_op jit(solution)/shard_map/ppermute | solution.py:57
  27.8 50.1 %collective-permute-start.2 = (f16[4,224,384]{2,1,0:T(8,128)(2,1)}, f16[4,224,384]{2,1,0:T(8,128)(2,1)}, u32[]{:S(2)}, u32[]{:S(2)}) collective-permute-start(f16[4,224,384]{2,1,0:T(8,128)(2,1)} %bitcast.13), channel_id=1, source_target_pairs={{0,12},{1,13},{2,14},{3,15},{4,0},{5,1},{6,2},{7,3},{8,4},{9,5},{1... | collective-permute-start | bytes 2064392 | tf_op jit(solution)/shard_map/ppermute | solution.py:60
  32.6 11.7 %slice-start = ((s8[9175040]{0:T(1024)(128)(4,1)}), s8[4194304]{0:T(1024)(128)(4,1)S(1)}, s32[]{:S(2)}) async-start(s8[9175040]{0:T(1024)(128)(4,1)} %bitcast.151), calls=%async_computation.2 | async-start | bytes 8388608
  33.0 11.3 %slice-start.1 = ((s8[9175040]{0:T(1024)(128)(4,1)}), s8[4194304]{0:T(1024)(128)(4,1)S(1)}, s32[]{:S(2)}) async-start(s8[9175040]{0:T(1024)(128)(4,1)} %bitcast.151), calls=%async_computation.3 | async-start | bytes 8388608
  33.1 11.3 %slice-start.2 = ((s8[9175040]{0:T(1024)(128)(4,1)}), s8[786432]{0:T(1024)(128)(4,1)S(1)}, s32[]{:S(2)}) async-start(s8[9175040]{0:T(1024)(128)(4,1)} %bitcast.151), calls=%async_computation.4 | async-start | bytes 1572864
  38.9 7.1 %copy-start.7 = (f16[3584,384]{1,0:T(8,128)(2,1)}, f16[3584,384]{1,0:T(8,128)(2,1)S(1)}, u32[]{:S(2)}) copy-start(f16[3584,384]{1,0:T(8,128)(2,1)S(1)} %convolution_convert_fusion) | copy-start | bytes 8257540
  40.6 22.0 %collective-permute-start.13 = (f16[4,224,384]{2,1,0:T(8,128)(2,1)}, f16[4,224,384]{2,1,0:T(8,128)(2,1)}, u32[]{:S(2)}, u32[]{:S(2)}) collective-permute-start(f16[4,224,384]{2,1,0:T(8,128)(2,1)} %get-tuple-element.17), channel_id=1, source_target_pairs={{0,3},{1,0},{2,1},{3,2},{4,7},{5,4},{6,5},{7,6},{8,11},{9,8},{10,9... | collective-permute-start | bytes 2064392 | tf_op jit(solution)/shard_map/ppermute | solution.py:58
  49.4 22.9 %copy-start.6 = (f16[3584,384]{1,0:T(8,128)(2,1)}, f16[3584,384]{1,0:T(8,128)(2,1)S(1)}, u32[]{:S(2)}) copy-start(f16[3584,384]{1,0:T(8,128)(2,1)S(1)} %convolution_convert_fusion.1) | copy-start | bytes 8257540
  55.8 5.3 %copy-start.15 = (f16[896,384]{1,0:T(8,128)(2,1)S(1)}, f16[896,384]{1,0:T(8,128)(2,1)}, u32[]{:S(2)}) copy-start(f16[896,384]{1,0:T(8,128)(2,1)} %convolution_convert_fusion.8) | copy-start | bytes 2064388
  56.1 16.2 %collective-permute-start.9 = (f16[4,224,384]{2,1,0:T(8,128)(2,1)S(1)}, f16[4,224,384]{2,1,0:T(8,128)(2,1)S(1)}, u32[]{:S(2)}, u32[]{:S(2)}) collective-permute-start(f16[4,224,384]{2,1,0:T(8,128)(2,1)S(1)} %get-tuple-element.18), channel_id=1, source_target_pairs={{0,1},{1,2},{2,3},{3,0},{4,5},{5,6},{6,7},{7,4},{8,9},{9,10},{10,1... | collective-permute-start | bytes 2064392 | tf_op jit(solution)/shard_map/ppermute | solution.py:57
  56.9 5.8 %copy-start.8 = (f16[3584,384]{1,0:T(8,128)(2,1)S(1)}, f16[3584,384]{1,0:T(8,128)(2,1)}, u32[]{:S(2)}) copy-start(f16[3584,384]{1,0:T(8,128)(2,1)} %copy-done.7) | copy-start | bytes 8257540
  58.4 16.9 %collective-permute-start.5 = (f16[4,224,384]{2,1,0:T(8,128)(2,1)S(1)}, f16[4,224,384]{2,1,0:T(8,128)(2,1)S(1)}, u32[]{:S(2)}, u32[]{:S(2)}) collective-permute-start(f16[4,224,384]{2,1,0:T(8,128)(2,1)S(1)} %fusion.12), channel_id=1, source_target_pairs={{0,12},{1,13},{2,14},{3,15},{4,0},{5,1},{6,2},{7,3},{8,4},{9,5},{1... | collective-permute-start | bytes 2064392 | tf_op jit(solution)/shard_map/ppermute | solution.py:62
  61.1 11.2 %copy-start.14 = (f16[4,224,384]{2,1,0:T(8,128)(2,1)S(1)}, f16[4,224,384]{2,1,0:T(8,128)(2,1)}, u32[]{:S(2)}) copy-start(f16[4,224,384]{2,1,0:T(8,128)(2,1)} %get-tuple-element.16) | copy-start | bytes 2064388
  62.6 15.8 %collective-permute-start.1 = (f16[4,224,384]{2,1,0:T(8,128)(2,1)S(1)}, f16[4,224,384]{2,1,0:T(8,128)(2,1)S(1)}, u32[]{:S(2)}, u32[]{:S(2)}) collective-permute-start(f16[4,224,384]{2,1,0:T(8,128)(2,1)S(1)} %fusion.16), channel_id=1, source_target_pairs={{0,4},{1,5},{2,6},{3,7},{4,8},{5,9},{6,10},{7,11},{8,12},{9,13},{1... | collective-permute-start | bytes 2064392 | tf_op jit(solution)/shard_map/ppermute | solution.py:61
  72.3 15.2 %collective-permute-start.12 = (f16[4,224,384]{2,1,0:T(8,128)(2,1)S(1)}, f16[4,224,384]{2,1,0:T(8,128)(2,1)S(1)}, u32[]{:S(2)}, u32[]{:S(2)}) collective-permute-start(f16[4,224,384]{2,1,0:T(8,128)(2,1)S(1)} %copy-done.14), channel_id=1, source_target_pairs={{0,1},{1,2},{2,3},{3,0},{4,5},{5,6},{6,7},{7,4},{8,9},{9,10},{10,1... | collective-permute-start | bytes 2064392 | tf_op jit(solution)/shard_map/ppermute | solution.py:59
  72.6 31.5 %collective-permute-start.11 = (f16[4,224,384]{2,1,0:T(8,128)(2,1)S(1)}, f16[4,224,384]{2,1,0:T(8,128)(2,1)S(1)}, u32[]{:S(2)}, u32[]{:S(2)}) collective-permute-start(f16[4,224,384]{2,1,0:T(8,128)(2,1)S(1)} %get-tuple-element.19), channel_id=1, source_target_pairs={{0,3},{1,0},{2,1},{3,2},{4,7},{5,4},{6,5},{7,6},{8,11},{9,8},{10,9... | collective-permute-start | bytes 2064392 | tf_op jit(solution)/shard_map/ppermute | solution.py:60
  75.3 26.2 %collective-permute-start.14 = (f16[4,224,384]{2,1,0:T(8,128)(2,1)S(1)}, f16[4,224,384]{2,1,0:T(8,128)(2,1)S(1)}, u32[]{:S(2)}, u32[]{:S(2)}) collective-permute-start(f16[4,224,384]{2,1,0:T(8,128)(2,1)S(1)} %fusion.4), channel_id=1, source_target_pairs={{0,3},{1,0},{2,1},{3,2},{4,7},{5,4},{6,5},{7,6},{8,11},{9,8},{10,9... | collective-permute-start | bytes 2064392 | tf_op jit(solution)/shard_map/ppermute | solution.py:62
  77.9 26.2 %collective-permute-start.10 = (f16[4,224,384]{2,1,0:T(8,128)(2,1)S(1)}, f16[4,224,384]{2,1,0:T(8,128)(2,1)S(1)}, u32[]{:S(2)}, u32[]{:S(2)}) collective-permute-start(f16[4,224,384]{2,1,0:T(8,128)(2,1)S(1)} %fusion.8), channel_id=1, source_target_pairs={{0,1},{1,2},{2,3},{3,0},{4,5},{5,6},{6,7},{7,4},{8,9},{9,10},{10,1... | collective-permute-start | bytes 2064392 | tf_op jit(solution)/shard_map/ppermute | solution.py:61
  80.1 32.1 %collective-permute-start.6 = (f16[224,768]{1,0:T(8,128)(2,1)S(1)}, f16[224,768]{1,0:T(8,128)(2,1)}, u32[]{:S(2)}, u32[]{:S(2)}) collective-permute-start(f16[224,768]{1,0:T(8,128)(2,1)S(1)} %get-tuple-element.20), channel_id=1, source_target_pairs={{0,1},{1,2},{2,3},{3,0},{4,5},{5,6},{6,7},{7,4},{8,9},{9,10},{10,1... | collective-permute-start | bytes 1032200 | tf_op jit(solution)/shard_map/ppermute | solution.py:76
  87.5 27.9 %collective-permute-start.7 = (f16[224,768]{1,0:T(8,128)(2,1)S(1)}, f16[224,768]{1,0:T(8,128)(2,1)}, u32[]{:S(2)}, u32[]{:S(2)}) collective-permute-start(f16[224,768]{1,0:T(8,128)(2,1)S(1)} %get-tuple-element.21), channel_id=1, source_target_pairs={{0,3},{1,0},{2,1},{3,2},{4,7},{5,4},{6,5},{7,6},{8,11},{9,8},{10,9... | collective-permute-start | bytes 1032200 | tf_op jit(solution)/shard_map/ppermute | solution.py:77
  101.5 13.8 %collective-permute-start.8 = (f16[224,768]{1,0:T(8,128)(2,1)S(1)}, f16[224,768]{1,0:T(8,128)(2,1)}, u32[]{:S(2)}, u32[]{:S(2)}) collective-permute-start(f16[224,768]{1,0:T(8,128)(2,1)S(1)} %get-tuple-element.22), channel_id=1, source_target_pairs={{0,2},{1,3},{2,0},{3,1},{4,6},{5,7},{6,4},{7,5},{8,10},{9,11},{10,... | collective-permute-start | bytes 1032200 | tf_op jit(solution)/shard_map/ppermute | solution.py:78
  106.7 12.5 %collective-permute-start.15 = (f16[224,768]{1,0:T(8,128)(2,1)}, f16[224,768]{1,0:T(8,128)(2,1)}, u32[]{:S(2)}, u32[]{:S(2)}) collective-permute-start(f16[224,768]{1,0:T(8,128)(2,1)} %get-tuple-element.23), channel_id=1, source_target_pairs={{0,4},{1,5},{2,6},{3,7},{4,8},{5,9},{6,10},{7,11},{8,12},{9,13},{1... | collective-permute-start | bytes 1032200 | tf_op jit(solution)/shard_map/ppermute | solution.py:76
  109.5 19.3 %collective-permute-start.16 = (f16[224,768]{1,0:T(8,128)(2,1)}, f16[224,768]{1,0:T(8,128)(2,1)}, u32[]{:S(2)}, u32[]{:S(2)}) collective-permute-start(f16[224,768]{1,0:T(8,128)(2,1)} %get-tuple-element.24), channel_id=1, source_target_pairs={{0,12},{1,13},{2,14},{3,15},{4,0},{5,1},{6,2},{7,3},{8,4},{9,5},{1... | collective-permute-start | bytes 1032200 | tf_op jit(solution)/shard_map/ppermute | solution.py:77
  112.1 16.7 %collective-permute-start.17 = (f16[224,768]{1,0:T(8,128)(2,1)}, f16[224,768]{1,0:T(8,128)(2,1)}, u32[]{:S(2)}, u32[]{:S(2)}) collective-permute-start(f16[224,768]{1,0:T(8,128)(2,1)} %get-tuple-element.25), channel_id=1, source_target_pairs={{0,8},{1,9},{2,10},{3,11},{4,12},{5,13},{6,14},{7,15},{8,0},{9,1},... | collective-permute-start | bytes 1032200 | tf_op jit(solution)/shard_map/ppermute | solution.py:78
  117.6 13.9 %copy-start.19 = (s32[4]{0:T(128)S(1)}, s32[4]{0:T(128)}, u32[]{:S(2)}) copy-start(s32[4]{0:T(128)} %constant.222.clone) | copy-start | bytes 52
  117.6 24.0 %copy-start.17 = (s32[8,2]{0,1:T(2,128)S(1)}, s32[8,2]{0,1:T(2,128)}, u32[]{:S(2)}) copy-start(s32[8,2]{0,1:T(2,128)} %param.12) | copy-start | bytes 196
  117.6 16.2 %collective-permute-start.18 = (f16[224,768]{1,0:T(8,128)(2,1)S(1)}, f16[224,768]{1,0:T(8,128)(2,1)S(1)}, u32[]{:S(2)}, u32[]{:S(2)}) collective-permute-start(f16[224,768]{1,0:T(8,128)(2,1)S(1)} %get-tuple-element.13), channel_id=1, source_target_pairs={{0,32},{16,48},{32,64},{48,80},{64,96},{80,112},{96,0},{112,16},{1... | collective-permute-start | bytes 1032200 | tf_op jit(solution)/shard_map/ppermute | solution.py:204
  117.7 18.0 %collective-permute-start.20 = (f16[224,768]{1,0:T(8,128)(2,1)S(1)}, f16[224,768]{1,0:T(8,128)(2,1)S(1)}, u32[]{:S(2)}, u32[]{:S(2)}) collective-permute-start(f16[224,768]{1,0:T(8,128)(2,1)S(1)} %get-tuple-element.13), channel_id=1, source_target_pairs={{0,96},{16,112},{32,0},{48,16},{64,32},{80,48},{96,64},{112,80},{1... | collective-permute-start | bytes 1032200 | tf_op jit(solution)/shard_map/ppermute | solution.py:205
  119.1 16.5 %collective-permute-start.24 = (f16[224,768]{1,0:T(8,128)(2,1)S(1)}, f16[224,768]{1,0:T(8,128)(2,1)S(1)}, u32[]{:S(2)}, u32[]{:S(2)}) collective-permute-start(f16[224,768]{1,0:T(8,128)(2,1)S(1)} %get-tuple-element.13), channel_id=1, source_target_pairs={{0,16},{16,0},{32,48},{48,32},{64,80},{80,64},{96,112},{112,96},{1... | collective-permute-start | bytes 1032200 | tf_op jit(solution)/shard_map/ppermute | solution.py:208
  131.1 9.7 %collective-permute-start.21 = (f16[224,768]{1,0:T(8,128)(2,1)S(1)}, f16[224,768]{1,0:T(8,128)(2,1)S(1)}, u32[]{:S(2)}, u32[]{:S(2)}) collective-permute-start(f16[224,768]{1,0:T(8,128)(2,1)S(1)} %get-tuple-element.15), channel_id=1, source_target_pairs={{0,96},{16,112},{32,0},{48,16},{64,32},{80,48},{96,64},{112,80},{1... | collective-permute-start | bytes 1032200 | tf_op jit(solution)/shard_map/ppermute | solution.py:205
  131.5 11.2 %collective-permute-start.19 = (f16[224,768]{1,0:T(8,128)(2,1)S(1)}, f16[224,768]{1,0:T(8,128)(2,1)S(1)}, u32[]{:S(2)}, u32[]{:S(2)}) collective-permute-start(f16[224,768]{1,0:T(8,128)(2,1)S(1)} %get-tuple-element.15), channel_id=1, source_target_pairs={{0,32},{16,48},{32,64},{48,80},{64,96},{80,112},{96,0},{112,16},{1... | collective-permute-start | bytes 1032200 | tf_op jit(solution)/shard_map/ppermute | solution.py:204
  133.9 10.6 %collective-permute-start.25 = (f16[224,768]{1,0:T(8,128)(2,1)S(1)}, f16[224,768]{1,0:T(8,128)(2,1)S(1)}, u32[]{:S(2)}, u32[]{:S(2)}) collective-permute-start(f16[224,768]{1,0:T(8,128)(2,1)S(1)} %get-tuple-element.15), channel_id=1, source_target_pairs={{0,16},{16,0},{32,48},{48,32},{64,80},{80,64},{96,112},{112,96},{1... | collective-permute-start | bytes 1032200 | tf_op jit(solution)/shard_map/ppermute | solution.py:208
  135.7 11.4 %collective-permute-start.22 = (f16[224,768]{1,0:T(8,128)(2,1)S(1)}, f16[224,768]{1,0:T(8,128)(2,1)S(1)}, u32[]{:S(2)}, u32[]{:S(2)}) collective-permute-start(f16[224,768]{1,0:T(8,128)(2,1)S(1)} %collective-permute-done.18), channel_id=1, source_target_pairs={{0,32},{16,48},{32,64},{48,80},{64,96},{80,112},{96,0},{112,16},{1... | collective-permute-start | bytes 1032200 | tf_op jit(solution)/shard_map/ppermute | solution.py:206
  135.7 13.8 %collective-permute-start.26 = (f16[224,768]{1,0:T(8,128)(2,1)S(1)}, f16[224,768]{1,0:T(8,128)(2,1)S(1)}, u32[]{:S(2)}, u32[]{:S(2)}) collective-permute-start(f16[224,768]{1,0:T(8,128)(2,1)S(1)} %collective-permute-done.18), channel_id=1, source_target_pairs={{0,16},{16,0},{32,48},{48,32},{64,80},{80,64},{96,112},{112,96},{1... | collective-permute-start | bytes 1032200 | tf_op jit(solution)/shard_map/ppermute | solution.py:208
  140.8 8.7 %collective-permute-start.23 = (f16[224,768]{1,0:T(8,128)(2,1)S(1)}, f16[224,768]{1,0:T(8,128)(2,1)S(1)}, u32[]{:S(2)}, u32[]{:S(2)}) collective-permute-start(f16[224,768]{1,0:T(8,128)(2,1)S(1)} %collective-permute-done.21), channel_id=1, source_target_pairs={{0,96},{16,112},{32,0},{48,16},{64,32},{80,48},{96,64},{112,80},{1... | collective-permute-start | bytes 1032200 | tf_op jit(solution)/shard_map/ppermute | solution.py:206
  142.7 10.5 %collective-permute-start.29 = (f16[224,768]{1,0:T(8,128)(2,1)S(1)}, f16[224,768]{1,0:T(8,128)(2,1)S(1)}, u32[]{:S(2)}, u32[]{:S(2)}) collective-permute-start(f16[224,768]{1,0:T(8,128)(2,1)S(1)} %collective-permute-done.21), channel_id=1, source_target_pairs={{0,16},{16,0},{32,48},{48,32},{64,80},{80,64},{96,112},{112,96},{1... | collective-permute-start | bytes 1032200 | tf_op jit(solution)/shard_map/ppermute | solution.py:208
  144.5 8.6 %collective-permute-start.28 = (f16[224,768]{1,0:T(8,128)(2,1)S(1)}, f16[224,768]{1,0:T(8,128)(2,1)S(1)}, u32[]{:S(2)}, u32[]{:S(2)}) collective-permute-start(f16[224,768]{1,0:T(8,128)(2,1)S(1)} %collective-permute-done.20), channel_id=1, source_target_pairs={{0,16},{16,0},{32,48},{48,32},{64,80},{80,64},{96,112},{112,96},{1... | collective-permute-start | bytes 1032200 | tf_op jit(solution)/shard_map/ppermute | solution.py:208
  147.1 6.1 %collective-permute-start.27 = (f16[224,768]{1,0:T(8,128)(2,1)S(1)}, f16[224,768]{1,0:T(8,128)(2,1)S(1)}, u32[]{:S(2)}, u32[]{:S(2)}) collective-permute-start(f16[224,768]{1,0:T(8,128)(2,1)S(1)} %collective-permute-done.19), channel_id=1, source_target_pairs={{0,16},{16,0},{32,48},{48,32},{64,80},{80,64},{96,112},{112,96},{1... | collective-permute-start | bytes 1032200 | tf_op jit(solution)/shard_map/ppermute | solution.py:208
  149.5 3.8 %collective-permute-start.30 = (f16[224,768]{1,0:T(8,128)(2,1)S(1)}, f16[224,768]{1,0:T(8,128)(2,1)S(1)}, u32[]{:S(2)}, u32[]{:S(2)}) collective-permute-start(f16[224,768]{1,0:T(8,128)(2,1)S(1)} %collective-permute-done.22), channel_id=1, source_target_pairs={{0,16},{16,0},{32,48},{48,32},{64,80},{80,64},{96,112},{112,96},{1... | collective-permute-start | bytes 1032200 | tf_op jit(solution)/shard_map/ppermute | solution.py:208
  149.5 4.2 %collective-permute-start.31 = (f16[224,768]{1,0:T(8,128)(2,1)S(1)}, f16[224,768]{1,0:T(8,128)(2,1)S(1)}, u32[]{:S(2)}, u32[]{:S(2)}) collective-permute-start(f16[224,768]{1,0:T(8,128)(2,1)S(1)} %collective-permute-done.23), channel_id=1, source_target_pairs={{0,16},{16,0},{32,48},{48,32},{64,80},{80,64},{96,112},{112,96},{1... | collective-permute-start | bytes 1032200 | tf_op jit(solution)/shard_map/ppermute | solution.py:208
  (9 other events, 17.9 us)
Sparse Core Ops, SparseCore 0:
  10.6 38.4 all-gather.4
  50.8 37.6 all-gather.2

commit v2 on v0

v2 whole, which is shorter than its diff:
```python
import functools

import jax
import jax.numpy as jnp
from jax import lax
from jax.experimental import pallas as pl
from jax.experimental.pallas import tpu as pltpu
from jax.sharding import PartitionSpec as P

F16 = jnp.float16
F32 = jnp.float32
NY, NZ, NX = 4, 4, 4
WINDOW = 656
CHUNKS = ((0, 176), (176, 160), (336, 160), (496, 160))
SCALE = 64.0


def plane_shift(d, first):
    pairs = []
    for e in range(2 * NX):
        along_y = (e % 2 == 0) == first
        for j in range(NY * NZ):
            y, z = j // NZ, j % NZ
            to = ((y + d) % NY) * NZ + z if along_y else y * NZ + (z + d) % NZ
            pairs.append((e * NY * NZ + j, e * NY * NZ + to))
    return pairs


def send(value, d, first):
    return lax.ppermute(value, ("expert", "dp"), plane_shift(d, first))


def x_shift(d):
    return [(e, ((e // 2 + d) % NX) * 2 + e % 2) for e in range(2 * NX)]


def send_x(value):
    pairs = [(e, ((e // 2 + (1 if e % 2 == 0 else -1)) % NX) * 2 + e % 2) for e in range(2 * NX)]
    return lax.ppermute(value, "expert", pairs)


def core_swap():
    return [(e, e ^ 1) for e in range(2 * NX)]


def encode_state(w, m, v):
    root = jnp.sqrt(jnp.sqrt(jnp.sqrt(jnp.minimum(jnp.abs(m) * (1.0 / 0.75), 1.0))))
    qm = jnp.round(jnp.where(m < 0, -root, root) * 32767.0).astype(jnp.int32)
    qv = jnp.round(jnp.sqrt(jnp.clip(v * 5.0, 0.0, 1.0)) * 65535.0).astype(jnp.int32)
    return jnp.stack([(w * 2.0**32).astype(jnp.int32), qm * 65536 + qv])


def decode_moments(code):
    qm = lax.shift_right_arithmetic(code, jnp.int32(16)).astype(F32) * (1.0 / 32767.0)
    qv = (code & jnp.int32(0xFFFF)).astype(F32) * (1.0 / 65535.0)
    m2 = qm * qm
    m4 = m2 * m2
    m8 = m4 * m4 * 0.75
    return jnp.where(qm < 0, -m8, m8), qv * qv * 0.2


def partial_kernel(which, here, counts, x, c, *refs):
    outs, (rows, plain, masked, total, load_sems, cot_sem, sems) = refs[:4], refs[4:]
    step = pl.program_id(0)
    core, y, z = here[0], here[1], here[2]
    first, second = counts[y * NZ + z, 0], counts[y * NZ + z, 1]
    if which == 0:
        start, low, high = 0, 0, first
    else:
        start = pl.multiple_of(jnp.minimum(first // 16 * 16, x.shape[0] - WINDOW), 16)
        low, high = first - start, first + second - start
    shard = total.shape[2]
    width = rows.shape[2]
    slot = lax.rem(step, 2)

    def loads(i):
        column = pl.multiple_of(lax.rem(y + 2 + i, NY) * width, width)
        for k, (at, size) in enumerate(CHUNKS):
            yield pltpu.make_async_copy(
                x.at[pl.ds(start + at, size), pl.ds(column, width)],
                rows.at[i, pl.ds(at, size)],
                load_sems.at[i, k],
            )

    @pl.when(step == 0)
    def _():
        cot_load = pltpu.make_async_copy(c.at[pl.ds(start, WINDOW)], plain, cot_sem)
        cot_load.start()
        for i in range(NY):
            for copy in loads(i):
                copy.start()
        cot_load.wait()
        index = lax.broadcasted_iota(jnp.int32, masked.shape, 0)
        value = plain[...].astype(F32) * SCALE
        masked[...] = jnp.where((index >= low) & (index < high), value, 0.0).astype(jnp.bfloat16)

    for copy in loads(step):
        copy.wait()
    product = lax.dot_general(
        rows[step], masked[...], (((0,), (0,)), ((), ())), preferred_element_type=F32
    )

    def wait(slot):
        for b in range(NZ):
            pltpu.make_async_copy(total.at[slot, b], outs[0].at[b], sems.at[slot, b]).wait()

    @pl.when(step >= 2)
    def _():
        wait(slot)

    block = lax.rem(y + 2 + step, NY)
    for b in range(NZ):
        total[slot, b] = product[b * shard : (b + 1) * shard]
        far = jnp.where(core == 0, lax.rem(2 + step, NY), lax.rem(b - z + NZ, NZ))
        place = jnp.where(core == 0, b, block)
        for d in range(4):

            @pl.when(far == d)
            def _():
                pltpu.make_async_copy(
                    total.at[slot, b], outs[d].at[place], sems.at[slot, b]
                ).start()

    @pl.when(step == NY - 1)
    def _():
        wait(1 - slot)
        wait(slot)


def partial(which, here, counts, inputs, cot, shard):
    rows, width_d = inputs.shape
    width_h = cot.shape[1]
    block = width_d // NY
    return pl.pallas_call(
        functools.partial(partial_kernel, which),
        grid_spec=pltpu.PrefetchScalarGridSpec(
            num_scalar_prefetch=2,
            grid=(NY,),
            in_specs=[
                pl.BlockSpec(memory_space=pl.ANY),
                pl.BlockSpec(memory_space=pl.ANY),
            ],
            out_specs=[pl.BlockSpec(memory_space=pltpu.HBM)] * 4,
            scratch_shapes=[
                pltpu.VMEM((NY, WINDOW, block), jnp.bfloat16),
                pltpu.VMEM((WINDOW, width_h), jnp.bfloat16),
                pltpu.VMEM((WINDOW, width_h), jnp.bfloat16),
                pltpu.VMEM((2, NZ, shard, width_h), F32),
                pltpu.SemaphoreType.DMA((NY, len(CHUNKS))),
                pltpu.SemaphoreType.DMA,
                pltpu.SemaphoreType.DMA((2, NZ)),
            ],
        ),
        out_shape=[pltpu.HBM((4, shard, width_h), F32)] * 4,
        compiler_params=pltpu.CompilerParams(vmem_limit_bytes=20 << 20),
        cost_estimate=pl.CostEstimate(
            flops=2 * WINDOW * width_d * width_h * 4, bytes_accessed=rows * width_d * 8, transcendentals=0
        ),
    )(here, counts, inputs, cot)


def exchange(total, me):
    def block(d):
        return lax.dynamic_index_in_dim(total, (me + d) % 4, 0, keepdims=False)

    return [block(0), send(block(1), 1, False), send(block(3), -1, False), send(block(2), 2, False)]


def add_up(parts):
    return sum(p.astype(F32) for p in parts)


def prepare_kernel(pick, *refs):
    sources = [ref.at[i] for ref in refs[:3] for i in range(2)] + list(refs[3:5])
    held, state, sems = refs[5:]
    for s in range(2):
        for k in range(8):

            @pl.when(pick[s] == k)
            def _():
                pltpu.make_async_copy(sources[k], state.at[s], sems.at[s]).start()

    for s in range(2):
        pltpu.make_async_copy(sources[0], state.at[s], sems.at[s]).wait()

        @pl.loop(0, state.shape[2], step=32)
        def _(at):
            part = pl.ds(pl.multiple_of(at, 32), 32)
            m, v = decode_moments(state[s, 1, part])
            held[0, s, part] = state[s, 0, part].astype(F32) * 2.0**-32
            held[1, s, part] = 0.9 * m
            held[2, s, part] = 0.95 * v


def prepare(pick, pairs, singles):
    _, rows, cols = singles[0].shape
    sources = pairs + singles
    sources = [pltpu.with_memory_space_constraint(v, pltpu.HBM) for v in sources]
    return pl.pallas_call(
        prepare_kernel,
        grid_spec=pltpu.PrefetchScalarGridSpec(
            num_scalar_prefetch=1,
            grid=(1,),
            in_specs=[pl.BlockSpec(memory_space=pl.ANY)] * 5,
            out_specs=pl.BlockSpec((3, 2, rows, cols), lambda i, pick: (0, 0, 0, 0)),
            scratch_shapes=[
                pltpu.VMEM((2, 2, rows, cols), jnp.int32),
                pltpu.SemaphoreType.DMA((2,)),
            ],
        ),
        out_shape=jax.ShapeDtypeStruct((3, 2, rows, cols), F32),
        compiler_params=pltpu.CompilerParams(vmem_limit_bytes=16 << 20),
    )(pick, *sources)


def adam_tail(gradient, w, m_decayed, v_decayed):
    first_new = m_decayed + 0.1 * gradient
    second_new = v_decayed + 0.05 * gradient * gradient
    root = jnp.sqrt(second_new * (1.0 / (1.0 - 0.95**20))) + 1e-08
    corrected = first_new * (1.0 / (1.0 - 0.9**20)) / root
    return w - 0.001 * (corrected + 0.1 * w), first_new, second_new


def adam_kernel(grad, w, m, v, held, master_out, hw, hf, hs):
    master_out[...] = adam_tail(grad[0], w[...], 0.9 * m[...], 0.95 * v[...])[0]
    for s in range(2):
        nw, nf, ns = adam_tail(grad[1 + s], held[0, s], held[1, s], held[2, s])
        hw[s] = nw.astype(jnp.bfloat16)
        hf[s] = nf
        hs[s] = ns


def finish(grads, w, m, v, held):
    rows, cols = w.shape
    step = 32
    flat = pl.BlockSpec((step, cols), lambda i: (i, 0))
    pair = pl.BlockSpec((2, step, cols), lambda i: (0, i, 0))
    return pl.pallas_call(
        adam_kernel,
        grid=(rows // step,),
        in_specs=[pl.BlockSpec((3, step, cols), lambda i: (0, i, 0)), flat, flat, flat]
        + [pl.BlockSpec((3, 2, step, cols), lambda i: (0, 0, i, 0))],
        out_specs=[flat, pair, pair, pair],
        out_shape=[
            jax.ShapeDtypeStruct((rows, cols), F32),
            jax.ShapeDtypeStruct((2, rows, cols), jnp.bfloat16),
            jax.ShapeDtypeStruct((2, rows, cols), F32),
            jax.ShapeDtypeStruct((2, rows, cols), F32),
        ],
        compiler_params=pltpu.CompilerParams(vmem_limit_bytes=10 << 20),
    )(grads, w, m, v, held)


def body(
    saved_inputs,
    saved_cotangents,
    row_counts,
    old_slots,
    new_slots,
    master,
    first_moment,
    second_moment,
):
    expert_index = lax.axis_index("expert")
    data_index = lax.axis_index("dp")
    y, z = data_index // NZ, data_index % NZ
    x, core = expert_index // 2, expert_index % 2
    inputs = saved_inputs[0]
    cot = saved_cotangents[0]
    rows = inputs.shape[0]
    shard = master.shape[1]
    offsets = jnp.array([0, 3, 1, 2], jnp.int32)
    ids = old_slots.reshape(NX, 2, 2)[(x + offsets) % NX]
    ids = jnp.where(core == 0, ids, ids[:, ::-1]).transpose(1, 0, 2).reshape(16)
    mine_new = lax.dynamic_index_in_dim(new_slots, expert_index, 0, keepdims=False)
    targets = jnp.concatenate([expert_index[None].astype(jnp.int32), mine_new])
    table = jnp.where(ids[:, None] == targets[None, :], 0.125, 0.0).astype(F32)

    here = jnp.stack([core, y, z])
    inputs = pltpu.with_memory_space_constraint(inputs, pltpu.HBM)
    cot = pltpu.with_memory_space_constraint(cot, pltpu.HBM)
    part0 = partial(0, here, row_counts[0], inputs, cot, shard)
    far_up = send(part0[2].astype(F16), 1, True)
    raw_down = send(part0[3].astype(F16), -1, True)
    w_late, m_late, v_late, part0 = lax.optimization_barrier(
        (master[0], first_moment[0], second_moment[0], part0)
    )
    state = encode_state(w_late, m_late, v_late)
    pair = jnp.stack([state, lax.ppermute(state, "expert", core_swap())])
    beside = send_x(pair)
    far_state = send_x(beside[0])
    pairs = [pair, beside, lax.ppermute(beside, "expert", core_swap())]
    singles = [far_state, lax.ppermute(far_state, "expert", core_swap())]
    cot, state = lax.optimization_barrier((cot, state))
    part1 = partial(1, here, row_counts[0], inputs, cot, shard)
    part1, far_up, raw_down = lax.optimization_barrier((part1, far_up, raw_down))
    far_down = send(part1[2].astype(F16), -1, True)
    raw_up = send(part1[1].astype(F16), 1, True)

    far_down, raw_up = lax.optimization_barrier((far_down, raw_up))
    both_up = send((part0[1] + far_up.astype(F32)).astype(F16), 1, True)
    both_down = send((part1[3] + far_down.astype(F32)).astype(F16), -1, True)
    sum_a = (part0[0] + both_up.astype(F32) + raw_down.astype(F32)) * 0.5
    sum_b = (part1[0] + raw_up.astype(F32) + both_down.astype(F32)) * 0.5
    me = jnp.where(core == 0, z, y)
    parts_a = exchange(sum_a.astype(F16), me)
    parts_b = exchange(sum_b.astype(F16), me)
    parts_a, parts_b[1] = lax.optimization_barrier((parts_a, parts_b[1]))

    back = 8.0 * 2.0 / SCALE

    def spread(parts):
        own = (add_up(parts) * back).astype(F16)
        return [own] + [lax.ppermute(own, "expert", x_shift(d)) for d in (1, -1, 2)]

    same_a = spread(parts_a)
    same_b = spread(parts_b)
    same_a, same_b[0] = lax.optimization_barrier((same_a, same_b[0]))
    other_a = [lax.ppermute(v, "expert", core_swap()) for v in same_a]
    other_a, pairs, singles, same_b[1] = lax.optimization_barrier(
        (other_a, pairs, singles, same_b[1])
    )

    def weighted(same, other, s):
        total = 0.0
        for k, g in enumerate(same + other):
            total = total + table[2 * k + s][:, None, None] * g.astype(F32)[None]
        return total

    at = (mine_new // 2 - x) % NX
    twist = (mine_new % 2 != core).astype(jnp.int32)
    near = jnp.where((at == 3) == (core == 0), 2 + twist, 5 - twist)
    pick = jnp.where(at == 0, twist, jnp.where(at == 2, 6 + twist, near))
    held = prepare(pick, pairs, singles)
    grads_a = weighted(same_a, other_a, 0)
    same_b[2], same_b[3], held, grads_a = lax.optimization_barrier(
        (same_b[2], same_b[3], held, grads_a)
    )
    other_b = [lax.ppermute(v, "expert", core_swap()) for v in same_b]
    grads = grads_a + weighted(same_b, other_b, 1)
    new_master, held_w, held_first, held_second = finish(
        grads, master[0], first_moment[0], second_moment[0], held
    )
    return new_master[None], held_w, held_first, held_second


def solution(mesh):
    return jax.shard_map(
        body,
        mesh=mesh,
        in_specs=(
            P("expert", "dp", None),
            P("expert", "dp", None),
            P("expert", None, None),
            P(),
            P(),
            P("expert", "dp", None),
            P("expert", "dp", None),
            P("expert", "dp", None),
        ),
        out_specs=(
            P("expert", "dp", None),
            P("expert", "dp", None),
            P("expert", "dp", None),
            P("expert", "dp", None),
        ),
        check_vma=False,
    )
```

time: 383 us -> 160 us (0.42)
  waiting for transfers between devices: 275 us -> 46 us
  matrix products: 46.5 us -> 0 us
  starting transfers between devices: 0.6 us -> 46.9 us
  Pallas kernels: 0 us -> 29.8 us
  local copies, waits for them, and re-layouts: 33.9 us -> 8.07 us
  other arithmetic: 9.11 us -> 25.5 us
  between operations: 13.9 us -> 1.03 us
    unnamed x6 -> x0, waiting for transfers between devices: 140 us -> none
    all_gather x3 -> x0, waiting for transfers between devices: 95.6 us -> none  [the longest x1 35.2 us: body(): lax.all_gather(new_master, 'expert', axis=0, tiled=True)]
    ppermute x0 -> x31, starting transfers between devices: none -> 46.9 us  [the longest x12 16.8 us: send(): return lax.ppermute(value, ('expert', 'dp'), plane_shift(d, first))]
    dot_general x5 -> x0, matrix products: 46.5 us -> none  [the longest x3 24.6 us: body(): jnp.einsum('sk,kdh->sdh', chooser, piece, precision=lax.Precision.HIGHEST)]
    ppermute x0 -> x31, waiting for transfers between devices: none -> 46 us  [the longest x12 32.3 us: send(): return lax.ppermute(value, ('expert', 'dp'), plane_shift(d, first))]
    reduce_scatter x1 -> x0, waiting for transfers between devices: 39.5 us -> none  [body(): lax.psum_scatter(spread, 'expert', scatter_dimension=0, tiled=True)[0]]
    pallas_call x0 -> x4, Pallas kernels: none -> 29.8 us  [the longest x2 22.7 us: partial(): pl.pallas_call(functools.partial(partial_kernel, which), grid_spec=pltpu....]
    unnamed x19 -> x32, local copies, waits for them, and re-layouts: 28.5 us -> 1.53 us
  transfers between devices with their start and end apart: 5 -> 31, of which waited for: 5 -> 12; matrix products, arithmetic and copies ran while one was open for 5% -> 18% of each run, Pallas kernels for 0% -> 9%
where the time goes in v2:
time: 160 us; the launch traced here: 157 us
  starting transfers between devices  46.9 us (29%)
  waiting for transfers between devices  46 us (29%)
  Pallas kernels  29.8 us (19%)
  other arithmetic  25.5 us (16%)
  local copies, waits for them, and re-layouts  8.07 us (5%)
    ppermute x12, waiting for transfers between devices, send(): return lax.ppermute(value, ('expert', 'dp'), plane_shift(d, first))  32.3 us
    pallas_call x2, Pallas kernels, partial(): pl.pallas_call(functools.partial(partial_kernel, which), grid_spec=pltpu....  22.7 us
    ppermute x12, starting transfers between devices, send(): return lax.ppermute(value, ('expert', 'dp'), plane_shift(d, first))  16.8 us
    ppermute x6, waiting for transfers between devices, spread(): return [own] + [lax.ppermute(own, 'expert', x_shift(d)) for d in (1, -1, 2)]  13.3 us
    ppermute x6, starting transfers between devices, spread(): return [own] + [lax.ppermute(own, 'expert', x_shift(d)) for d in (1, -1, 2)]  8.33 us
    ppermute x1, starting transfers between devices, body(): singles = [far_state, lax.ppermute(far_state, 'expert', core_swap())]  7.62 us
    ppermute x4, starting transfers between devices, body(): other_a = [lax.ppermute(v, 'expert', core_swap()) for v in same_a]  6.68 us
    convert_element_type x16, other arithmetic, weighted(): total = total + table[2 * k + s][:, None, None] * g.astype(F32)[None]  5.65 us
  transfers between devices with their start and end apart: 31, of which 12 were waited for; matrix products, arithmetic and copies ran while one was open for 18% of the time, Pallas kernels for 9%

profile of v2, /device:TPU:15, one launch (start us, length us, event | category | flops | bytes accessed | tf_op | source)
XLA Modules:
  0.0 157.4 jit_solution(10530991744069351494)
XLA Ops:
  1.5 11.3 %shard_map.120 = (f32[4,224,768]{2,1,0:T(8,128)}, f32[4,224,768]{2,1,0:T(8,128)}, f32[4,224,768]{2,1,0:T(8,128)}, f32[4,224,768]{2,1,0:T(8,128)}) custom-call(s32[3]{0:T(128)S(1)} %pad_add_fusion.2.here, s32[16,3]{1,0:T(8,128)S(1)} %bitcast.78, bf16[1280,3584]{1,0:T(8,128)(2,1)} %bitcast.82, bf16[1280,768]{1,0:T(8,128)(2,1)} %bitcast.84), custom_call_target="tpu_custom_call" | custom-call | flops 14445182976 | bytes 36700160 | tf_op jit(solution)/shard_map/pallas_call | solution.py:134
  15.8 1.7 %collective-permute-start = (f16[4,224,768]{2,1,0:T(8,128)(2,1)S(1)}, f16[4,224,768]{2,1,0:T(8,128)(2,1)S(1)}, u32[]{:S(2)}, u32[]{:S(2)}) collective-permute-start(f16[4,224,768]{2,1,0:T(8,128)(2,1)S(1)} %convert_element_type.138), channel_id=1, source_target_pairs={{0,4},{1,5},{2,6},{3,7},{4,8},{5,9},{6,10},{7,11},{8,12},{9,13},{1... | collective-permute-start | bytes 4128776 | tf_op jit(solution)/shard_map/ppermute | solution.py:30
  17.7 2.8 %collective-permute-start.1 = (f16[4,224,768]{2,1,0:T(8,128)(2,1)S(1)}, f16[4,224,768]{2,1,0:T(8,128)(2,1)S(1)}, u32[]{:S(2)}, u32[]{:S(2)}) collective-permute-start(f16[4,224,768]{2,1,0:T(8,128)(2,1)S(1)} %convert_element_type.139), channel_id=1, source_target_pairs={{0,12},{1,13},{2,14},{3,15},{4,0},{5,1},{6,2},{7,3},{8,4},{9,5},{1... | collective-permute-start | bytes 4128776 | tf_op jit(solution)/shard_map/ppermute | solution.py:30
  20.6 1.7 %pad_add_fusion.refs_0_ = s32[2,2,224,768]{3,2,1,0:T(8,128)} fusion(s32[1,2,224,768]{3,2,1,0:T(8,128)S(1)} %bitcast.80, s32[1,2,224,768]{3,2,1,0:T(8,128)S(1)} %get-tuple-element.104), kind=kLoop, calls=%fused_computation.1 | loop fusion | flops 688128 | bytes 5505024 | tf_op jit(solution)/shard_map/stack | solution.py:289
  22.8 11.4 %shard_map.121 = (f32[4,224,768]{2,1,0:T(8,128)}, f32[4,224,768]{2,1,0:T(8,128)}, f32[4,224,768]{2,1,0:T(8,128)}, f32[4,224,768]{2,1,0:T(8,128)}) custom-call(s32[3]{0:T(128)S(1)} %pad_add_fusion.2.here, s32[16,3]{1,0:T(8,128)S(1)} %bitcast.79, bf16[1280,3584]{1,0:T(8,128)(2,1)} %bitcast.83, bf16[1280,768]{1,0:T(8,128)(2,1)} %bitcast.85), custom_call_target="tpu_custom_call" | custom-call | flops 14445182976 | bytes 36700160 | tf_op jit(solution)/shard_map/pallas_call | solution.py:134
  34.2 1.1 collective-permute-done
  35.8 2.1 %convert_element_type.140 = f16[4,224,768]{2,1,0:T(8,128)(2,1)S(1)} convert(f32[4,224,768]{2,1,0:T(8,128)} %get-tuple-element.67) | non-fusion elementwise | flops 688128 | bytes 4128768 | tf_op jit(solution)/shard_map/convert_element_type | solution.py:297
  37.9 3.2 %collective-permute-start.2 = (f16[4,224,768]{2,1,0:T(8,128)(2,1)S(1)}, f16[4,224,768]{2,1,0:T(8,128)(2,1)S(1)}, u32[]{:S(2)}, u32[]{:S(2)}) collective-permute-start(f16[4,224,768]{2,1,0:T(8,128)(2,1)S(1)} %convert_element_type.140), channel_id=1, source_target_pairs={{0,12},{1,13},{2,14},{3,15},{4,0},{5,1},{6,2},{7,3},{8,4},{9,5},{1... | collective-permute-start | bytes 4128776 | tf_op jit(solution)/shard_map/ppermute | solution.py:30
  41.4 1.5 add_convert_fusion
  42.9 13.5 %collective-permute-done.2 = f16[4,224,768]{2,1,0:T(8,128)(2,1)S(1)} collective-permute-done((f16[4,224,768]{2,1,0:T(8,128)(2,1)S(1)}, f16[4,224,768]{2,1,0:T(8,128)(2,1)S(1)}, u32[]{:S(2)}, u32[]{:S(2)}) %collective-permute-start.2) | collective-permute-done | bytes 1376288 | tf_op jit(solution)/shard_map/ppermute | solution.py:30
  56.4 3.4 %collective-permute-done.3 = f16[4,224,768]{2,1,0:T(8,128)(2,1)S(1)} collective-permute-done((f16[4,224,768]{2,1,0:T(8,128)(2,1)S(1)}, f16[4,224,768]{2,1,0:T(8,128)(2,1)S(1)}, u32[]{:S(2)}, u32[]{:S(2)}) %collective-permute-start.3) | collective-permute-done | bytes 1376288 | tf_op jit(solution)/shard_map/ppermute | solution.py:30
  59.8 1.5 add_convert_fusion.1
  61.3 2.6 %slice_bitcast_fusion = s32[2,224,768]{2,1,0:T(8,128)} fusion(s32[2,2,224,768]{3,2,1,0:T(8,128)} %collective-permute-done.22.refs_1_), kind=kLoop, calls=%fused_computation.8 | loop fusion | bytes 2752512 | tf_op jit(solution)/shard_map/squeeze | solution.py:291
  64.5 2.7 %collective-permute-start.23 = (s32[2,2,224,768]{3,2,1,0:T(8,128)}, s32[2,2,224,768]{3,2,1,0:T(8,128)}, u32[]{:S(2)}, u32[]{:S(2)}) collective-permute-start(s32[2,2,224,768]{3,2,1,0:T(8,128)} %collective-permute-done.22.refs_1_), channel_id=1, source_target_pairs={{0,16},{16,0},{32,48},{48,32},{64,80},{80,64},{96,112},{112,96},{1... | collective-permute-start | bytes 8257544 | tf_op jit(solution)/shard_map/ppermute | solution.py:292
  67.2 7.4 %collective-permute-done.5 = f16[4,224,768]{2,1,0:T(8,128)(2,1)} collective-permute-done((f16[4,224,768]{2,1,0:T(8,128)(2,1)}, f16[4,224,768]{2,1,0:T(8,128)(2,1)}, u32[]{:S(2)}, u32[]{:S(2)}) %collective-permute-start.5) | collective-permute-done | bytes 1376288 | tf_op jit(solution)/shard_map/ppermute | solution.py:30
  74.6 2.3 %multiply_convert_fusion = f16[4,224,768]{2,1,0:T(8,128)(2,1)S(1)} fusion(f16[4,224,768]{2,1,0:T(8,128)(2,1)S(1)} %collective-permute-done.1, f32[4,224,768]{2,1,0:T(8,128)S(1)} %copy-done.4, f16[4,224,768]{2,1,0:T(8,128)(2,1)} %collective-permute-done.5), kind=kLoop, calls=%fused_computation.2 | loop fusion | flops 4128768 | bytes 6881280 | tf_op jit(solution)/shard_map/convert_element_type | solution.py:306
  76.9 1.1 dynamic-slice_bitcast_fusion.3
  78.0 1.3 collective-permute-start.6
  79.5 2.7 %collective-permute-start.8 = (f16[224,768]{1,0:T(8,128)(2,1)}, f16[224,768]{1,0:T(8,128)(2,1)}, u32[]{:S(2)}, u32[]{:S(2)}) collective-permute-start(f16[224,768]{1,0:T(8,128)(2,1)} %get-tuple-element.109), channel_id=1, source_target_pairs={{0,2},{1,3},{2,0},{3,1},{4,6},{5,7},{6,4},{7,5},{8,10},{9,11},{10,... | collective-permute-start | bytes 1032200 | tf_op jit(solution)/shard_map/ppermute | solution.py:30
  82.1 2.1 %multiply_convert_fusion.1 = f16[4,224,768]{2,1,0:T(8,128)(2,1)S(1)} fusion(f16[4,224,768]{2,1,0:T(8,128)(2,1)} %collective-permute-done.4, f32[4,224,768]{2,1,0:T(8,128)S(1)} %copy-done.5, f16[4,224,768]{2,1,0:T(8,128)(2,1)S(1)} %copy-done.12), kind=kLoop, calls=%fused_computation.4 | loop fusion | flops 4128768 | bytes 6881280 | tf_op jit(solution)/shard_map/convert_element_type | solution.py:307
  84.3 1.1 dynamic-slice_bitcast_fusion.2
  86.7 3.1 %collective-permute-start.10 = (f16[224,768]{1,0:T(8,128)(2,1)}, f16[224,768]{1,0:T(8,128)(2,1)}, u32[]{:S(2)}, u32[]{:S(2)}) collective-permute-start(f16[224,768]{1,0:T(8,128)(2,1)} %get-tuple-element.108), channel_id=1, source_target_pairs={{0,3},{1,0},{2,1},{3,2},{4,7},{5,4},{6,5},{7,6},{8,11},{9,8},{10,9... | collective-permute-start | bytes 1032200 | tf_op jit(solution)/shard_map/ppermute | solution.py:30
  89.8 1.3 collective-permute-done.8
  91.0 1.2 collective-permute-start.11
  92.8 2.2 %multiply_convert_fusion.2 = f16[224,768]{1,0:T(8,128)(2,1)} fusion(f16[224,768]{1,0:T(8,128)(2,1)} %collective-permute-done.8, f16[224,768]{1,0:T(8,128)(2,1)} %collective-permute-done.7, f16[224,768]{1,0:T(8,128)(2,1)} %copy-done.13, f16[224,768]{1,0:T(8,128)(2,1)} %get-tuple-element.77), kind=kLoop, calls=%fused_computation.22 | loop fusion | flops 1548288 | bytes 1720320 | tf_op jit(solution)/shard_map/convert_element_type | solution.py:313
  95.3 1.2 collective-permute-start.15
  96.5 4.7 %collective-permute-done.11 = f16[224,768]{1,0:T(8,128)(2,1)} collective-permute-done((f16[224,768]{1,0:T(8,128)(2,1)}, f16[224,768]{1,0:T(8,128)(2,1)}, u32[]{:S(2)}, u32[]{:S(2)}) %collective-permute-start.11) | collective-permute-done | bytes 344096 | tf_op jit(solution)/shard_map/ppermute | solution.py:30
  101.2 1.1 collective-permute-start.16
  102.3 7.6 %collective-permute-start.25 = (s32[2,224,768]{2,1,0:T(8,128)}, s32[2,224,768]{2,1,0:T(8,128)}, u32[]{:S(2)}, u32[]{:S(2)}) collective-permute-start(s32[2,224,768]{2,1,0:T(8,128)} %collective-permute-done.24.refs_3_), channel_id=1, source_target_pairs={{0,16},{16,0},{32,48},{48,32},{64,80},{80,64},{96,112},{112,96},{1... | collective-permute-start | bytes 4128776 | tf_op jit(solution)/shard_map/ppermute | solution.py:293
  110.5 2.2 %fusion.9 = f16[224,768]{1,0:T(8,128)(2,1)} fusion(f16[224,768]{1,0:T(8,128)(2,1)} %collective-permute-done.11, f16[224,768]{1,0:T(8,128)(2,1)} %collective-permute-done.10, f16[224,768]{1,0:T(8,128)(2,1)} %collective-permute-done.9, f16[4,224,768]{2,1,0:T(8,128)(2,1)S(1)} %multiply_convert_fusion.1, s32[]{:T(128)S(6)} %select_n.121), kind=kLoop, calls=%fused_computation.21 | loop fusion | flops 1548288 | bytes 1720324 | tf_op jit(solution)/shard_map/convert_element_type | solution.py:313
  112.7 1.8 %collective-permute-start.26 = (f16[224,768]{1,0:T(8,128)(2,1)}, f16[224,768]{1,0:T(8,128)(2,1)S(1)}, u32[]{:S(2)}, u32[]{:S(2)}) collective-permute-start(f16[224,768]{1,0:T(8,128)(2,1)} %fusion.9), channel_id=1, source_target_pairs={{0,32},{16,48},{32,64},{48,80},{64,96},{80,112},{96,0},{112,16},{1... | collective-permute-start | bytes 1032200 | tf_op jit(solution)/shard_map/ppermute | solution.py:314
  114.5 4.9 %collective-permute-start.17 = (f16[224,768]{1,0:T(8,128)(2,1)}, f16[224,768]{1,0:T(8,128)(2,1)S(1)}, u32[]{:S(2)}, u32[]{:S(2)}) collective-permute-start(f16[224,768]{1,0:T(8,128)(2,1)} %multiply_convert_fusion.2), channel_id=1, source_target_pairs={{0,16},{16,0},{32,48},{48,32},{64,80},{80,64},{96,112},{112,96},{1... | collective-permute-start | bytes 1032200 | tf_op jit(solution)/shard_map/ppermute | solution.py:319
  119.9 3.3 %collective-permute-done.26 = f16[224,768]{1,0:T(8,128)(2,1)S(1)} collective-permute-done((f16[224,768]{1,0:T(8,128)(2,1)}, f16[224,768]{1,0:T(8,128)(2,1)S(1)}, u32[]{:S(2)}, u32[]{:S(2)}) %collective-permute-start.26) | collective-permute-done | bytes 344096 | tf_op jit(solution)/shard_map/ppermute | solution.py:314
  123.2 1.8 %collective-permute-start.19 = (f16[224,768]{1,0:T(8,128)(2,1)}, f16[224,768]{1,0:T(8,128)(2,1)S(1)}, u32[]{:S(2)}, u32[]{:S(2)}) collective-permute-start(f16[224,768]{1,0:T(8,128)(2,1)} %collective-permute-done.15), channel_id=1, source_target_pairs={{0,16},{16,0},{32,48},{48,32},{64,80},{80,64},{96,112},{112,96},{1... | collective-permute-start | bytes 1032200 | tf_op jit(solution)/shard_map/ppermute | solution.py:319
  125.0 1.0 convert_element_type.164
  126.1 1.0 convert_element_type.165
  127.1 1.0 convert_element_type.166
  128.1 1.0 convert_element_type.167
  129.8 3.3 %collective-permute-start.13 = (f16[224,768]{1,0:T(8,128)(2,1)}, f16[224,768]{1,0:T(8,128)(2,1)S(1)}, u32[]{:S(2)}, u32[]{:S(2)}) collective-permute-start(f16[224,768]{1,0:T(8,128)(2,1)} %fusion.9), channel_id=1, source_target_pairs={{0,64},{16,80},{32,96},{48,112},{64,0},{80,16},{96,32},{112,48},{1... | collective-permute-start | bytes 1032200 | tf_op jit(solution)/shard_map/ppermute | solution.py:314
  133.1 1.1 collective-permute-start.27
  134.4 2.9 %shard_map.122.held = f32[3,2,224,768]{3,2,1,0:T(8,128)S(1)} custom-call(s32[2]{0:T(128)S(1)} %compare_select_fusion.8.pick, s32[2,2,224,768]{3,2,1,0:T(8,128)} %pad_add_fusion.refs_0_, s32[2,2,224,768]{3,2,1,0:T(8,128)} %collective-permute-done.22.refs_1_, s32[2,2,224,768]{3,2,1,0:T(8,128)} %collective-permute-done.23.refs_2_, ...), custom_call_target="tpu_custom_call" | custom-call | tf_op jit(solution)/shard_map/pallas_call | solution.py:199
  137.3 1.1 multiply_add_fusion
  138.3 1.4 collective-permute-done.12
  139.8 8.5 %collective-permute-done.13 = f16[224,768]{1,0:T(8,128)(2,1)S(1)} collective-permute-done((f16[224,768]{1,0:T(8,128)(2,1)}, f16[224,768]{1,0:T(8,128)(2,1)S(1)}, u32[]{:S(2)}, u32[]{:S(2)}) %collective-permute-start.13) | collective-permute-done | bytes 344096 | tf_op jit(solution)/shard_map/ppermute | solution.py:314
  148.3 1.4 collective-permute-start.29
  150.2 1.0 convert_element_type.172
  152.0 1.1 add_add_fusion.grad
  153.1 4.3 %shard_map.123 = (f32[224,768]{1,0:T(8,128)}, bf16[2,224,768]{2,1,0:T(8,128)(2,1)}, f32[2,224,768]{2,1,0:T(8,128)}, f32[2,224,768]{2,1,0:T(8,128)}) custom-call(f32[3,224,768]{2,1,0:T(8,128)S(1)} %add_add_fusion.grad, f32[224,768]{1,0:T(8,128)S(1)} %bitcast.73, f32[224,768]{1,0:T(8,128)S(1)} %bitcast.75, f32[224,768]{1,0:T(8,128)S(1)} %bitcast.77, ...), custom_call_target="tpu_custom_call" | custom-call | tf_op jit(solution)/shard_map/pallas_call | solution.py:238
  (100 shorter events, 11.3 us)
Async XLA Ops:
  0.6 118.9 %copy-start = (s32[8,2]{0,1:T(2,128)S(1)}, s32[8,2]{0,1:T(2,128)}, u32[]{:S(2)}) copy-start(s32[8,2]{0,1:T(2,128)} %param.13) | copy-start | bytes 196
  1.5 11.3 %copy-start.1 = (f32[1,224,768]{2,1,0:T(8,128)S(1)}, f32[1,224,768]{2,1,0:T(8,128)}, u32[]{:S(2)}) copy-start(f32[1,224,768]{2,1,0:T(8,128)} %param.14) | copy-start | bytes 2064388
  1.5 11.4 %copy-start.2 = (f32[1,224,768]{2,1,0:T(8,128)S(1)}, f32[1,224,768]{2,1,0:T(8,128)}, u32[]{:S(2)}) copy-start(f32[1,224,768]{2,1,0:T(8,128)} %param.15) | copy-start | bytes 2064388
  1.5 11.4 %copy-start.3 = (f32[1,224,768]{2,1,0:T(8,128)S(1)}, f32[1,224,768]{2,1,0:T(8,128)}, u32[]{:S(2)}) copy-start(f32[1,224,768]{2,1,0:T(8,128)} %param.16) | copy-start | bytes 2064388
  13.9 1.8 %copy-start.10 = (f32[4,224,768]{2,1,0:T(8,128)S(1)}, f32[4,224,768]{2,1,0:T(8,128)}, u32[]{:S(2)}) copy-start(f32[4,224,768]{2,1,0:T(8,128)} %get-tuple-element.56) | copy-start | bytes 8257540
  14.1 3.4 %copy-start.8 = (f32[4,224,768]{2,1,0:T(8,128)S(1)}, f32[4,224,768]{2,1,0:T(8,128)}, u32[]{:S(2)}) copy-start(f32[4,224,768]{2,1,0:T(8,128)} %get-tuple-element.57) | copy-start | bytes 8257540
  14.1 6.4 %collective-permute-start.21 = (s32[2,224,768]{2,1,0:T(8,128)S(1)}, s32[2,224,768]{2,1,0:T(8,128)S(1)}, u32[]{:S(2)}, u32[]{:S(2)}) collective-permute-start(s32[2,224,768]{2,1,0:T(8,128)S(1)} %get-tuple-element.105), channel_id=1, source_target_pairs={{0,16},{16,0},{32,48},{48,32},{64,80},{80,64},{96,112},{112,96},{1... | collective-permute-start | bytes 4128776 | tf_op jit(solution)/shard_map/ppermute | solution.py:289
  15.8 19.5 %collective-permute-start = (f16[4,224,768]{2,1,0:T(8,128)(2,1)S(1)}, f16[4,224,768]{2,1,0:T(8,128)(2,1)S(1)}, u32[]{:S(2)}, u32[]{:S(2)}) collective-permute-start(f16[4,224,768]{2,1,0:T(8,128)(2,1)S(1)} %convert_element_type.138), channel_id=1, source_target_pairs={{0,4},{1,5},{2,6},{3,7},{4,8},{5,9},{6,10},{7,11},{8,12},{9,13},{1... | collective-permute-start | bytes 4128776 | tf_op jit(solution)/shard_map/ppermute | solution.py:30
  17.7 18.1 %collective-permute-start.1 = (f16[4,224,768]{2,1,0:T(8,128)(2,1)S(1)}, f16[4,224,768]{2,1,0:T(8,128)(2,1)S(1)}, u32[]{:S(2)}, u32[]{:S(2)}) collective-permute-start(f16[4,224,768]{2,1,0:T(8,128)(2,1)S(1)} %convert_element_type.139), channel_id=1, source_target_pairs={{0,12},{1,13},{2,14},{3,15},{4,0},{5,1},{6,2},{7,3},{8,4},{9,5},{1... | collective-permute-start | bytes 4128776 | tf_op jit(solution)/shard_map/ppermute | solution.py:30
  22.3 39.0 %collective-permute-start.22 = (s32[2,2,224,768]{3,2,1,0:T(8,128)}, s32[2,2,224,768]{3,2,1,0:T(8,128)}, u32[]{:S(2)}, u32[]{:S(2)}) collective-permute-start(s32[2,2,224,768]{3,2,1,0:T(8,128)} %pad_add_fusion.refs_0_), channel_id=1, source_target_pairs={{0,32},{16,112},{32,64},{48,16},{64,96},{80,48},{96,0},{112,80},{1... | collective-permute-start | bytes 8257544 | tf_op jit(solution)/shard_map/ppermute | solution.py:39
  35.8 5.3 %copy-start.9 = (f32[4,224,768]{2,1,0:T(8,128)S(1)}, f32[4,224,768]{2,1,0:T(8,128)}, u32[]{:S(2)}) copy-start(f32[4,224,768]{2,1,0:T(8,128)} %get-tuple-element.68) | copy-start | bytes 8257540
  37.9 3.5 %copy-start.6 = (f32[4,224,768]{2,1,0:T(8,128)S(1)}, f32[4,224,768]{2,1,0:T(8,128)}, u32[]{:S(2)}) copy-start(f32[4,224,768]{2,1,0:T(8,128)} %get-tuple-element.73) | copy-start | bytes 8257540
  37.9 18.4 %collective-permute-start.2 = (f16[4,224,768]{2,1,0:T(8,128)(2,1)S(1)}, f16[4,224,768]{2,1,0:T(8,128)(2,1)S(1)}, u32[]{:S(2)}, u32[]{:S(2)}) collective-permute-start(f16[4,224,768]{2,1,0:T(8,128)(2,1)S(1)} %convert_element_type.140), channel_id=1, source_target_pairs={{0,12},{1,13},{2,14},{3,15},{4,0},{5,1},{6,2},{7,3},{8,4},{9,5},{1... | collective-permute-start | bytes 4128776 | tf_op jit(solution)/shard_map/ppermute | solution.py:30
  41.3 18.5 %copy-start.7 = (f32[4,224,768]{2,1,0:T(8,128)S(1)}, f32[4,224,768]{2,1,0:T(8,128)}, u32[]{:S(2)}) copy-start(f32[4,224,768]{2,1,0:T(8,128)} %get-tuple-element.70) | copy-start | bytes 8257540
  41.3 18.4 %collective-permute-start.3 = (f16[4,224,768]{2,1,0:T(8,128)(2,1)S(1)}, f16[4,224,768]{2,1,0:T(8,128)(2,1)S(1)}, u32[]{:S(2)}, u32[]{:S(2)}) collective-permute-start(f16[4,224,768]{2,1,0:T(8,128)(2,1)S(1)} %convert_element_type.141), channel_id=1, source_target_pairs={{0,4},{1,5},{2,6},{3,7},{4,8},{5,9},{6,10},{7,11},{8,12},{9,13},{1... | collective-permute-start | bytes 4128776 | tf_op jit(solution)/shard_map/ppermute | solution.py:30
  42.9 31.7 %collective-permute-start.5 = (f16[4,224,768]{2,1,0:T(8,128)(2,1)}, f16[4,224,768]{2,1,0:T(8,128)(2,1)}, u32[]{:S(2)}, u32[]{:S(2)}) collective-permute-start(f16[4,224,768]{2,1,0:T(8,128)(2,1)} %add_convert_fusion), channel_id=1, source_target_pairs={{0,4},{1,5},{2,6},{3,7},{4,8},{5,9},{6,10},{7,11},{8,12},{9,13},{1... | collective-permute-start | bytes 4128776 | tf_op jit(solution)/shard_map/ppermute | solution.py:30
  59.8 1.5 copy-start.11
  61.3 18.2 %collective-permute-start.4 = (f16[4,224,768]{2,1,0:T(8,128)(2,1)}, f16[4,224,768]{2,1,0:T(8,128)(2,1)}, u32[]{:S(2)}, u32[]{:S(2)}) collective-permute-start(f16[4,224,768]{2,1,0:T(8,128)(2,1)} %add_convert_fusion.1), channel_id=1, source_target_pairs={{0,12},{1,13},{2,14},{3,15},{4,0},{5,1},{6,2},{7,3},{8,4},{9,5},{1... | collective-permute-start | bytes 4128776 | tf_op jit(solution)/shard_map/ppermute | solution.py:30
  61.3 13.3 %copy-start.4 = (f32[4,224,768]{2,1,0:T(8,128)S(1)}, f32[4,224,768]{2,1,0:T(8,128)}, u32[]{:S(2)}) copy-start(f32[4,224,768]{2,1,0:T(8,128)} %get-tuple-element.72) | copy-start | bytes 8257540
  64.0 38.4 %collective-permute-start.24 = (s32[2,224,768]{2,1,0:T(8,128)}, s32[2,224,768]{2,1,0:T(8,128)}, u32[]{:S(2)}, u32[]{:S(2)}) collective-permute-start(s32[2,224,768]{2,1,0:T(8,128)} %slice_bitcast_fusion), channel_id=1, source_target_pairs={{0,32},{16,112},{32,64},{48,16},{64,96},{80,48},{96,0},{112,80},{1... | collective-permute-start | bytes 4128776 | tf_op jit(solution)/shard_map/ppermute | solution.py:39
  64.5 69.7 %collective-permute-start.23 = (s32[2,2,224,768]{3,2,1,0:T(8,128)}, s32[2,2,224,768]{3,2,1,0:T(8,128)}, u32[]{:S(2)}, u32[]{:S(2)}) collective-permute-start(s32[2,2,224,768]{3,2,1,0:T(8,128)} %collective-permute-done.22.refs_1_), channel_id=1, source_target_pairs={{0,16},{16,0},{32,48},{48,32},{64,80},{80,64},{96,112},{112,96},{1... | collective-permute-start | bytes 8257544 | tf_op jit(solution)/shard_map/ppermute | solution.py:292
  74.6 7.5 %copy-start.12 = (f16[4,224,768]{2,1,0:T(8,128)(2,1)S(1)}, f16[4,224,768]{2,1,0:T(8,128)(2,1)}, u32[]{:S(2)}) copy-start(f16[4,224,768]{2,1,0:T(8,128)(2,1)} %copy-done.11) | copy-start | bytes 4128772
  76.9 5.3 %copy-start.5 = (f32[4,224,768]{2,1,0:T(8,128)S(1)}, f32[4,224,768]{2,1,0:T(8,128)}, u32[]{:S(2)}) copy-start(f32[4,224,768]{2,1,0:T(8,128)} %get-tuple-element.66) | copy-start | bytes 8257540
  78.0 7.3 %collective-permute-start.6 = (f16[224,768]{1,0:T(8,128)(2,1)S(1)}, f16[224,768]{1,0:T(8,128)(2,1)S(1)}, u32[]{:S(2)}, u32[]{:S(2)}) collective-permute-start(f16[224,768]{1,0:T(8,128)(2,1)S(1)} %get-tuple-element.111), channel_id=1, source_target_pairs={{0,1},{1,2},{2,3},{3,0},{4,5},{5,6},{6,7},{7,4},{8,9},{9,10},{10,1... | collective-permute-start | bytes 1032200 | tf_op jit(solution)/shard_map/ppermute | solution.py:30
  79.3 7.4 %collective-permute-start.7 = (f16[224,768]{1,0:T(8,128)(2,1)}, f16[224,768]{1,0:T(8,128)(2,1)}, u32[]{:S(2)}, u32[]{:S(2)}) collective-permute-start(f16[224,768]{1,0:T(8,128)(2,1)} %get-tuple-element.110), channel_id=1, source_target_pairs={{0,3},{1,0},{2,1},{3,2},{4,7},{5,4},{6,5},{7,6},{8,11},{9,8},{10,9... | collective-permute-start | bytes 1032200 | tf_op jit(solution)/shard_map/ppermute | solution.py:30
  79.5 11.6 %collective-permute-start.8 = (f16[224,768]{1,0:T(8,128)(2,1)}, f16[224,768]{1,0:T(8,128)(2,1)}, u32[]{:S(2)}, u32[]{:S(2)}) collective-permute-start(f16[224,768]{1,0:T(8,128)(2,1)} %get-tuple-element.109), channel_id=1, source_target_pairs={{0,2},{1,3},{2,0},{3,1},{4,6},{5,7},{6,4},{7,5},{8,10},{9,11},{10,... | collective-permute-start | bytes 1032200 | tf_op jit(solution)/shard_map/ppermute | solution.py:30
  84.2 8.0 %copy-start.15 = (s32[4]{0:T(128)S(1)}, s32[4]{0:T(128)}, u32[]{:S(2)}) copy-start(s32[4]{0:T(128)} %constant.166.clone) | copy-start | bytes 52
  84.3 8.0 %copy-start.14 = (s32[8,2]{0,1:T(2,128)S(1)}, s32[8,2]{0,1:T(2,128)}, u32[]{:S(2)}) copy-start(s32[8,2]{0,1:T(2,128)} %param.12) | copy-start | bytes 196
  85.3 0.7 copy-start.13
  86.1 6.7 %collective-permute-start.9 = (f16[224,768]{1,0:T(8,128)(2,1)}, f16[224,768]{1,0:T(8,128)(2,1)}, u32[]{:S(2)}, u32[]{:S(2)}) collective-permute-start(f16[224,768]{1,0:T(8,128)(2,1)} %get-tuple-element.106), channel_id=1, source_target_pairs={{0,1},{1,2},{2,3},{3,0},{4,5},{5,6},{6,7},{7,4},{8,9},{9,10},{10,1... | collective-permute-start | bytes 1032200 | tf_op jit(solution)/shard_map/ppermute | solution.py:30
  86.7 8.6 %collective-permute-start.10 = (f16[224,768]{1,0:T(8,128)(2,1)}, f16[224,768]{1,0:T(8,128)(2,1)}, u32[]{:S(2)}, u32[]{:S(2)}) collective-permute-start(f16[224,768]{1,0:T(8,128)(2,1)} %get-tuple-element.108), channel_id=1, source_target_pairs={{0,3},{1,0},{2,1},{3,2},{4,7},{5,4},{6,5},{7,6},{8,11},{9,8},{10,9... | collective-permute-start | bytes 1032200 | tf_op jit(solution)/shard_map/ppermute | solution.py:30
  91.0 10.1 %collective-permute-start.11 = (f16[224,768]{1,0:T(8,128)(2,1)}, f16[224,768]{1,0:T(8,128)(2,1)}, u32[]{:S(2)}, u32[]{:S(2)}) collective-permute-start(f16[224,768]{1,0:T(8,128)(2,1)} %get-tuple-element.107), channel_id=1, source_target_pairs={{0,2},{1,3},{2,0},{3,1},{4,6},{5,7},{6,4},{7,5},{8,10},{9,11},{10,... | collective-permute-start | bytes 1032200 | tf_op jit(solution)/shard_map/ppermute | solution.py:30
  95.0 17.7 %collective-permute-start.14 = (f16[224,768]{1,0:T(8,128)(2,1)}, f16[224,768]{1,0:T(8,128)(2,1)}, u32[]{:S(2)}, u32[]{:S(2)}) collective-permute-start(f16[224,768]{1,0:T(8,128)(2,1)} %multiply_convert_fusion.2), channel_id=1, source_target_pairs={{0,32},{16,48},{32,64},{48,80},{64,96},{80,112},{96,0},{112,16},{1... | collective-permute-start | bytes 1032200 | tf_op jit(solution)/shard_map/ppermute | solution.py:314
  95.3 19.2 %collective-permute-start.15 = (f16[224,768]{1,0:T(8,128)(2,1)}, f16[224,768]{1,0:T(8,128)(2,1)}, u32[]{:S(2)}, u32[]{:S(2)}) collective-permute-start(f16[224,768]{1,0:T(8,128)(2,1)} %multiply_convert_fusion.2), channel_id=1, source_target_pairs={{0,96},{16,112},{32,0},{48,16},{64,32},{80,48},{96,64},{112,80},{1... | collective-permute-start | bytes 1032200 | tf_op jit(solution)/shard_map/ppermute | solution.py:314
  101.2 13.3 %collective-permute-start.16 = (f16[224,768]{1,0:T(8,128)(2,1)}, f16[224,768]{1,0:T(8,128)(2,1)}, u32[]{:S(2)}, u32[]{:S(2)}) collective-permute-start(f16[224,768]{1,0:T(8,128)(2,1)} %multiply_convert_fusion.2), channel_id=1, source_target_pairs={{0,64},{16,80},{32,96},{48,112},{64,0},{80,16},{96,32},{112,48},{1... | collective-permute-start | bytes 1032200 | tf_op jit(solution)/shard_map/ppermute | solution.py:314
  102.3 31.9 %collective-permute-start.25 = (s32[2,224,768]{2,1,0:T(8,128)}, s32[2,224,768]{2,1,0:T(8,128)}, u32[]{:S(2)}, u32[]{:S(2)}) collective-permute-start(s32[2,224,768]{2,1,0:T(8,128)} %collective-permute-done.24.refs_3_), channel_id=1, source_target_pairs={{0,16},{16,0},{32,48},{48,32},{64,80},{80,64},{96,112},{112,96},{1... | collective-permute-start | bytes 4128776 | tf_op jit(solution)/shard_map/ppermute | solution.py:293
  112.7 10.5 %collective-permute-start.26 = (f16[224,768]{1,0:T(8,128)(2,1)}, f16[224,768]{1,0:T(8,128)(2,1)S(1)}, u32[]{:S(2)}, u32[]{:S(2)}) collective-permute-start(f16[224,768]{1,0:T(8,128)(2,1)} %fusion.9), channel_id=1, source_target_pairs={{0,32},{16,48},{32,64},{48,80},{64,96},{80,112},{96,0},{112,16},{1... | collective-permute-start | bytes 1032200 | tf_op jit(solution)/shard_map/ppermute | solution.py:314
  114.5 10.5 %collective-permute-start.17 = (f16[224,768]{1,0:T(8,128)(2,1)}, f16[224,768]{1,0:T(8,128)(2,1)S(1)}, u32[]{:S(2)}, u32[]{:S(2)}) collective-permute-start(f16[224,768]{1,0:T(8,128)(2,1)} %multiply_convert_fusion.2), channel_id=1, source_target_pairs={{0,16},{16,0},{32,48},{48,32},{64,80},{80,64},{96,112},{112,96},{1... | collective-permute-start | bytes 1032200 | tf_op jit(solution)/shard_map/ppermute | solution.py:319
  119.9 9.3 %collective-permute-start.18 = (f16[224,768]{1,0:T(8,128)(2,1)}, f16[224,768]{1,0:T(8,128)(2,1)S(1)}, u32[]{:S(2)}, u32[]{:S(2)}) collective-permute-start(f16[224,768]{1,0:T(8,128)(2,1)} %collective-permute-done.14), channel_id=1, source_target_pairs={{0,16},{16,0},{32,48},{48,32},{64,80},{80,64},{96,112},{112,96},{1... | collective-permute-start | bytes 1032200 | tf_op jit(solution)/shard_map/ppermute | solution.py:319
  123.2 6.6 %collective-permute-start.19 = (f16[224,768]{1,0:T(8,128)(2,1)}, f16[224,768]{1,0:T(8,128)(2,1)S(1)}, u32[]{:S(2)}, u32[]{:S(2)}) collective-permute-start(f16[224,768]{1,0:T(8,128)(2,1)} %collective-permute-done.15), channel_id=1, source_target_pairs={{0,16},{16,0},{32,48},{48,32},{64,80},{80,64},{96,112},{112,96},{1... | collective-permute-start | bytes 1032200 | tf_op jit(solution)/shard_map/ppermute | solution.py:319
  125.0 8.1 %collective-permute-start.20 = (f16[224,768]{1,0:T(8,128)(2,1)}, f16[224,768]{1,0:T(8,128)(2,1)S(1)}, u32[]{:S(2)}, u32[]{:S(2)}) collective-permute-start(f16[224,768]{1,0:T(8,128)(2,1)} %collective-permute-done.16), channel_id=1, source_target_pairs={{0,16},{16,0},{32,48},{48,32},{64,80},{80,64},{96,112},{112,96},{1... | collective-permute-start | bytes 1032200 | tf_op jit(solution)/shard_map/ppermute | solution.py:319
  129.2 10.6 %collective-permute-start.12 = (f16[224,768]{1,0:T(8,128)(2,1)}, f16[224,768]{1,0:T(8,128)(2,1)S(1)}, u32[]{:S(2)}, u32[]{:S(2)}) collective-permute-start(f16[224,768]{1,0:T(8,128)(2,1)} %fusion.9), channel_id=1, source_target_pairs={{0,96},{16,112},{32,0},{48,16},{64,32},{80,48},{96,64},{112,80},{1... | collective-permute-start | bytes 1032200 | tf_op jit(solution)/shard_map/ppermute | solution.py:314
  129.8 18.5 %collective-permute-start.13 = (f16[224,768]{1,0:T(8,128)(2,1)}, f16[224,768]{1,0:T(8,128)(2,1)S(1)}, u32[]{:S(2)}, u32[]{:S(2)}) collective-permute-start(f16[224,768]{1,0:T(8,128)(2,1)} %fusion.9), channel_id=1, source_target_pairs={{0,64},{16,80},{32,96},{48,112},{64,0},{80,16},{96,32},{112,48},{1... | collective-permute-start | bytes 1032200 | tf_op jit(solution)/shard_map/ppermute | solution.py:314
  133.1 18.1 %collective-permute-start.27 = (f16[224,768]{1,0:T(8,128)(2,1)}, f16[224,768]{1,0:T(8,128)(2,1)S(1)}, u32[]{:S(2)}, u32[]{:S(2)}) collective-permute-start(f16[224,768]{1,0:T(8,128)(2,1)} %fusion.9), channel_id=1, source_target_pairs={{0,16},{16,0},{32,48},{48,32},{64,80},{80,64},{96,112},{112,96},{1... | collective-permute-start | bytes 1032200 | tf_op jit(solution)/shard_map/ppermute | solution.py:339
  148.3 3.1 %collective-permute-start.29 = (f16[224,768]{1,0:T(8,128)(2,1)S(1)}, f16[224,768]{1,0:T(8,128)(2,1)S(1)}, u32[]{:S(2)}, u32[]{:S(2)}) collective-permute-start(f16[224,768]{1,0:T(8,128)(2,1)S(1)} %collective-permute-done.12), channel_id=1, source_target_pairs={{0,16},{16,0},{32,48},{48,32},{64,80},{80,64},{96,112},{112,96},{1... | collective-permute-start | bytes 1032200 | tf_op jit(solution)/shard_map/ppermute | solution.py:339
  149.7 1.8 %collective-permute-start.30 = (f16[224,768]{1,0:T(8,128)(2,1)S(1)}, f16[224,768]{1,0:T(8,128)(2,1)S(1)}, u32[]{:S(2)}, u32[]{:S(2)}) collective-permute-start(f16[224,768]{1,0:T(8,128)(2,1)S(1)} %collective-permute-done.13), channel_id=1, source_target_pairs={{0,16},{16,0},{32,48},{48,32},{64,80},{80,64},{96,112},{112,96},{1... | collective-permute-start | bytes 1032200 | tf_op jit(solution)/shard_map/ppermute | solution.py:339
  149.7 2.3 %collective-permute-start.28 = (f16[224,768]{1,0:T(8,128)(2,1)S(1)}, f16[224,768]{1,0:T(8,128)(2,1)S(1)}, u32[]{:S(2)}, u32[]{:S(2)}) collective-permute-start(f16[224,768]{1,0:T(8,128)(2,1)S(1)} %collective-permute-done.26), channel_id=1, source_target_pairs={{0,16},{16,0},{32,48},{48,32},{64,80},{80,64},{96,112},{112,96},{1... | collective-permute-start | bytes 1032200 | tf_op jit(solution)/shard_map/ppermute | solution.py:339

commit v3 on v2

--- a/solution.py
+++ b/solution.py
@@ -47,7 +47,7 @@
     root = jnp.sqrt(jnp.sqrt(jnp.sqrt(jnp.minimum(jnp.abs(m) * (1.0 / 0.75), 1.0))))
     qm = jnp.round(jnp.where(m < 0, -root, root) * 32767.0).astype(jnp.int32)
     qv = jnp.round(jnp.sqrt(jnp.clip(v * 5.0, 0.0, 1.0)) * 65535.0).astype(jnp.int32)
-    return jnp.stack([(w * 2.0**32).astype(jnp.int32), qm * 65536 + qv])
+    return (w * 2.0**32).astype(jnp.int32), qm * 65536 + qv
 
 
 def decode_moments(code):
@@ -60,7 +60,12 @@
 
 
 def partial_kernel(which, here, counts, x, c, *refs):
-    outs, (rows, plain, masked, total, load_sems, cot_sem, sems) = refs[:4], refs[4:]
+    if which == 0:
+        owned, outs, state_out, refs = refs[:3], refs[3:7], refs[7], refs[8:]
+        held, state, held_sems, state_sem = refs[7:]
+    else:
+        outs, refs = refs[:4], refs[4:]
+    rows, plain, masked, total, load_sems, cot_sem, sems = refs[:7]
     step = pl.program_id(0)
     core, y, z = here[0], here[1], here[2]
     first, second = counts[y * NZ + z, 0], counts[y * NZ + z, 1]
@@ -86,39 +91,66 @@
     def _():
         cot_load = pltpu.make_async_copy(c.at[pl.ds(start, WINDOW)], plain, cot_sem)
         cot_load.start()
-        for i in range(NY):
-            for copy in loads(i):
-                copy.start()
+        for copy in loads(0):
+            copy.start()
         cot_load.wait()
         index = lax.broadcasted_iota(jnp.int32, masked.shape, 0)
         value = plain[...].astype(F32) * SCALE
         masked[...] = jnp.where((index >= low) & (index < high), value, 0.0).astype(jnp.bfloat16)
+        for i in range(1, NY):
+            for copy in loads(i):
+                copy.start()
+        if which == 0:
+            for k in range(3):
+                pltpu.make_async_copy(owned[k], held.at[k], held_sems.at[k]).start()
+
+    if which == 0:
+
+        @pl.when(step == 2)
+        def _():
+            for k in range(3):
+                pltpu.make_async_copy(owned[k], held.at[k], held_sems.at[k]).wait()
+
+            @pl.loop(0, shard, step=32)
+            def _(at):
+                part = pl.ds(pl.multiple_of(at, 32), 32)
+                state[0, part], state[1, part] = encode_state(
+                    held[0, part], held[1, part], held[2, part]
+                )
+
+            pltpu.make_async_copy(state, state_out, state_sem).start()
+
+        @pl.when(step == NY - 1)
+        def _():
+            pltpu.make_async_copy(state, state_out, state_sem).wait()
 
     for copy in loads(step):
         copy.wait()
+
+    def wait(slot):
+        pltpu.make_async_copy(total.at[slot], outs[0], sems.at[slot]).wait()
+
+    @pl.when(step >= 2)
+    def _():
+        wait(slot)
+
     product = lax.dot_general(
         rows[step], masked[...], (((0,), (0,)), ((), ())), preferred_element_type=F32
     )
-
-    def wait(slot):
-        for b in range(NZ):
-            pltpu.make_async_copy(total.at[slot, b], outs[0].at[b], sems.at[slot, b]).wait()
-
-    @pl.when(step >= 2)
-    def _():
-        wait(slot)
-
-    block = lax.rem(y + 2 + step, NY)
     for b in range(NZ):
         total[slot, b] = product[b * shard : (b + 1) * shard]
-        far = jnp.where(core == 0, lax.rem(2 + step, NY), lax.rem(b - z + NZ, NZ))
-        place = jnp.where(core == 0, b, block)
-        for d in range(4):
-
-            @pl.when(far == d)
-            def _():
+
+    for d in range(4):
+
+        @pl.when((core == 0) & (lax.rem(2 + step, NY) == d))
+        def _():
+            pltpu.make_async_copy(total.at[slot], outs[d], sems.at[slot]).start()
+
+        @pl.when((core == 1) & (z == d))
+        def _():
+            for b in range(NZ):
                 pltpu.make_async_copy(
-                    total.at[slot, b], outs[d].at[place], sems.at[slot, b]
+                    total.at[slot, b], outs[(b - d) % NZ].at[lax.rem(y + 2 + step, NY)], sems.at[slot]
                 ).start()
 
     @pl.when(step == NY - 1)
@@ -127,43 +159,52 @@
         wait(slot)
 
 
-def partial(which, here, counts, inputs, cot, shard):
+def partial(which, here, counts, inputs, cot, shard, owned=()):
     rows, width_d = inputs.shape
     width_h = cot.shape[1]
     block = width_d // NY
+    piece = pltpu.HBM((4, shard, width_h), F32)
+    out_shape = [piece] * 4
+    scratch = [
+        pltpu.VMEM((NY, WINDOW, block), jnp.bfloat16),
+        pltpu.VMEM((WINDOW, width_h), jnp.bfloat16),
+        pltpu.VMEM((WINDOW, width_h), jnp.bfloat16),
+        pltpu.VMEM((2, NZ, shard, width_h), F32),
+        pltpu.SemaphoreType.DMA((NY, len(CHUNKS))),
+        pltpu.SemaphoreType.DMA,
+        pltpu.SemaphoreType.DMA((2,)),
+    ]
+    if which == 0:
+        out_shape = out_shape + [pltpu.HBM((2, shard, width_h), jnp.int32)]
+        scratch = scratch + [
+            pltpu.VMEM((3, shard, width_h), F32),
+            pltpu.VMEM((2, shard, width_h), jnp.int32),
+            pltpu.SemaphoreType.DMA((3,)),
+            pltpu.SemaphoreType.DMA,
+        ]
+    operands = [pltpu.with_memory_space_constraint(v, pltpu.HBM) for v in (inputs, cot, *owned)]
     return pl.pallas_call(
         functools.partial(partial_kernel, which),
         grid_spec=pltpu.PrefetchScalarGridSpec(
             num_scalar_prefetch=2,
             grid=(NY,),
-            in_specs=[
-                pl.BlockSpec(memory_space=pl.ANY),
-                pl.BlockSpec(memory_space=pl.ANY),
-            ],
-            out_specs=[pl.BlockSpec(memory_space=pltpu.HBM)] * 4,
-            scratch_shapes=[
-                pltpu.VMEM((NY, WINDOW, block), jnp.bfloat16),
-                pltpu.VMEM((WINDOW, width_h), jnp.bfloat16),
-                pltpu.VMEM((WINDOW, width_h), jnp.bfloat16),
-                pltpu.VMEM((2, NZ, shard, width_h), F32),
-                pltpu.SemaphoreType.DMA((NY, len(CHUNKS))),
-                pltpu.SemaphoreType.DMA,
-                pltpu.SemaphoreType.DMA((2, NZ)),
-            ],
+            in_specs=[pl.BlockSpec(memory_space=pl.ANY)] * len(operands),
+            out_specs=[pl.BlockSpec(memory_space=pltpu.HBM)] * len(out_shape),
+            scratch_shapes=scratch,
         ),
-        out_shape=[pltpu.HBM((4, shard, width_h), F32)] * 4,
-        compiler_params=pltpu.CompilerParams(vmem_limit_bytes=20 << 20),
-        cost_estimate=pl.CostEstimate(
-            flops=2 * WINDOW * width_d * width_h * 4, bytes_accessed=rows * width_d * 8, transcendentals=0
-        ),
-    )(here, counts, inputs, cot)
-
-
-def exchange(total, me):
-    def block(d):
-        return lax.dynamic_index_in_dim(total, (me + d) % 4, 0, keepdims=False)
-
-    return [block(0), send(block(1), 1, False), send(block(3), -1, False), send(block(2), 2, False)]
+        out_shape=out_shape,
+        compiler_params=pltpu.CompilerParams(vmem_limit_bytes=28 << 20),
+        cost_estimate=pl.CostEstimate(flops=1 << 33, bytes_accessed=1 << 24, transcendentals=0),
+    )(here, counts, *operands)
+
+
+def exchange(total):
+    groups = []
+    for e in range(2 * NX):
+        for fixed in range(4):
+            members = [fixed * NZ + q if e % 2 == 0 else q * NZ + fixed for q in range(4)]
+            groups.append([e * NY * NZ + j for j in members])
+    return lax.all_to_all(total, ("expert", "dp"), 0, 0, axis_index_groups=groups, tiled=True)
 
 
 def add_up(parts):
@@ -221,10 +262,10 @@
     return w - 0.001 * (corrected + 0.1 * w), first_new, second_new
 
 
-def adam_kernel(grad, w, m, v, held, master_out, hw, hf, hs):
-    master_out[...] = adam_tail(grad[0], w[...], 0.9 * m[...], 0.95 * v[...])[0]
-    for s in range(2):
-        nw, nf, ns = adam_tail(grad[1 + s], held[0, s], held[1, s], held[2, s])
+def adam_kernel(grad_own, grad_0, grad_1, w, m, v, held, master_out, hw, hf, hs):
+    master_out[...] = adam_tail(grad_own[...], w[...], 0.9 * m[...], 0.95 * v[...])[0]
+    for s, grad in enumerate((grad_0, grad_1)):
+        nw, nf, ns = adam_tail(grad[...], held[0, s], held[1, s], held[2, s])
         hw[s] = nw.astype(jnp.bfloat16)
         hf[s] = nf
         hs[s] = ns
@@ -238,7 +279,7 @@
     return pl.pallas_call(
         adam_kernel,
         grid=(rows // step,),
-        in_specs=[pl.BlockSpec((3, step, cols), lambda i: (0, i, 0)), flat, flat, flat]
+        in_specs=[flat] * 6
         + [pl.BlockSpec((3, 2, step, cols), lambda i: (0, 0, i, 0))],
         out_specs=[flat, pair, pair, pair],
         out_shape=[
@@ -248,7 +289,7 @@
             jax.ShapeDtypeStruct((2, rows, cols), F32),
         ],
         compiler_params=pltpu.CompilerParams(vmem_limit_bytes=10 << 20),
-    )(grads, w, m, v, held)
+    )(*grads, w, m, v, held)
 
 
 def body(
@@ -275,69 +316,70 @@
     mine_new = lax.dynamic_index_in_dim(new_slots, expert_index, 0, keepdims=False)
     targets = jnp.concatenate([expert_index[None].astype(jnp.int32), mine_new])
     table = jnp.where(ids[:, None] == targets[None, :], 0.125, 0.0).astype(F32)
+    table = jnp.broadcast_to(table[:, :, None, None], (16, 3, 1, master.shape[2]))
+    table = lax.optimization_barrier(table)
 
     here = jnp.stack([core, y, z])
-    inputs = pltpu.with_memory_space_constraint(inputs, pltpu.HBM)
-    cot = pltpu.with_memory_space_constraint(cot, pltpu.HBM)
-    part0 = partial(0, here, row_counts[0], inputs, cot, shard)
-    far_up = send(part0[2].astype(F16), 1, True)
-    raw_down = send(part0[3].astype(F16), -1, True)
-    w_late, m_late, v_late, part0 = lax.optimization_barrier(
-        (master[0], first_moment[0], second_moment[0], part0)
+    *part0, state = partial(
+        0, here, row_counts[0], inputs, cot, shard, (master[0], first_moment[0], second_moment[0])
     )
-    state = encode_state(w_late, m_late, v_late)
-    pair = jnp.stack([state, lax.ppermute(state, "expert", core_swap())])
+    other_state = lax.ppermute(state, "expert", core_swap())
+    small = [part0[2].astype(F16), part0[3].astype(F16)]
+    small, other_state = lax.optimization_barrier((small, other_state))
+    far_up = send(small[0], 1, True)
+    raw_down = send(small[1], -1, True)
+    pair = jnp.stack([state, other_state])
     beside = send_x(pair)
-    far_state = send_x(beside[0])
-    pairs = [pair, beside, lax.ppermute(beside, "expert", core_swap())]
-    singles = [far_state, lax.ppermute(far_state, "expert", core_swap())]
-    cot, state = lax.optimization_barrier((cot, state))
+
+    cot, part0, pair = lax.optimization_barrier((cot, part0, pair))
     part1 = partial(1, here, row_counts[0], inputs, cot, shard)
     part1, far_up, raw_down = lax.optimization_barrier((part1, far_up, raw_down))
     far_down = send(part1[2].astype(F16), -1, True)
-    raw_up = send(part1[1].astype(F16), 1, True)
-
-    far_down, raw_up = lax.optimization_barrier((far_down, raw_up))
     both_up = send((part0[1] + far_up.astype(F32)).astype(F16), 1, True)
+    far_down, both_up, part1_near = lax.optimization_barrier((far_down, both_up, part1[1]))
+    raw_up = send(part1_near.astype(F16), 1, True)
     both_down = send((part1[3] + far_down.astype(F32)).astype(F16), -1, True)
+    back = 8.0 * 2.0 / SCALE
+
+    def swap(value):
+        return lax.ppermute(value, "expert", core_swap())
+
+    def spread(got):
+        own = (jnp.sum(got.astype(F32), 0) * back).astype(F16)
+        return [own] + [lax.ppermute(own, "expert", x_shift(d)) for d in (1, -1, 2)]
+
+    beside, both_up = lax.optimization_barrier((beside, both_up))
+    far_state = send_x(beside[0])
+    cross_state = swap(beside)
     sum_a = (part0[0] + both_up.astype(F32) + raw_down.astype(F32)) * 0.5
+    got_a = exchange(sum_a.astype(F16))
+    got_a, both_down, raw_up, far_state, cross_state = lax.optimization_barrier(
+        (got_a, both_down, raw_up, far_state, cross_state)
+    )
     sum_b = (part1[0] + raw_up.astype(F32) + both_down.astype(F32)) * 0.5
-    me = jnp.where(core == 0, z, y)
-    parts_a = exchange(sum_a.astype(F16), me)
-    parts_b = exchange(sum_b.astype(F16), me)
-    parts_a, parts_b[1] = lax.optimization_barrier((parts_a, parts_b[1]))
-
-    back = 8.0 * 2.0 / SCALE
-
-    def spread(parts):
-        own = (add_up(parts) * back).astype(F16)
-        return [own] + [lax.ppermute(own, "expert", x_shift(d)) for d in (1, -1, 2)]
-
-    same_a = spread(parts_a)
-    same_b = spread(parts_b)
-    same_a, same_b[0] = lax.optimization_barrier((same_a, same_b[0]))
-    other_a = [lax.ppermute(v, "expert", core_swap()) for v in same_a]
-    other_a, pairs, singles, same_b[1] = lax.optimization_barrier(
-        (other_a, pairs, singles, same_b[1])
-    )
-
-    def weighted(same, other, s):
-        total = 0.0
-        for k, g in enumerate(same + other):
-            total = total + table[2 * k + s][:, None, None] * g.astype(F32)[None]
-        return total
+    got_b = exchange(sum_b.astype(F16))
+    same_a = spread(got_a)
 
     at = (mine_new // 2 - x) % NX
     twist = (mine_new % 2 != core).astype(jnp.int32)
     near = jnp.where((at == 3) == (core == 0), 2 + twist, 5 - twist)
     pick = jnp.where(at == 0, twist, jnp.where(at == 2, 6 + twist, near))
-    held = prepare(pick, pairs, singles)
-    grads_a = weighted(same_a, other_a, 0)
-    same_b[2], same_b[3], held, grads_a = lax.optimization_barrier(
-        (same_b[2], same_b[3], held, grads_a)
-    )
+    held = prepare(pick, [pair, beside, cross_state], [far_state, swap(far_state)])
+    got_b, same_a, held = lax.optimization_barrier((got_b, same_a, held))
+    same_b = spread(got_b)
+    other_a = [swap(v) for v in same_a]
+    other_a, same_b = lax.optimization_barrier((other_a, same_b))
+
+    def weighted(same, other, s, t):
+        total = 0.0
+        for k, g in enumerate(same + other):
+            total = total + table[2 * k + s, t] * g.astype(F32)
+        return total
+
+    grads_a = [weighted(same_a, other_a, 0, t) for t in range(3)]
+    grads_a = lax.optimization_barrier(grads_a)
     other_b = [lax.ppermute(v, "expert", core_swap()) for v in same_b]
-    grads = grads_a + weighted(same_b, other_b, 1)
+    grads = [grads_a[t] + weighted(same_b, other_b, 1, t) for t in range(3)]
     new_master, held_w, held_first, held_second = finish(
         grads, master[0], first_moment[0], second_moment[0], held
     )

time: 160 us -> 149 us (0.931); the launches traced: 157 us -> 148 us
  blocking collectives: 0 us -> 21.2 us
  starting transfers between devices: 46.9 us -> 30.8 us
  other arithmetic: 25.5 us -> 10.1 us
  waiting for transfers between devices: 46 us -> 49.8 us
  Pallas kernels: 29.8 us -> 27.9 us
    all_to_all x0 -> x1, blocking collectives: none -> 21.2 us  [exchange(): lax.all_to_all(total, ('expert', 'dp'), 0, 0, axis_index_groups=groups, t...]
    ppermute x7, starting transfers between devices: 17.8 us -> 6.25 us  [the longest x6 5.41 us: swap(): return lax.ppermute(value, 'expert', core_swap())]
    ppermute x6, waiting for transfers between devices: 13.3 us -> 23.8 us  [spread(): return [own] + [lax.ppermute(own, 'expert', x_shift(d)) for d in (1, -1, 2)]]
    convert_element_type x23 -> x7, other arithmetic: 15 us -> 4.85 us  [the longest x2 2.13 us: body(): small = [part0[2].astype(F16), part0[3].astype(F16)]]
    ppermute x12 -> x6, waiting for transfers between devices: 32.3 us -> 23.8 us  [send(): return lax.ppermute(value, ('expert', 'dp'), plane_shift(d, first))]
    all_to_all x0 -> x1, starting transfers between devices: none -> 5.37 us  [exchange(): lax.all_to_all(total, ('expert', 'dp'), 0, 0, axis_index_groups=groups, t...]
    ppermute x12 -> x6, starting transfers between devices: 16.8 us -> 11.7 us  [send(): return lax.ppermute(value, ('expert', 'dp'), plane_shift(d, first))]
    unnamed x32 -> x38, local copies, waits for them, and re-layouts: 1.53 us -> 5.33 us
  transfers between devices with their start and end apart: 31 -> 26, of which waited for: 12 -> 11; matrix products, arithmetic and copies ran while one was open for 18% -> 6% of each run, Pallas kernels for 9% -> 9%
where the time goes in v3:
time: 149 us; the launch traced here: 148 us
  waiting for transfers between devices  49.8 us (33%)
  starting transfers between devices  30.8 us (21%)
  Pallas kernels  27.9 us (19%)
  blocking collectives  21.2 us (14%)
  other arithmetic  10.1 us (7%)
  local copies, waits for them, and re-layouts  7.68 us (5%)
    ppermute x6, waiting for transfers between devices, spread(): return [own] + [lax.ppermute(own, 'expert', x_shift(d)) for d in (1, -1, 2)]  23.8 us
    ppermute x6, waiting for transfers between devices, send(): return lax.ppermute(value, ('expert', 'dp'), plane_shift(d, first))  23.8 us
    all_to_all x1, blocking collectives, exchange(): lax.all_to_all(total, ('expert', 'dp'), 0, 0, axis_index_groups=groups, t...  21.2 us
    pallas_call x2, Pallas kernels, partial(): pl.pallas_call(functools.partial(partial_kernel, which), grid_spec=pltpu....  20.8 us
    ppermute x6, starting transfers between devices, send(): return lax.ppermute(value, ('expert', 'dp'), plane_shift(d, first))  11.7 us
    ppermute x6, starting transfers between devices, swap(): return lax.ppermute(value, 'expert', core_swap())  5.41 us
    all_to_all x1, starting transfers between devices, exchange(): lax.all_to_all(total, ('expert', 'dp'), 0, 0, axis_index_groups=groups, t...  5.37 us
    unnamed x38, local copies, waits for them, and re-layouts  5.33 us
  transfers between devices with their start and end apart: 26, of which 11 were waited for; matrix products, arithmetic and copies ran while one was open for 6% of the time, Pallas kernels for 9%

profile of v3, /device:TPU:15, one launch (start us, length us, event | category | flops | bytes accessed | tf_op | source)
XLA Modules:
  0.0 148.4 jit_solution(4492832035596965325)
XLA Ops:
  0.7 0.8 copy.21
  1.5 10.7 %shard_map.120 = (f32[4,224,768]{2,1,0:T(8,128)}, f32[4,224,768]{2,1,0:T(8,128)}, f32[4,224,768]{2,1,0:T(8,128)}, f32[4,224,768]{2,1,0:T(8,128)}, s32[2,224,768]{2,1,0:T(8,128)}) custom-call(s32[3]{0:T(128)S(1)} %pad_add_fusion.2.here, s32[16,3]{1,0:T(8,128)S(1)} %bitcast.24, bf16[1280,3584]{1,0:T(8,128)(2,1)} %bitcast.29, bf16[1280,768]{1,0:T(8,128)(2,1)} %bitcast.31, ...), custom_call_target="tpu_custom_call" | custom-call | flops 8589934592 | bytes 16777216 | tf_op jit(solution)/shard_map/pallas_call | solution.py:186
  12.2 0.8 collective-permute-start
  13.0 1.9 %convert_element_type.137 = f16[4,224,768]{2,1,0:T(8,128)(2,1)S(1)} convert(f32[4,224,768]{2,1,0:T(8,128)} %get-tuple-element.59) | non-fusion elementwise | flops 688128 | bytes 4128768 | tf_op jit(solution)/shard_map/convert_element_type | solution.py:327
  15.2 0.8 collective-permute-done
  16.0 1.6 %collective-permute-start.1 = (f16[4,224,768]{2,1,0:T(8,128)(2,1)S(1)}, f16[4,224,768]{2,1,0:T(8,128)(2,1)S(1)}, u32[]{:S(2)}, u32[]{:S(2)}) collective-permute-start(f16[4,224,768]{2,1,0:T(8,128)(2,1)S(1)} %convert_element_type.137), channel_id=1, source_target_pairs={{0,4},{1,5},{2,6},{3,7},{4,8},{5,9},{6,10},{7,11},{8,12},{9,13},{1... | collective-permute-start | bytes 4128776 | tf_op jit(solution)/shard_map/ppermute | solution.py:30
  17.6 2.1 %collective-permute-start.2 = (f16[4,224,768]{2,1,0:T(8,128)(2,1)S(1)}, f16[4,224,768]{2,1,0:T(8,128)(2,1)S(1)}, u32[]{:S(2)}, u32[]{:S(2)}) collective-permute-start(f16[4,224,768]{2,1,0:T(8,128)(2,1)S(1)} %convert_element_type.138), channel_id=1, source_target_pairs={{0,12},{1,13},{2,14},{3,15},{4,0},{5,1},{6,2},{7,3},{8,4},{9,5},{1... | collective-permute-start | bytes 4128776 | tf_op jit(solution)/shard_map/ppermute | solution.py:30
  20.0 0.6 collective-permute-start.3
  20.6 10.2 %shard_map.121 = (f32[4,224,768]{2,1,0:T(8,128)}, f32[4,224,768]{2,1,0:T(8,128)}, f32[4,224,768]{2,1,0:T(8,128)}, f32[4,224,768]{2,1,0:T(8,128)}) custom-call(s32[3]{0:T(128)S(1)} %pad_add_fusion.2.here, s32[16,3]{1,0:T(8,128)S(1)} %bitcast.25, bf16[1280,3584]{1,0:T(8,128)(2,1)} %bitcast.30, bf16[1280,768]{1,0:T(8,128)(2,1)} %bitcast.32), custom_call_target="tpu_custom_call" | custom-call | flops 8589934592 | bytes 16777216 | tf_op jit(solution)/shard_map/pallas_call | solution.py:186
  30.8 4.7 %collective-permute-done.1 = f16[4,224,768]{2,1,0:T(8,128)(2,1)S(1)} collective-permute-done((f16[4,224,768]{2,1,0:T(8,128)(2,1)S(1)}, f16[4,224,768]{2,1,0:T(8,128)(2,1)S(1)}, u32[]{:S(2)}, u32[]{:S(2)}) %collective-permute-start.1) | collective-permute-done | bytes 1376288 | tf_op jit(solution)/shard_map/ppermute | solution.py:30
  35.5 0.4 add_convert_fusion.1
  35.8 1.3 collective-permute-start.5
  37.4 2.7 %collective-permute-start.4 = (f16[4,224,768]{2,1,0:T(8,128)(2,1)S(1)}, f16[4,224,768]{2,1,0:T(8,128)(2,1)S(1)}, u32[]{:S(2)}, u32[]{:S(2)}) collective-permute-start(f16[4,224,768]{2,1,0:T(8,128)(2,1)S(1)} %convert_element_type.139), channel_id=1, source_target_pairs={{0,12},{1,13},{2,14},{3,15},{4,0},{5,1},{6,2},{7,3},{8,4},{9,5},{1... | collective-permute-start | bytes 4128776 | tf_op jit(solution)/shard_map/ppermute | solution.py:30
  40.2 14.1 %collective-permute-done.5 = f16[4,224,768]{2,1,0:T(8,128)(2,1)S(1)} collective-permute-done((f16[4,224,768]{2,1,0:T(8,128)(2,1)S(1)}, f16[4,224,768]{2,1,0:T(8,128)(2,1)S(1)}, u32[]{:S(2)}, u32[]{:S(2)}) %collective-permute-start.5) | collective-permute-done | bytes 1376288 | tf_op jit(solution)/shard_map/ppermute | solution.py:30
  54.3 1.1 collective-permute-done.4
  55.4 1.2 collective-permute-start.9
  56.6 0.5 add_convert_fusion
  57.1 3.8 %collective-permute-start.6 = (f16[4,224,768]{2,1,0:T(8,128)(2,1)S(1)}, f16[4,224,768]{2,1,0:T(8,128)(2,1)S(1)}, u32[]{:S(2)}, u32[]{:S(2)}) collective-permute-start(f16[4,224,768]{2,1,0:T(8,128)(2,1)S(1)} %add_convert_fusion), channel_id=1, source_target_pairs={{0,12},{1,13},{2,14},{3,15},{4,0},{5,1},{6,2},{7,3},{8,4},{9,5},{1... | collective-permute-start | bytes 4128776 | tf_op jit(solution)/shard_map/ppermute | solution.py:30
  61.0 0.6 collective-permute-start.8
  61.9 0.6 multiply_convert_fusion.1
  62.6 21.2 %all_to_all.10 = f16[4,224,768]{2,1,0:T(8,128)(2,1)S(1)} all-to-all(f16[4,224,768]{2,1,0:T(8,128)(2,1)S(1)} %multiply_convert_fusion.1), channel_id=1, replica_groups={{0,1,2,3},{4,5,6,7},{8,9,10,11},{12,13,14,15},{16,20,24,28},{17,21,25,2..., dimensions={0} | all-to-all | bytes 2752512 | tf_op jit(solution)/shard_map/all_to_all | solution.py:207
  83.8 3.9 %collective-permute-done.7 = f16[4,224,768]{2,1,0:T(8,128)(2,1)S(1)} collective-permute-done((f16[4,224,768]{2,1,0:T(8,128)(2,1)S(1)}, f16[4,224,768]{2,1,0:T(8,128)(2,1)S(1)}, u32[]{:S(2)}, u32[]{:S(2)}) %collective-permute-start.7) | collective-permute-done | bytes 1376288 | tf_op jit(solution)/shard_map/ppermute | solution.py:30
  87.6 1.6 %copy-done.8 = s32[2,2,224,768]{3,2,1,0:T(8,128)} copy-done((s32[2,2,224,768]{3,2,1,0:T(8,128)}, s32[2,2,224,768]{3,2,1,0:T(8,128)S(1)}, u32[]{:S(2)}) %copy-start.8) | copy-done | bytes 2752536
  89.2 1.8 %multiply_convert_fusion = f16[4,224,768]{2,1,0:T(8,128)(2,1)} fusion(f16[4,224,768]{2,1,0:T(8,128)(2,1)S(1)} %collective-permute-done.6, f32[4,224,768]{2,1,0:T(8,128)S(1)} %copy-done.10, f16[4,224,768]{2,1,0:T(8,128)(2,1)S(1)} %collective-permute-done.7), kind=kLoop, calls=%fused_computation.4 | loop fusion | flops 4128768 | bytes 6881280 | tf_op jit(solution)/shard_map/convert_element_type | solution.py:360
  91.0 5.4 %all-to-all-start.1 = ((f16[4,224,768]{2,1,0:T(8,128)(2,1)}), f16[4,224,768]{2,1,0:T(8,128)(2,1)S(1)}, u32[]{:S(2)}, u32[]{:S(2)}) async-start(f16[4,224,768]{2,1,0:T(8,128)(2,1)} %multiply_convert_fusion), calls=%async_computation.1 | async-start | bytes 2752512 | tf_op jit(solution)/shard_map/all_to_all | solution.py:207
  96.6 2.2 %collective-permute-start.10 = (f16[224,768]{1,0:T(8,128)(2,1)S(1)}, f16[224,768]{1,0:T(8,128)(2,1)S(1)}, u32[]{:S(2)}, u32[]{:S(2)}) collective-permute-start(f16[224,768]{1,0:T(8,128)(2,1)S(1)} %multiply_convert_fusion.3), channel_id=1, source_target_pairs={{0,32},{16,48},{32,64},{48,80},{64,96},{80,112},{96,0},{112,16},{1... | collective-permute-start | bytes 1032200 | tf_op jit(solution)/shard_map/ppermute | solution.py:349
  98.8 1.3 collective-permute-start.12
  100.3 0.6 gather_fusion
  101.1 2.9 %shard_map.122.held = f32[3,2,224,768]{3,2,1,0:T(8,128)S(1)} custom-call(s32[2]{0:T(128)S(1)} %compare_select_fusion.8.pick, s32[2,2,224,768]{3,2,1,0:T(8,128)} %copy-done.6, s32[2,2,224,768]{3,2,1,0:T(8,128)} %copy-done.7, s32[2,2,224,768]{3,2,1,0:T(8,128)} %copy-done.8, s32[2,224,768]{2,1,0:T(8,128)} %collective-permute-done.8.refs_3_, ...), custom_call_target="tpu_custom_call" | custom-call | tf_op jit(solution)/shard_map/pallas_call | solution.py:240
  104.0 1.9 %copy-done.1 = f32[3,2,224,768]{3,2,1,0:T(8,128)} copy-done((f32[3,2,224,768]{3,2,1,0:T(8,128)}, f32[3,2,224,768]{3,2,1,0:T(8,128)S(1)}, u32[]{:S(2)}) %copy-start.1) | copy-done | bytes 4128792
  105.9 7.5 %collective-permute-done.10 = f16[224,768]{1,0:T(8,128)(2,1)S(1)} collective-permute-done((f16[224,768]{1,0:T(8,128)(2,1)S(1)}, f16[224,768]{1,0:T(8,128)(2,1)S(1)}, u32[]{:S(2)}, u32[]{:S(2)}) %collective-permute-start.10) | collective-permute-done | bytes 344096 | tf_op jit(solution)/shard_map/ppermute | solution.py:349
  113.4 3.4 %collective-permute-done.11 = f16[224,768]{1,0:T(8,128)(2,1)S(1)} collective-permute-done((f16[224,768]{1,0:T(8,128)(2,1)S(1)}, f16[224,768]{1,0:T(8,128)(2,1)S(1)}, u32[]{:S(2)}, u32[]{:S(2)}) %collective-permute-start.11) | collective-permute-done | bytes 344096 | tf_op jit(solution)/shard_map/ppermute | solution.py:349
  117.2 1.5 collective-permute-start.19
  119.1 1.0 collective-permute-start.14
  120.2 6.3 %collective-permute-done.18 = f16[224,768]{1,0:T(8,128)(2,1)S(1)} collective-permute-done((f16[224,768]{1,0:T(8,128)(2,1)S(1)}, f16[224,768]{1,0:T(8,128)(2,1)S(1)}, u32[]{:S(2)}, u32[]{:S(2)}) %collective-permute-start.18) | collective-permute-done | bytes 344096 | tf_op jit(solution)/shard_map/ppermute | solution.py:349
  126.4 2.0 %collective-permute-start.16 = (f16[224,768]{1,0:T(8,128)(2,1)S(1)}, f16[224,768]{1,0:T(8,128)(2,1)S(1)}, u32[]{:S(2)}, u32[]{:S(2)}) collective-permute-start(f16[224,768]{1,0:T(8,128)(2,1)S(1)} %collective-permute-done.11), channel_id=1, source_target_pairs={{0,16},{16,0},{32,48},{48,32},{64,80},{80,64},{96,112},{112,96},{1... | collective-permute-start | bytes 1032200 | tf_op jit(solution)/shard_map/ppermute | solution.py:345
  128.4 6.7 %collective-permute-done.19 = f16[224,768]{1,0:T(8,128)(2,1)S(1)} collective-permute-done((f16[224,768]{1,0:T(8,128)(2,1)S(1)}, f16[224,768]{1,0:T(8,128)(2,1)S(1)}, u32[]{:S(2)}, u32[]{:S(2)}) %collective-permute-start.19) | collective-permute-done | bytes 344096 | tf_op jit(solution)/shard_map/ppermute | solution.py:349
  135.1 1.2 collective-permute-start.17
  136.7 0.8 collective-permute-done.17
  138.6 0.5 fusion.20
  139.1 0.5 fusion.13
  139.6 0.5 fusion.6
  140.2 0.5 collective-permute-done.24
  140.7 0.6 fusion.44.grad_1
  141.3 0.6 fusion.36.grad_0
  141.9 0.6 fusion.28.grad_own
  142.8 1.4 copy-done.2
  144.2 4.2 %shard_map.123 = (f32[224,768]{1,0:T(8,128)}, bf16[2,224,768]{2,1,0:T(8,128)(2,1)}, f32[2,224,768]{2,1,0:T(8,128)}, f32[2,224,768]{2,1,0:T(8,128)}) custom-call(f32[224,768]{1,0:T(8,128)S(1)} %fusion.28.grad_own, f32[224,768]{1,0:T(8,128)S(1)} %fusion.36.grad_0, f32[224,768]{1,0:T(8,128)S(1)} %fusion.44.grad_1, f32[224,768]{1,0:T(8,128)S(1)} %bitcast.19, ...), custom_call_target="tpu_custom_call" | custom-call | tf_op jit(solution)/shard_map/pallas_call | solution.py:279
  (85 shorter events, 4.4 us)
Async XLA Ops:
  0.6 100.3 %copy-start = (s32[8,2]{0,1:T(2,128)S(1)}, s32[8,2]{0,1:T(2,128)}, u32[]{:S(2)}) copy-start(s32[8,2]{0,1:T(2,128)} %param.13) | copy-start | bytes 196
  12.2 2.8 %copy-start.15 = (f32[4,224,768]{2,1,0:T(8,128)S(1)}, f32[4,224,768]{2,1,0:T(8,128)}, u32[]{:S(2)}) copy-start(f32[4,224,768]{2,1,0:T(8,128)} %get-tuple-element.60) | copy-start | bytes 8257540
  12.2 3.8 %collective-permute-start = (s32[2,224,768]{2,1,0:T(8,128)}, s32[2,224,768]{2,1,0:T(8,128)S(1)}, u32[]{:S(2)}, u32[]{:S(2)}) collective-permute-start(s32[2,224,768]{2,1,0:T(8,128)} %get-tuple-element.61), channel_id=1, source_target_pairs={{0,16},{16,0},{32,48},{48,32},{64,80},{80,64},{96,112},{112,96},{1... | collective-permute-start | bytes 4128776 | tf_op jit(solution)/shard_map/ppermute | solution.py:326
  15.0 4.8 %copy-start.16 = (s32[2,224,768]{2,1,0:T(8,128)S(1)}, s32[2,224,768]{2,1,0:T(8,128)}, u32[]{:S(2)}) copy-start(s32[2,224,768]{2,1,0:T(8,128)} %get-tuple-element.61) | copy-start | bytes 4128772
  16.0 19.5 %collective-permute-start.1 = (f16[4,224,768]{2,1,0:T(8,128)(2,1)S(1)}, f16[4,224,768]{2,1,0:T(8,128)(2,1)S(1)}, u32[]{:S(2)}, u32[]{:S(2)}) collective-permute-start(f16[4,224,768]{2,1,0:T(8,128)(2,1)S(1)} %convert_element_type.137), channel_id=1, source_target_pairs={{0,4},{1,5},{2,6},{3,7},{4,8},{5,9},{6,10},{7,11},{8,12},{9,13},{1... | collective-permute-start | bytes 4128776 | tf_op jit(solution)/shard_map/ppermute | solution.py:30
  17.6 17.8 %collective-permute-start.2 = (f16[4,224,768]{2,1,0:T(8,128)(2,1)S(1)}, f16[4,224,768]{2,1,0:T(8,128)(2,1)S(1)}, u32[]{:S(2)}, u32[]{:S(2)}) collective-permute-start(f16[4,224,768]{2,1,0:T(8,128)(2,1)S(1)} %convert_element_type.138), channel_id=1, source_target_pairs={{0,12},{1,13},{2,14},{3,15},{4,0},{5,1},{6,2},{7,3},{8,4},{9,5},{1... | collective-permute-start | bytes 4128776 | tf_op jit(solution)/shard_map/ppermute | solution.py:30
  20.0 10.8 %copy-start.6 = (s32[2,2,224,768]{3,2,1,0:T(8,128)}, s32[2,2,224,768]{3,2,1,0:T(8,128)S(1)}, u32[]{:S(2)}) copy-start(s32[2,2,224,768]{3,2,1,0:T(8,128)S(1)} %pad_add_fusion.refs_0_) | copy-start | bytes 8257540
  20.0 35.4 %collective-permute-start.3 = (s32[2,2,224,768]{3,2,1,0:T(8,128)S(1)}, s32[2,2,224,768]{3,2,1,0:T(8,128)S(1)}, u32[]{:S(2)}, u32[]{:S(2)}) collective-permute-start(s32[2,2,224,768]{3,2,1,0:T(8,128)S(1)} %pad_add_fusion.refs_0_), channel_id=1, source_target_pairs={{0,32},{16,112},{32,64},{48,16},{64,96},{80,48},{96,0},{112,80},{1... | collective-permute-start | bytes 8257544 | tf_op jit(solution)/shard_map/ppermute | solution.py:39
  20.6 14.8 %copy-start.11 = (f32[4,224,768]{2,1,0:T(8,128)S(1)}, f32[4,224,768]{2,1,0:T(8,128)}, u32[]{:S(2)}) copy-start(f32[4,224,768]{2,1,0:T(8,128)} %get-tuple-element.73) | copy-start | bytes 8257540
  35.5 1.8 %copy-start.14 = (f32[4,224,768]{2,1,0:T(8,128)S(1)}, f32[4,224,768]{2,1,0:T(8,128)}, u32[]{:S(2)}) copy-start(f32[4,224,768]{2,1,0:T(8,128)} %get-tuple-element.72) | copy-start | bytes 8257540
  35.8 20.8 %copy-start.12 = (f32[4,224,768]{2,1,0:T(8,128)S(1)}, f32[4,224,768]{2,1,0:T(8,128)}, u32[]{:S(2)}) copy-start(f32[4,224,768]{2,1,0:T(8,128)} %get-tuple-element.79) | copy-start | bytes 8257540
  35.8 18.4 %collective-permute-start.5 = (f16[4,224,768]{2,1,0:T(8,128)(2,1)S(1)}, f16[4,224,768]{2,1,0:T(8,128)(2,1)S(1)}, u32[]{:S(2)}, u32[]{:S(2)}) collective-permute-start(f16[4,224,768]{2,1,0:T(8,128)(2,1)S(1)} %add_convert_fusion.1), channel_id=1, source_target_pairs={{0,4},{1,5},{2,6},{3,7},{4,8},{5,9},{6,10},{7,11},{8,12},{9,13},{1... | collective-permute-start | bytes 4128776 | tf_op jit(solution)/shard_map/ppermute | solution.py:30
  37.4 18.0 %collective-permute-start.4 = (f16[4,224,768]{2,1,0:T(8,128)(2,1)S(1)}, f16[4,224,768]{2,1,0:T(8,128)(2,1)S(1)}, u32[]{:S(2)}, u32[]{:S(2)}) collective-permute-start(f16[4,224,768]{2,1,0:T(8,128)(2,1)S(1)} %convert_element_type.139), channel_id=1, source_target_pairs={{0,12},{1,13},{2,14},{3,15},{4,0},{5,1},{6,2},{7,3},{8,4},{9,5},{1... | collective-permute-start | bytes 4128776 | tf_op jit(solution)/shard_map/ppermute | solution.py:30
  55.4 5.5 %copy-start.7 = (s32[2,2,224,768]{3,2,1,0:T(8,128)}, s32[2,2,224,768]{3,2,1,0:T(8,128)S(1)}, u32[]{:S(2)}) copy-start(s32[2,2,224,768]{3,2,1,0:T(8,128)S(1)} %collective-permute-done.3.refs_1_) | copy-start | bytes 8257540
  55.4 32.2 %collective-permute-start.9 = (s32[2,2,224,768]{3,2,1,0:T(8,128)S(1)}, s32[2,2,224,768]{3,2,1,0:T(8,128)S(1)}, u32[]{:S(2)}, u32[]{:S(2)}) collective-permute-start(s32[2,2,224,768]{3,2,1,0:T(8,128)S(1)} %collective-permute-done.3.refs_1_), channel_id=1, source_target_pairs={{0,16},{16,0},{32,48},{48,32},{64,80},{80,64},{96,112},{112,96},{1... | collective-permute-start | bytes 8257544 | tf_op jit(solution)/shard_map/ppermute | solution.py:345
  56.6 5.0 %copy-start.13 = (f32[4,224,768]{2,1,0:T(8,128)S(1)}, f32[4,224,768]{2,1,0:T(8,128)}, u32[]{:S(2)}) copy-start(f32[4,224,768]{2,1,0:T(8,128)} %get-tuple-element.81) | copy-start | bytes 8257540
  57.1 4.8 %copy-start.9 = (f32[4,224,768]{2,1,0:T(8,128)S(1)}, f32[4,224,768]{2,1,0:T(8,128)}, u32[]{:S(2)}) copy-start(f32[4,224,768]{2,1,0:T(8,128)} %get-tuple-element.71) | copy-start | bytes 8257540
  57.1 26.7 %collective-permute-start.6 = (f16[4,224,768]{2,1,0:T(8,128)(2,1)S(1)}, f16[4,224,768]{2,1,0:T(8,128)(2,1)S(1)}, u32[]{:S(2)}, u32[]{:S(2)}) collective-permute-start(f16[4,224,768]{2,1,0:T(8,128)(2,1)S(1)} %add_convert_fusion), channel_id=1, source_target_pairs={{0,12},{1,13},{2,14},{3,15},{4,0},{5,1},{6,2},{7,3},{8,4},{9,5},{1... | collective-permute-start | bytes 4128776 | tf_op jit(solution)/shard_map/ppermute | solution.py:30
  61.0 22.8 %collective-permute-start.8 = (s32[2,224,768]{2,1,0:T(8,128)S(1)}, s32[2,224,768]{2,1,0:T(8,128)}, u32[]{:S(2)}, u32[]{:S(2)}) collective-permute-start(s32[2,224,768]{2,1,0:T(8,128)S(1)} %slice_bitcast_fusion), channel_id=1, source_target_pairs={{0,32},{16,112},{32,64},{48,16},{64,96},{80,48},{96,0},{112,80},{1... | collective-permute-start | bytes 4128776 | tf_op jit(solution)/shard_map/ppermute | solution.py:39
  61.8 25.8 %collective-permute-start.7 = (f16[4,224,768]{2,1,0:T(8,128)(2,1)S(1)}, f16[4,224,768]{2,1,0:T(8,128)(2,1)S(1)}, u32[]{:S(2)}, u32[]{:S(2)}) collective-permute-start(f16[4,224,768]{2,1,0:T(8,128)(2,1)S(1)} %convert_element_type.147), channel_id=1, source_target_pairs={{0,4},{1,5},{2,6},{3,7},{4,8},{5,9},{6,10},{7,11},{8,12},{9,13},{1... | collective-permute-start | bytes 4128776 | tf_op jit(solution)/shard_map/ppermute | solution.py:30
  62.5 26.7 %copy-start.10 = (f32[4,224,768]{2,1,0:T(8,128)S(1)}, f32[4,224,768]{2,1,0:T(8,128)}, u32[]{:S(2)}) copy-start(f32[4,224,768]{2,1,0:T(8,128)} %get-tuple-element.70) | copy-start | bytes 8257540
  87.6 1.6 %copy-start.8 = (s32[2,2,224,768]{3,2,1,0:T(8,128)}, s32[2,2,224,768]{3,2,1,0:T(8,128)S(1)}, u32[]{:S(2)}) copy-start(s32[2,2,224,768]{3,2,1,0:T(8,128)S(1)} %collective-permute-done.9.refs_2_) | copy-start | bytes 8257540
  89.2 11.9 %collective-permute-start.13 = (s32[2,224,768]{2,1,0:T(8,128)}, s32[2,224,768]{2,1,0:T(8,128)}, u32[]{:S(2)}, u32[]{:S(2)}) collective-permute-start(s32[2,224,768]{2,1,0:T(8,128)} %collective-permute-done.8.refs_3_), channel_id=1, source_target_pairs={{0,16},{16,0},{32,48},{48,32},{64,80},{80,64},{96,112},{112,96},{1... | collective-permute-start | bytes 4128776 | tf_op jit(solution)/shard_map/ppermute | solution.py:345
  91.0 9.2 %copy-start.18 = (s32[4]{0:T(128)S(1)}, s32[4]{0:T(128)}, u32[]{:S(2)}) copy-start(s32[4]{0:T(128)} %constant.106.clone) | copy-start | bytes 52
  91.0 9.2 %copy-start.17 = (s32[8,2]{0,1:T(2,128)S(1)}, s32[8,2]{0,1:T(2,128)}, u32[]{:S(2)}) copy-start(s32[8,2]{0,1:T(2,128)} %param.12) | copy-start | bytes 196
  91.0 25.8 %all-to-all-start.1 = ((f16[4,224,768]{2,1,0:T(8,128)(2,1)}), f16[4,224,768]{2,1,0:T(8,128)(2,1)S(1)}, u32[]{:S(2)}, u32[]{:S(2)}) async-start(f16[4,224,768]{2,1,0:T(8,128)(2,1)} %multiply_convert_fusion), calls=%async_computation.1 | async-start | bytes 2752512 | tf_op jit(solution)/shard_map/all_to_all | solution.py:207
  96.6 16.8 %collective-permute-start.10 = (f16[224,768]{1,0:T(8,128)(2,1)S(1)}, f16[224,768]{1,0:T(8,128)(2,1)S(1)}, u32[]{:S(2)}, u32[]{:S(2)}) collective-permute-start(f16[224,768]{1,0:T(8,128)(2,1)S(1)} %multiply_convert_fusion.3), channel_id=1, source_target_pairs={{0,32},{16,48},{32,64},{48,80},{64,96},{80,112},{96,0},{112,16},{1... | collective-permute-start | bytes 1032200 | tf_op jit(solution)/shard_map/ppermute | solution.py:349
  98.8 18.0 %collective-permute-start.11 = (f16[224,768]{1,0:T(8,128)(2,1)S(1)}, f16[224,768]{1,0:T(8,128)(2,1)S(1)}, u32[]{:S(2)}, u32[]{:S(2)}) collective-permute-start(f16[224,768]{1,0:T(8,128)(2,1)S(1)} %multiply_convert_fusion.3), channel_id=1, source_target_pairs={{0,96},{16,112},{32,0},{48,16},{64,32},{80,48},{96,64},{112,80},{1... | collective-permute-start | bytes 1032200 | tf_op jit(solution)/shard_map/ppermute | solution.py:349
  98.8 18.0 %collective-permute-start.12 = (f16[224,768]{1,0:T(8,128)(2,1)S(1)}, f16[224,768]{1,0:T(8,128)(2,1)S(1)}, u32[]{:S(2)}, u32[]{:S(2)}) collective-permute-start(f16[224,768]{1,0:T(8,128)(2,1)S(1)} %multiply_convert_fusion.3), channel_id=1, source_target_pairs={{0,64},{16,80},{32,96},{48,112},{64,0},{80,16},{96,32},{112,48},{1... | collective-permute-start | bytes 1032200 | tf_op jit(solution)/shard_map/ppermute | solution.py:349
  104.0 1.9 %copy-start.1 = (f32[3,2,224,768]{3,2,1,0:T(8,128)}, f32[3,2,224,768]{3,2,1,0:T(8,128)S(1)}, u32[]{:S(2)}) copy-start(f32[3,2,224,768]{3,2,1,0:T(8,128)S(1)} %shard_map.122.held) | copy-start | bytes 12386308
  117.1 9.4 %collective-permute-start.18 = (f16[224,768]{1,0:T(8,128)(2,1)S(1)}, f16[224,768]{1,0:T(8,128)(2,1)S(1)}, u32[]{:S(2)}, u32[]{:S(2)}) collective-permute-start(f16[224,768]{1,0:T(8,128)(2,1)S(1)} %multiply_convert_fusion.2), channel_id=1, source_target_pairs={{0,32},{16,48},{32,64},{48,80},{64,96},{80,112},{96,0},{112,16},{1... | collective-permute-start | bytes 1032200 | tf_op jit(solution)/shard_map/ppermute | solution.py:349
  117.2 17.9 %collective-permute-start.19 = (f16[224,768]{1,0:T(8,128)(2,1)S(1)}, f16[224,768]{1,0:T(8,128)(2,1)S(1)}, u32[]{:S(2)}, u32[]{:S(2)}) collective-permute-start(f16[224,768]{1,0:T(8,128)(2,1)S(1)} %multiply_convert_fusion.2), channel_id=1, source_target_pairs={{0,96},{16,112},{32,0},{48,16},{64,32},{80,48},{96,64},{112,80},{1... | collective-permute-start | bytes 1032200 | tf_op jit(solution)/shard_map/ppermute | solution.py:349
  119.0 17.7 %collective-permute-start.20 = (f16[224,768]{1,0:T(8,128)(2,1)S(1)}, f16[224,768]{1,0:T(8,128)(2,1)S(1)}, u32[]{:S(2)}, u32[]{:S(2)}) collective-permute-start(f16[224,768]{1,0:T(8,128)(2,1)S(1)} %multiply_convert_fusion.2), channel_id=1, source_target_pairs={{0,64},{16,80},{32,96},{48,112},{64,0},{80,16},{96,32},{112,48},{1... | collective-permute-start | bytes 1032200 | tf_op jit(solution)/shard_map/ppermute | solution.py:349
  119.1 17.6 %collective-permute-start.14 = (f16[224,768]{1,0:T(8,128)(2,1)S(1)}, f16[224,768]{1,0:T(8,128)(2,1)S(1)}, u32[]{:S(2)}, u32[]{:S(2)}) collective-permute-start(f16[224,768]{1,0:T(8,128)(2,1)S(1)} %multiply_convert_fusion.3), channel_id=1, source_target_pairs={{0,16},{16,0},{32,48},{48,32},{64,80},{80,64},{96,112},{112,96},{1... | collective-permute-start | bytes 1032200 | tf_op jit(solution)/shard_map/ppermute | solution.py:345
  120.1 16.6 %collective-permute-start.15 = (f16[224,768]{1,0:T(8,128)(2,1)S(1)}, f16[224,768]{1,0:T(8,128)(2,1)S(1)}, u32[]{:S(2)}, u32[]{:S(2)}) collective-permute-start(f16[224,768]{1,0:T(8,128)(2,1)S(1)} %collective-permute-done.10), channel_id=1, source_target_pairs={{0,16},{16,0},{32,48},{48,32},{64,80},{80,64},{96,112},{112,96},{1... | collective-permute-start | bytes 1032200 | tf_op jit(solution)/shard_map/ppermute | solution.py:345
  126.4 10.3 %collective-permute-start.16 = (f16[224,768]{1,0:T(8,128)(2,1)S(1)}, f16[224,768]{1,0:T(8,128)(2,1)S(1)}, u32[]{:S(2)}, u32[]{:S(2)}) collective-permute-start(f16[224,768]{1,0:T(8,128)(2,1)S(1)} %collective-permute-done.11), channel_id=1, source_target_pairs={{0,16},{16,0},{32,48},{48,32},{64,80},{80,64},{96,112},{112,96},{1... | collective-permute-start | bytes 1032200 | tf_op jit(solution)/shard_map/ppermute | solution.py:345
  135.1 2.5 %collective-permute-start.17 = (f16[224,768]{1,0:T(8,128)(2,1)S(1)}, f16[224,768]{1,0:T(8,128)(2,1)S(1)}, u32[]{:S(2)}, u32[]{:S(2)}) collective-permute-start(f16[224,768]{1,0:T(8,128)(2,1)S(1)} %collective-permute-done.12), channel_id=1, source_target_pairs={{0,16},{16,0},{32,48},{48,32},{64,80},{80,64},{96,112},{112,96},{1... | collective-permute-start | bytes 1032200 | tf_op jit(solution)/shard_map/ppermute | solution.py:345
  137.6 2.6 %collective-permute-start.21 = (f16[224,768]{1,0:T(8,128)(2,1)S(1)}, f16[224,768]{1,0:T(8,128)(2,1)S(1)}, u32[]{:S(2)}, u32[]{:S(2)}) collective-permute-start(f16[224,768]{1,0:T(8,128)(2,1)S(1)} %multiply_convert_fusion.2), channel_id=1, source_target_pairs={{0,16},{16,0},{32,48},{48,32},{64,80},{80,64},{96,112},{112,96},{1... | collective-permute-start | bytes 1032200 | tf_op jit(solution)/shard_map/ppermute | solution.py:381
  137.9 2.3 %collective-permute-start.22 = (f16[224,768]{1,0:T(8,128)(2,1)S(1)}, f16[224,768]{1,0:T(8,128)(2,1)S(1)}, u32[]{:S(2)}, u32[]{:S(2)}) collective-permute-start(f16[224,768]{1,0:T(8,128)(2,1)S(1)} %collective-permute-done.18), channel_id=1, source_target_pairs={{0,16},{16,0},{32,48},{48,32},{64,80},{80,64},{96,112},{112,96},{1... | collective-permute-start | bytes 1032200 | tf_op jit(solution)/shard_map/ppermute | solution.py:381
  138.1 2.1 %collective-permute-start.23 = (f16[224,768]{1,0:T(8,128)(2,1)S(1)}, f16[224,768]{1,0:T(8,128)(2,1)S(1)}, u32[]{:S(2)}, u32[]{:S(2)}) collective-permute-start(f16[224,768]{1,0:T(8,128)(2,1)S(1)} %collective-permute-done.19), channel_id=1, source_target_pairs={{0,16},{16,0},{32,48},{48,32},{64,80},{80,64},{96,112},{112,96},{1... | collective-permute-start | bytes 1032200 | tf_op jit(solution)/shard_map/ppermute | solution.py:381
  138.4 2.2 %collective-permute-start.24 = (f16[224,768]{1,0:T(8,128)(2,1)S(1)}, f16[224,768]{1,0:T(8,128)(2,1)S(1)}, u32[]{:S(2)}, u32[]{:S(2)}) collective-permute-start(f16[224,768]{1,0:T(8,128)(2,1)S(1)} %collective-permute-done.20), channel_id=1, source_target_pairs={{0,16},{16,0},{32,48},{48,32},{64,80},{80,64},{96,112},{112,96},{1... | collective-permute-start | bytes 1032200 | tf_op jit(solution)/shard_map/ppermute | solution.py:381
  141.3 1.2 copy-start.3
  141.3 1.3 copy-start.4
  141.3 1.5 %copy-start.5 = (f32[1,224,768]{2,1,0:T(8,128)S(1)}, f32[1,224,768]{2,1,0:T(8,128)}, u32[]{:S(2)}) copy-start(f32[1,224,768]{2,1,0:T(8,128)} %param.16) | copy-start | bytes 2064388
  141.9 2.3 %copy-start.2 = (f32[3,2,224,768]{3,2,1,0:T(8,128)S(1)}, f32[3,2,224,768]{3,2,1,0:T(8,128)}, u32[]{:S(2)}) copy-start(f32[3,2,224,768]{3,2,1,0:T(8,128)} %copy-done.1) | copy-start | bytes 12386308

commit v4 on v3

--- a/solution.py
+++ b/solution.py
@@ -44,7 +44,7 @@
 
 
 def encode_state(w, m, v):
-    root = jnp.sqrt(jnp.sqrt(jnp.sqrt(jnp.minimum(jnp.abs(m) * (1.0 / 0.75), 1.0))))
+    root = jnp.exp2(0.125 * jnp.log2(jnp.clip(jnp.abs(m) * (1.0 / 0.75), 1e-30, 1.0)))
     qm = jnp.round(jnp.where(m < 0, -root, root) * 32767.0).astype(jnp.int32)
     qv = jnp.round(jnp.sqrt(jnp.clip(v * 5.0, 0.0, 1.0)) * 65535.0).astype(jnp.int32)
     return (w * 2.0**32).astype(jnp.int32), qm * 65536 + qv
@@ -273,7 +273,7 @@
 
 def finish(grads, w, m, v, held):
     rows, cols = w.shape
-    step = 32
+    step = 112
     flat = pl.BlockSpec((step, cols), lambda i: (i, 0))
     pair = pl.BlockSpec((2, step, cols), lambda i: (0, i, 0))
     return pl.pallas_call(
@@ -288,7 +288,7 @@
             jax.ShapeDtypeStruct((2, rows, cols), F32),
             jax.ShapeDtypeStruct((2, rows, cols), F32),
         ],
-        compiler_params=pltpu.CompilerParams(vmem_limit_bytes=10 << 20),
+        compiler_params=pltpu.CompilerParams(vmem_limit_bytes=26 << 20),
     )(*grads, w, m, v, held)
 
 

time: 149 us -> 147 us (0.987)
  Pallas kernels: 27.9 us -> 26.3 us
  transfers between devices with their start and end apart: 26 -> 26, of which waited for: 11 -> 11; matrix products, arithmetic and copies ran while one was open for 6% -> 7% of each run, Pallas kernels for 9% -> 9%
where the time goes in v4:
time: 147 us
  waiting for transfers between devices  49.8 us (34%)
  starting transfers between devices  30.8 us (21%)
  Pallas kernels  26.3 us (18%)
  blocking collectives  21.2 us (14%)
  other arithmetic  10.1 us (7%)
  local copies, waits for them, and re-layouts  7.68 us (5%)
    ppermute x6, waiting for transfers between devices, spread(): return [own] + [lax.ppermute(own, 'expert', x_shift(d)) for d in (1, -1, 2)]  23.8 us
    ppermute x6, waiting for transfers between devices, send(): return lax.ppermute(value, ('expert', 'dp'), plane_shift(d, first))  23.8 us
    all_to_all x1, blocking collectives, exchange(): lax.all_to_all(total, ('expert', 'dp'), 0, 0, axis_index_groups=groups, t...  21.2 us
    pallas_call x2, Pallas kernels, partial(): pl.pallas_call(functools.partial(partial_kernel, which), grid_spec=pltpu....  20.4 us
    ppermute x6, starting transfers between devices, send(): return lax.ppermute(value, ('expert', 'dp'), plane_shift(d, first))  11.7 us
    ppermute x6, starting transfers between devices, swap(): return lax.ppermute(value, 'expert', core_swap())  5.41 us
    all_to_all x1, starting transfers between devices, exchange(): lax.all_to_all(total, ('expert', 'dp'), 0, 0, axis_index_groups=groups, t...  5.37 us
    unnamed x38, local copies, waits for them, and re-layouts  5.33 us
  transfers between devices with their start and end apart: 26, of which 11 were waited for; matrix products, arithmetic and copies ran while one was open for 7% of the time, Pallas kernels for 9%

profile of v4, /device:TPU:15, one launch (start us, length us, event | category | flops | bytes accessed | tf_op | source)
XLA Modules:
  0.0 146.8 jit_solution(95867042386941161)
XLA Ops:
  0.7 0.8 copy.21
  1.5 10.3 %shard_map.120 = (f32[4,224,768]{2,1,0:T(8,128)}, f32[4,224,768]{2,1,0:T(8,128)}, f32[4,224,768]{2,1,0:T(8,128)}, f32[4,224,768]{2,1,0:T(8,128)}, s32[2,224,768]{2,1,0:T(8,128)}) custom-call(s32[3]{0:T(128)S(1)} %pad_add_fusion.2.here, s32[16,3]{1,0:T(8,128)S(1)} %bitcast.24, bf16[1280,3584]{1,0:T(8,128)(2,1)} %bitcast.29, bf16[1280,768]{1,0:T(8,128)(2,1)} %bitcast.31, ...), custom_call_target="tpu_custom_call" | custom-call | flops 8589934592 | bytes 16777216 | tf_op jit(solution)/shard_map/pallas_call | solution.py:186
  11.8 0.8 collective-permute-start
  12.6 1.9 %convert_element_type.137 = f16[4,224,768]{2,1,0:T(8,128)(2,1)S(1)} convert(f32[4,224,768]{2,1,0:T(8,128)} %get-tuple-element.59) | non-fusion elementwise | flops 688128 | bytes 4128768 | tf_op jit(solution)/shard_map/convert_element_type | solution.py:327
  14.8 0.8 collective-permute-done
  15.6 1.6 %collective-permute-start.1 = (f16[4,224,768]{2,1,0:T(8,128)(2,1)S(1)}, f16[4,224,768]{2,1,0:T(8,128)(2,1)S(1)}, u32[]{:S(2)}, u32[]{:S(2)}) collective-permute-start(f16[4,224,768]{2,1,0:T(8,128)(2,1)S(1)} %convert_element_type.137), channel_id=1, source_target_pairs={{0,4},{1,5},{2,6},{3,7},{4,8},{5,9},{6,10},{7,11},{8,12},{9,13},{1... | collective-permute-start | bytes 4128776 | tf_op jit(solution)/shard_map/ppermute | solution.py:30
  17.2 2.1 %collective-permute-start.2 = (f16[4,224,768]{2,1,0:T(8,128)(2,1)S(1)}, f16[4,224,768]{2,1,0:T(8,128)(2,1)S(1)}, u32[]{:S(2)}, u32[]{:S(2)}) collective-permute-start(f16[4,224,768]{2,1,0:T(8,128)(2,1)S(1)} %convert_element_type.138), channel_id=1, source_target_pairs={{0,12},{1,13},{2,14},{3,15},{4,0},{5,1},{6,2},{7,3},{8,4},{9,5},{1... | collective-permute-start | bytes 4128776 | tf_op jit(solution)/shard_map/ppermute | solution.py:30
  19.6 0.6 collective-permute-start.3
  20.2 10.2 %shard_map.121 = (f32[4,224,768]{2,1,0:T(8,128)}, f32[4,224,768]{2,1,0:T(8,128)}, f32[4,224,768]{2,1,0:T(8,128)}, f32[4,224,768]{2,1,0:T(8,128)}) custom-call(s32[3]{0:T(128)S(1)} %pad_add_fusion.2.here, s32[16,3]{1,0:T(8,128)S(1)} %bitcast.25, bf16[1280,3584]{1,0:T(8,128)(2,1)} %bitcast.30, bf16[1280,768]{1,0:T(8,128)(2,1)} %bitcast.32), custom_call_target="tpu_custom_call" | custom-call | flops 8589934592 | bytes 16777216 | tf_op jit(solution)/shard_map/pallas_call | solution.py:186
  30.4 4.7 %collective-permute-done.1 = f16[4,224,768]{2,1,0:T(8,128)(2,1)S(1)} collective-permute-done((f16[4,224,768]{2,1,0:T(8,128)(2,1)S(1)}, f16[4,224,768]{2,1,0:T(8,128)(2,1)S(1)}, u32[]{:S(2)}, u32[]{:S(2)}) %collective-permute-start.1) | collective-permute-done | bytes 1376288 | tf_op jit(solution)/shard_map/ppermute | solution.py:30
  35.1 0.4 add_convert_fusion.1
  35.5 1.3 collective-permute-start.5
  37.0 2.7 %collective-permute-start.4 = (f16[4,224,768]{2,1,0:T(8,128)(2,1)S(1)}, f16[4,224,768]{2,1,0:T(8,128)(2,1)S(1)}, u32[]{:S(2)}, u32[]{:S(2)}) collective-permute-start(f16[4,224,768]{2,1,0:T(8,128)(2,1)S(1)} %convert_element_type.139), channel_id=1, source_target_pairs={{0,12},{1,13},{2,14},{3,15},{4,0},{5,1},{6,2},{7,3},{8,4},{9,5},{1... | collective-permute-start | bytes 4128776 | tf_op jit(solution)/shard_map/ppermute | solution.py:30
  39.8 14.1 %collective-permute-done.5 = f16[4,224,768]{2,1,0:T(8,128)(2,1)S(1)} collective-permute-done((f16[4,224,768]{2,1,0:T(8,128)(2,1)S(1)}, f16[4,224,768]{2,1,0:T(8,128)(2,1)S(1)}, u32[]{:S(2)}, u32[]{:S(2)}) %collective-permute-start.5) | collective-permute-done | bytes 1376288 | tf_op jit(solution)/shard_map/ppermute | solution.py:30
  53.9 1.1 collective-permute-done.4
  55.0 1.2 collective-permute-start.9
  56.2 0.5 add_convert_fusion
  56.7 3.8 %collective-permute-start.6 = (f16[4,224,768]{2,1,0:T(8,128)(2,1)S(1)}, f16[4,224,768]{2,1,0:T(8,128)(2,1)S(1)}, u32[]{:S(2)}, u32[]{:S(2)}) collective-permute-start(f16[4,224,768]{2,1,0:T(8,128)(2,1)S(1)} %add_convert_fusion), channel_id=1, source_target_pairs={{0,12},{1,13},{2,14},{3,15},{4,0},{5,1},{6,2},{7,3},{8,4},{9,5},{1... | collective-permute-start | bytes 4128776 | tf_op jit(solution)/shard_map/ppermute | solution.py:30
  60.6 0.6 collective-permute-start.8
  61.5 0.6 multiply_convert_fusion.1
  62.2 21.2 %all_to_all.10 = f16[4,224,768]{2,1,0:T(8,128)(2,1)S(1)} all-to-all(f16[4,224,768]{2,1,0:T(8,128)(2,1)S(1)} %multiply_convert_fusion.1), channel_id=1, replica_groups={{0,1,2,3},{4,5,6,7},{8,9,10,11},{12,13,14,15},{16,20,24,28},{17,21,25,2..., dimensions={0} | all-to-all | bytes 2752512 | tf_op jit(solution)/shard_map/all_to_all | solution.py:207
  83.4 3.9 %collective-permute-done.7 = f16[4,224,768]{2,1,0:T(8,128)(2,1)S(1)} collective-permute-done((f16[4,224,768]{2,1,0:T(8,128)(2,1)S(1)}, f16[4,224,768]{2,1,0:T(8,128)(2,1)S(1)}, u32[]{:S(2)}, u32[]{:S(2)}) %collective-permute-start.7) | collective-permute-done | bytes 1376288 | tf_op jit(solution)/shard_map/ppermute | solution.py:30
  87.2 1.6 %copy-done.8 = s32[2,2,224,768]{3,2,1,0:T(8,128)} copy-done((s32[2,2,224,768]{3,2,1,0:T(8,128)}, s32[2,2,224,768]{3,2,1,0:T(8,128)S(1)}, u32[]{:S(2)}) %copy-start.8) | copy-done | bytes 2752536
  88.8 1.8 %multiply_convert_fusion = f16[4,224,768]{2,1,0:T(8,128)(2,1)} fusion(f16[4,224,768]{2,1,0:T(8,128)(2,1)S(1)} %collective-permute-done.6, f32[4,224,768]{2,1,0:T(8,128)S(1)} %copy-done.10, f16[4,224,768]{2,1,0:T(8,128)(2,1)S(1)} %collective-permute-done.7), kind=kLoop, calls=%fused_computation.4 | loop fusion | flops 4128768 | bytes 6881280 | tf_op jit(solution)/shard_map/convert_element_type | solution.py:360
  90.6 5.4 %all-to-all-start.1 = ((f16[4,224,768]{2,1,0:T(8,128)(2,1)}), f16[4,224,768]{2,1,0:T(8,128)(2,1)S(1)}, u32[]{:S(2)}, u32[]{:S(2)}) async-start(f16[4,224,768]{2,1,0:T(8,128)(2,1)} %multiply_convert_fusion), calls=%async_computation.1 | async-start | bytes 2752512 | tf_op jit(solution)/shard_map/all_to_all | solution.py:207
  96.2 2.2 %collective-permute-start.10 = (f16[224,768]{1,0:T(8,128)(2,1)S(1)}, f16[224,768]{1,0:T(8,128)(2,1)S(1)}, u32[]{:S(2)}, u32[]{:S(2)}) collective-permute-start(f16[224,768]{1,0:T(8,128)(2,1)S(1)} %multiply_convert_fusion.3), channel_id=1, source_target_pairs={{0,32},{16,48},{32,64},{48,80},{64,96},{80,112},{96,0},{112,16},{1... | collective-permute-start | bytes 1032200 | tf_op jit(solution)/shard_map/ppermute | solution.py:349
  98.4 1.3 collective-permute-start.12
  99.9 0.6 gather_fusion
  100.7 2.9 %shard_map.122.held = f32[3,2,224,768]{3,2,1,0:T(8,128)S(1)} custom-call(s32[2]{0:T(128)S(1)} %compare_select_fusion.8.pick, s32[2,2,224,768]{3,2,1,0:T(8,128)} %copy-done.6, s32[2,2,224,768]{3,2,1,0:T(8,128)} %copy-done.7, s32[2,2,224,768]{3,2,1,0:T(8,128)} %copy-done.8, s32[2,224,768]{2,1,0:T(8,128)} %collective-permute-done.8.refs_3_, ...), custom_call_target="tpu_custom_call" | custom-call | tf_op jit(solution)/shard_map/pallas_call | solution.py:240
  103.6 1.9 %copy-done.1 = f32[3,2,224,768]{3,2,1,0:T(8,128)} copy-done((f32[3,2,224,768]{3,2,1,0:T(8,128)}, f32[3,2,224,768]{3,2,1,0:T(8,128)S(1)}, u32[]{:S(2)}) %copy-start.1) | copy-done | bytes 4128792
  105.5 7.5 %collective-permute-done.10 = f16[224,768]{1,0:T(8,128)(2,1)S(1)} collective-permute-done((f16[224,768]{1,0:T(8,128)(2,1)S(1)}, f16[224,768]{1,0:T(8,128)(2,1)S(1)}, u32[]{:S(2)}, u32[]{:S(2)}) %collective-permute-start.10) | collective-permute-done | bytes 344096 | tf_op jit(solution)/shard_map/ppermute | solution.py:349
  113.0 3.4 %collective-permute-done.11 = f16[224,768]{1,0:T(8,128)(2,1)S(1)} collective-permute-done((f16[224,768]{1,0:T(8,128)(2,1)S(1)}, f16[224,768]{1,0:T(8,128)(2,1)S(1)}, u32[]{:S(2)}, u32[]{:S(2)}) %collective-permute-start.11) | collective-permute-done | bytes 344096 | tf_op jit(solution)/shard_map/ppermute | solution.py:349
  116.8 1.5 collective-permute-start.19
  118.7 1.0 collective-permute-start.14
  119.8 6.3 %collective-permute-done.18 = f16[224,768]{1,0:T(8,128)(2,1)S(1)} collective-permute-done((f16[224,768]{1,0:T(8,128)(2,1)S(1)}, f16[224,768]{1,0:T(8,128)(2,1)S(1)}, u32[]{:S(2)}, u32[]{:S(2)}) %collective-permute-start.18) | collective-permute-done | bytes 344096 | tf_op jit(solution)/shard_map/ppermute | solution.py:349
  126.0 2.0 %collective-permute-start.16 = (f16[224,768]{1,0:T(8,128)(2,1)S(1)}, f16[224,768]{1,0:T(8,128)(2,1)S(1)}, u32[]{:S(2)}, u32[]{:S(2)}) collective-permute-start(f16[224,768]{1,0:T(8,128)(2,1)S(1)} %collective-permute-done.11), channel_id=1, source_target_pairs={{0,16},{16,0},{32,48},{48,32},{64,80},{80,64},{96,112},{112,96},{1... | collective-permute-start | bytes 1032200 | tf_op jit(solution)/shard_map/ppermute | solution.py:345
  128.0 6.7 %collective-permute-done.19 = f16[224,768]{1,0:T(8,128)(2,1)S(1)} collective-permute-done((f16[224,768]{1,0:T(8,128)(2,1)S(1)}, f16[224,768]{1,0:T(8,128)(2,1)S(1)}, u32[]{:S(2)}, u32[]{:S(2)}) %collective-permute-start.19) | collective-permute-done | bytes 344096 | tf_op jit(solution)/shard_map/ppermute | solution.py:349
  134.7 1.2 collective-permute-start.17
  136.3 0.8 collective-permute-done.17
  138.2 0.5 fusion.20
  138.7 0.5 fusion.13
  139.2 0.5 fusion.6
  139.8 0.5 collective-permute-done.24
  140.3 0.6 fusion.44.grad_1
  140.9 0.6 fusion.36.grad_0
  141.5 0.6 fusion.28.grad_own
  142.4 1.4 copy-done.2
  143.8 3.0 %shard_map.123 = (f32[224,768]{1,0:T(8,128)}, bf16[2,224,768]{2,1,0:T(8,128)(2,1)}, f32[2,224,768]{2,1,0:T(8,128)}, f32[2,224,768]{2,1,0:T(8,128)}) custom-call(f32[224,768]{1,0:T(8,128)S(1)} %fusion.28.grad_own, f32[224,768]{1,0:T(8,128)S(1)} %fusion.36.grad_0, f32[224,768]{1,0:T(8,128)S(1)} %fusion.44.grad_1, f32[224,768]{1,0:T(8,128)S(1)} %bitcast.19, ...), custom_call_target="tpu_custom_call" | custom-call | tf_op jit(solution)/shard_map/pallas_call | solution.py:279
  (85 shorter events, 4.4 us)
Async XLA Ops:
  0.6 99.9 %copy-start = (s32[8,2]{0,1:T(2,128)S(1)}, s32[8,2]{0,1:T(2,128)}, u32[]{:S(2)}) copy-start(s32[8,2]{0,1:T(2,128)} %param.13) | copy-start | bytes 196
  11.8 2.8 %copy-start.15 = (f32[4,224,768]{2,1,0:T(8,128)S(1)}, f32[4,224,768]{2,1,0:T(8,128)}, u32[]{:S(2)}) copy-start(f32[4,224,768]{2,1,0:T(8,128)} %get-tuple-element.60) | copy-start | bytes 8257540
  11.8 3.8 %collective-permute-start = (s32[2,224,768]{2,1,0:T(8,128)}, s32[2,224,768]{2,1,0:T(8,128)S(1)}, u32[]{:S(2)}, u32[]{:S(2)}) collective-permute-start(s32[2,224,768]{2,1,0:T(8,128)} %get-tuple-element.61), channel_id=1, source_target_pairs={{0,16},{16,0},{32,48},{48,32},{64,80},{80,64},{96,112},{112,96},{1... | collective-permute-start | bytes 4128776 | tf_op jit(solution)/shard_map/ppermute | solution.py:326
  14.6 4.8 %copy-start.16 = (s32[2,224,768]{2,1,0:T(8,128)S(1)}, s32[2,224,768]{2,1,0:T(8,128)}, u32[]{:S(2)}) copy-start(s32[2,224,768]{2,1,0:T(8,128)} %get-tuple-element.61) | copy-start | bytes 4128772
  15.6 19.5 %collective-permute-start.1 = (f16[4,224,768]{2,1,0:T(8,128)(2,1)S(1)}, f16[4,224,768]{2,1,0:T(8,128)(2,1)S(1)}, u32[]{:S(2)}, u32[]{:S(2)}) collective-permute-start(f16[4,224,768]{2,1,0:T(8,128)(2,1)S(1)} %convert_element_type.137), channel_id=1, source_target_pairs={{0,4},{1,5},{2,6},{3,7},{4,8},{5,9},{6,10},{7,11},{8,12},{9,13},{1... | collective-permute-start | bytes 4128776 | tf_op jit(solution)/shard_map/ppermute | solution.py:30
  17.2 17.8 %collective-permute-start.2 = (f16[4,224,768]{2,1,0:T(8,128)(2,1)S(1)}, f16[4,224,768]{2,1,0:T(8,128)(2,1)S(1)}, u32[]{:S(2)}, u32[]{:S(2)}) collective-permute-start(f16[4,224,768]{2,1,0:T(8,128)(2,1)S(1)} %convert_element_type.138), channel_id=1, source_target_pairs={{0,12},{1,13},{2,14},{3,15},{4,0},{5,1},{6,2},{7,3},{8,4},{9,5},{1... | collective-permute-start | bytes 4128776 | tf_op jit(solution)/shard_map/ppermute | solution.py:30
  19.6 10.8 %copy-start.6 = (s32[2,2,224,768]{3,2,1,0:T(8,128)}, s32[2,2,224,768]{3,2,1,0:T(8,128)S(1)}, u32[]{:S(2)}) copy-start(s32[2,2,224,768]{3,2,1,0:T(8,128)S(1)} %pad_add_fusion.refs_0_) | copy-start | bytes 8257540
  19.6 35.4 %collective-permute-start.3 = (s32[2,2,224,768]{3,2,1,0:T(8,128)S(1)}, s32[2,2,224,768]{3,2,1,0:T(8,128)S(1)}, u32[]{:S(2)}, u32[]{:S(2)}) collective-permute-start(s32[2,2,224,768]{3,2,1,0:T(8,128)S(1)} %pad_add_fusion.refs_0_), channel_id=1, source_target_pairs={{0,32},{16,112},{32,64},{48,16},{64,96},{80,48},{96,0},{112,80},{1... | collective-permute-start | bytes 8257544 | tf_op jit(solution)/shard_map/ppermute | solution.py:39
  20.2 14.9 %copy-start.11 = (f32[4,224,768]{2,1,0:T(8,128)S(1)}, f32[4,224,768]{2,1,0:T(8,128)}, u32[]{:S(2)}) copy-start(f32[4,224,768]{2,1,0:T(8,128)} %get-tuple-element.73) | copy-start | bytes 8257540
  35.1 1.8 %copy-start.14 = (f32[4,224,768]{2,1,0:T(8,128)S(1)}, f32[4,224,768]{2,1,0:T(8,128)}, u32[]{:S(2)}) copy-start(f32[4,224,768]{2,1,0:T(8,128)} %get-tuple-element.72) | copy-start | bytes 8257540
  35.4 20.8 %copy-start.12 = (f32[4,224,768]{2,1,0:T(8,128)S(1)}, f32[4,224,768]{2,1,0:T(8,128)}, u32[]{:S(2)}) copy-start(f32[4,224,768]{2,1,0:T(8,128)} %get-tuple-element.79) | copy-start | bytes 8257540
  35.5 18.4 %collective-permute-start.5 = (f16[4,224,768]{2,1,0:T(8,128)(2,1)S(1)}, f16[4,224,768]{2,1,0:T(8,128)(2,1)S(1)}, u32[]{:S(2)}, u32[]{:S(2)}) collective-permute-start(f16[4,224,768]{2,1,0:T(8,128)(2,1)S(1)} %add_convert_fusion.1), channel_id=1, source_target_pairs={{0,4},{1,5},{2,6},{3,7},{4,8},{5,9},{6,10},{7,11},{8,12},{9,13},{1... | collective-permute-start | bytes 4128776 | tf_op jit(solution)/shard_map/ppermute | solution.py:30
  37.0 18.0 %collective-permute-start.4 = (f16[4,224,768]{2,1,0:T(8,128)(2,1)S(1)}, f16[4,224,768]{2,1,0:T(8,128)(2,1)S(1)}, u32[]{:S(2)}, u32[]{:S(2)}) collective-permute-start(f16[4,224,768]{2,1,0:T(8,128)(2,1)S(1)} %convert_element_type.139), channel_id=1, source_target_pairs={{0,12},{1,13},{2,14},{3,15},{4,0},{5,1},{6,2},{7,3},{8,4},{9,5},{1... | collective-permute-start | bytes 4128776 | tf_op jit(solution)/shard_map/ppermute | solution.py:30
  55.0 5.5 %copy-start.7 = (s32[2,2,224,768]{3,2,1,0:T(8,128)}, s32[2,2,224,768]{3,2,1,0:T(8,128)S(1)}, u32[]{:S(2)}) copy-start(s32[2,2,224,768]{3,2,1,0:T(8,128)S(1)} %collective-permute-done.3.refs_1_) | copy-start | bytes 8257540
  55.0 32.2 %collective-permute-start.9 = (s32[2,2,224,768]{3,2,1,0:T(8,128)S(1)}, s32[2,2,224,768]{3,2,1,0:T(8,128)S(1)}, u32[]{:S(2)}, u32[]{:S(2)}) collective-permute-start(s32[2,2,224,768]{3,2,1,0:T(8,128)S(1)} %collective-permute-done.3.refs_1_), channel_id=1, source_target_pairs={{0,16},{16,0},{32,48},{48,32},{64,80},{80,64},{96,112},{112,96},{1... | collective-permute-start | bytes 8257544 | tf_op jit(solution)/shard_map/ppermute | solution.py:345
  56.2 5.0 %copy-start.13 = (f32[4,224,768]{2,1,0:T(8,128)S(1)}, f32[4,224,768]{2,1,0:T(8,128)}, u32[]{:S(2)}) copy-start(f32[4,224,768]{2,1,0:T(8,128)} %get-tuple-element.81) | copy-start | bytes 8257540
  56.7 4.8 %copy-start.9 = (f32[4,224,768]{2,1,0:T(8,128)S(1)}, f32[4,224,768]{2,1,0:T(8,128)}, u32[]{:S(2)}) copy-start(f32[4,224,768]{2,1,0:T(8,128)} %get-tuple-element.71) | copy-start | bytes 8257540
  56.7 26.7 %collective-permute-start.6 = (f16[4,224,768]{2,1,0:T(8,128)(2,1)S(1)}, f16[4,224,768]{2,1,0:T(8,128)(2,1)S(1)}, u32[]{:S(2)}, u32[]{:S(2)}) collective-permute-start(f16[4,224,768]{2,1,0:T(8,128)(2,1)S(1)} %add_convert_fusion), channel_id=1, source_target_pairs={{0,12},{1,13},{2,14},{3,15},{4,0},{5,1},{6,2},{7,3},{8,4},{9,5},{1... | collective-permute-start | bytes 4128776 | tf_op jit(solution)/shard_map/ppermute | solution.py:30
  60.6 22.8 %collective-permute-start.8 = (s32[2,224,768]{2,1,0:T(8,128)S(1)}, s32[2,224,768]{2,1,0:T(8,128)}, u32[]{:S(2)}, u32[]{:S(2)}) collective-permute-start(s32[2,224,768]{2,1,0:T(8,128)S(1)} %slice_bitcast_fusion), channel_id=1, source_target_pairs={{0,32},{16,112},{32,64},{48,16},{64,96},{80,48},{96,0},{112,80},{1... | collective-permute-start | bytes 4128776 | tf_op jit(solution)/shard_map/ppermute | solution.py:39
  61.4 25.8 %collective-permute-start.7 = (f16[4,224,768]{2,1,0:T(8,128)(2,1)S(1)}, f16[4,224,768]{2,1,0:T(8,128)(2,1)S(1)}, u32[]{:S(2)}, u32[]{:S(2)}) collective-permute-start(f16[4,224,768]{2,1,0:T(8,128)(2,1)S(1)} %convert_element_type.147), channel_id=1, source_target_pairs={{0,4},{1,5},{2,6},{3,7},{4,8},{5,9},{6,10},{7,11},{8,12},{9,13},{1... | collective-permute-start | bytes 4128776 | tf_op jit(solution)/shard_map/ppermute | solution.py:30
  62.1 26.7 %copy-start.10 = (f32[4,224,768]{2,1,0:T(8,128)S(1)}, f32[4,224,768]{2,1,0:T(8,128)}, u32[]{:S(2)}) copy-start(f32[4,224,768]{2,1,0:T(8,128)} %get-tuple-element.70) | copy-start | bytes 8257540
  87.2 1.6 %copy-start.8 = (s32[2,2,224,768]{3,2,1,0:T(8,128)}, s32[2,2,224,768]{3,2,1,0:T(8,128)S(1)}, u32[]{:S(2)}) copy-start(s32[2,2,224,768]{3,2,1,0:T(8,128)S(1)} %collective-permute-done.9.refs_2_) | copy-start | bytes 8257540
  88.8 11.9 %collective-permute-start.13 = (s32[2,224,768]{2,1,0:T(8,128)}, s32[2,224,768]{2,1,0:T(8,128)}, u32[]{:S(2)}, u32[]{:S(2)}) collective-permute-start(s32[2,224,768]{2,1,0:T(8,128)} %collective-permute-done.8.refs_3_), channel_id=1, source_target_pairs={{0,16},{16,0},{32,48},{48,32},{64,80},{80,64},{96,112},{112,96},{1... | collective-permute-start | bytes 4128776 | tf_op jit(solution)/shard_map/ppermute | solution.py:345
  90.6 9.2 %copy-start.18 = (s32[4]{0:T(128)S(1)}, s32[4]{0:T(128)}, u32[]{:S(2)}) copy-start(s32[4]{0:T(128)} %constant.106.clone) | copy-start | bytes 52
  90.6 9.2 %copy-start.17 = (s32[8,2]{0,1:T(2,128)S(1)}, s32[8,2]{0,1:T(2,128)}, u32[]{:S(2)}) copy-start(s32[8,2]{0,1:T(2,128)} %param.12) | copy-start | bytes 196
  90.6 25.8 %all-to-all-start.1 = ((f16[4,224,768]{2,1,0:T(8,128)(2,1)}), f16[4,224,768]{2,1,0:T(8,128)(2,1)S(1)}, u32[]{:S(2)}, u32[]{:S(2)}) async-start(f16[4,224,768]{2,1,0:T(8,128)(2,1)} %multiply_convert_fusion), calls=%async_computation.1 | async-start | bytes 2752512 | tf_op jit(solution)/shard_map/all_to_all | solution.py:207
  96.2 16.8 %collective-permute-start.10 = (f16[224,768]{1,0:T(8,128)(2,1)S(1)}, f16[224,768]{1,0:T(8,128)(2,1)S(1)}, u32[]{:S(2)}, u32[]{:S(2)}) collective-permute-start(f16[224,768]{1,0:T(8,128)(2,1)S(1)} %multiply_convert_fusion.3), channel_id=1, source_target_pairs={{0,32},{16,48},{32,64},{48,80},{64,96},{80,112},{96,0},{112,16},{1... | collective-permute-start | bytes 1032200 | tf_op jit(solution)/shard_map/ppermute | solution.py:349
  98.4 18.0 %collective-permute-start.11 = (f16[224,768]{1,0:T(8,128)(2,1)S(1)}, f16[224,768]{1,0:T(8,128)(2,1)S(1)}, u32[]{:S(2)}, u32[]{:S(2)}) collective-permute-start(f16[224,768]{1,0:T(8,128)(2,1)S(1)} %multiply_convert_fusion.3), channel_id=1, source_target_pairs={{0,96},{16,112},{32,0},{48,16},{64,32},{80,48},{96,64},{112,80},{1... | collective-permute-start | bytes 1032200 | tf_op jit(solution)/shard_map/ppermute | solution.py:349
  98.4 18.0 %collective-permute-start.12 = (f16[224,768]{1,0:T(8,128)(2,1)S(1)}, f16[224,768]{1,0:T(8,128)(2,1)S(1)}, u32[]{:S(2)}, u32[]{:S(2)}) collective-permute-start(f16[224,768]{1,0:T(8,128)(2,1)S(1)} %multiply_convert_fusion.3), channel_id=1, source_target_pairs={{0,64},{16,80},{32,96},{48,112},{64,0},{80,16},{96,32},{112,48},{1... | collective-permute-start | bytes 1032200 | tf_op jit(solution)/shard_map/ppermute | solution.py:349
  103.6 1.9 %copy-start.1 = (f32[3,2,224,768]{3,2,1,0:T(8,128)}, f32[3,2,224,768]{3,2,1,0:T(8,128)S(1)}, u32[]{:S(2)}) copy-start(f32[3,2,224,768]{3,2,1,0:T(8,128)S(1)} %shard_map.122.held) | copy-start | bytes 12386308
  116.7 9.4 %collective-permute-start.18 = (f16[224,768]{1,0:T(8,128)(2,1)S(1)}, f16[224,768]{1,0:T(8,128)(2,1)S(1)}, u32[]{:S(2)}, u32[]{:S(2)}) collective-permute-start(f16[224,768]{1,0:T(8,128)(2,1)S(1)} %multiply_convert_fusion.2), channel_id=1, source_target_pairs={{0,32},{16,48},{32,64},{48,80},{64,96},{80,112},{96,0},{112,16},{1... | collective-permute-start | bytes 1032200 | tf_op jit(solution)/shard_map/ppermute | solution.py:349
  116.8 17.9 %collective-permute-start.19 = (f16[224,768]{1,0:T(8,128)(2,1)S(1)}, f16[224,768]{1,0:T(8,128)(2,1)S(1)}, u32[]{:S(2)}, u32[]{:S(2)}) collective-permute-start(f16[224,768]{1,0:T(8,128)(2,1)S(1)} %multiply_convert_fusion.2), channel_id=1, source_target_pairs={{0,96},{16,112},{32,0},{48,16},{64,32},{80,48},{96,64},{112,80},{1... | collective-permute-start | bytes 1032200 | tf_op jit(solution)/shard_map/ppermute | solution.py:349
  118.6 17.7 %collective-permute-start.20 = (f16[224,768]{1,0:T(8,128)(2,1)S(1)}, f16[224,768]{1,0:T(8,128)(2,1)S(1)}, u32[]{:S(2)}, u32[]{:S(2)}) collective-permute-start(f16[224,768]{1,0:T(8,128)(2,1)S(1)} %multiply_convert_fusion.2), channel_id=1, source_target_pairs={{0,64},{16,80},{32,96},{48,112},{64,0},{80,16},{96,32},{112,48},{1... | collective-permute-start | bytes 1032200 | tf_op jit(solution)/shard_map/ppermute | solution.py:349
  118.7 17.6 %collective-permute-start.14 = (f16[224,768]{1,0:T(8,128)(2,1)S(1)}, f16[224,768]{1,0:T(8,128)(2,1)S(1)}, u32[]{:S(2)}, u32[]{:S(2)}) collective-permute-start(f16[224,768]{1,0:T(8,128)(2,1)S(1)} %multiply_convert_fusion.3), channel_id=1, source_target_pairs={{0,16},{16,0},{32,48},{48,32},{64,80},{80,64},{96,112},{112,96},{1... | collective-permute-start | bytes 1032200 | tf_op jit(solution)/shard_map/ppermute | solution.py:345
  119.7 16.6 %collective-permute-start.15 = (f16[224,768]{1,0:T(8,128)(2,1)S(1)}, f16[224,768]{1,0:T(8,128)(2,1)S(1)}, u32[]{:S(2)}, u32[]{:S(2)}) collective-permute-start(f16[224,768]{1,0:T(8,128)(2,1)S(1)} %collective-permute-done.10), channel_id=1, source_target_pairs={{0,16},{16,0},{32,48},{48,32},{64,80},{80,64},{96,112},{112,96},{1... | collective-permute-start | bytes 1032200 | tf_op jit(solution)/shard_map/ppermute | solution.py:345
  126.0 10.3 %collective-permute-start.16 = (f16[224,768]{1,0:T(8,128)(2,1)S(1)}, f16[224,768]{1,0:T(8,128)(2,1)S(1)}, u32[]{:S(2)}, u32[]{:S(2)}) collective-permute-start(f16[224,768]{1,0:T(8,128)(2,1)S(1)} %collective-permute-done.11), channel_id=1, source_target_pairs={{0,16},{16,0},{32,48},{48,32},{64,80},{80,64},{96,112},{112,96},{1... | collective-permute-start | bytes 1032200 | tf_op jit(solution)/shard_map/ppermute | solution.py:345
  134.7 2.5 %collective-permute-start.17 = (f16[224,768]{1,0:T(8,128)(2,1)S(1)}, f16[224,768]{1,0:T(8,128)(2,1)S(1)}, u32[]{:S(2)}, u32[]{:S(2)}) collective-permute-start(f16[224,768]{1,0:T(8,128)(2,1)S(1)} %collective-permute-done.12), channel_id=1, source_target_pairs={{0,16},{16,0},{32,48},{48,32},{64,80},{80,64},{96,112},{112,96},{1... | collective-permute-start | bytes 1032200 | tf_op jit(solution)/shard_map/ppermute | solution.py:345
  137.2 2.6 %collective-permute-start.21 = (f16[224,768]{1,0:T(8,128)(2,1)S(1)}, f16[224,768]{1,0:T(8,128)(2,1)S(1)}, u32[]{:S(2)}, u32[]{:S(2)}) collective-permute-start(f16[224,768]{1,0:T(8,128)(2,1)S(1)} %multiply_convert_fusion.2), channel_id=1, source_target_pairs={{0,16},{16,0},{32,48},{48,32},{64,80},{80,64},{96,112},{112,96},{1... | collective-permute-start | bytes 1032200 | tf_op jit(solution)/shard_map/ppermute | solution.py:381
  137.5 2.3 %collective-permute-start.22 = (f16[224,768]{1,0:T(8,128)(2,1)S(1)}, f16[224,768]{1,0:T(8,128)(2,1)S(1)}, u32[]{:S(2)}, u32[]{:S(2)}) collective-permute-start(f16[224,768]{1,0:T(8,128)(2,1)S(1)} %collective-permute-done.18), channel_id=1, source_target_pairs={{0,16},{16,0},{32,48},{48,32},{64,80},{80,64},{96,112},{112,96},{1... | collective-permute-start | bytes 1032200 | tf_op jit(solution)/shard_map/ppermute | solution.py:381
  137.7 2.1 %collective-permute-start.23 = (f16[224,768]{1,0:T(8,128)(2,1)S(1)}, f16[224,768]{1,0:T(8,128)(2,1)S(1)}, u32[]{:S(2)}, u32[]{:S(2)}) collective-permute-start(f16[224,768]{1,0:T(8,128)(2,1)S(1)} %collective-permute-done.19), channel_id=1, source_target_pairs={{0,16},{16,0},{32,48},{48,32},{64,80},{80,64},{96,112},{112,96},{1... | collective-permute-start | bytes 1032200 | tf_op jit(solution)/shard_map/ppermute | solution.py:381
  138.0 2.2 %collective-permute-start.24 = (f16[224,768]{1,0:T(8,128)(2,1)S(1)}, f16[224,768]{1,0:T(8,128)(2,1)S(1)}, u32[]{:S(2)}, u32[]{:S(2)}) collective-permute-start(f16[224,768]{1,0:T(8,128)(2,1)S(1)} %collective-permute-done.20), channel_id=1, source_target_pairs={{0,16},{16,0},{32,48},{48,32},{64,80},{80,64},{96,112},{112,96},{1... | collective-permute-start | bytes 1032200 | tf_op jit(solution)/shard_map/ppermute | solution.py:381
  140.9 1.2 copy-start.3
  140.9 1.3 copy-start.4
  140.9 1.5 %copy-start.5 = (f32[1,224,768]{2,1,0:T(8,128)S(1)}, f32[1,224,768]{2,1,0:T(8,128)}, u32[]{:S(2)}) copy-start(f32[1,224,768]{2,1,0:T(8,128)} %param.16) | copy-start | bytes 2064388
  141.5 2.3 %copy-start.2 = (f32[3,2,224,768]{3,2,1,0:T(8,128)S(1)}, f32[3,2,224,768]{3,2,1,0:T(8,128)}, u32[]{:S(2)}) copy-start(f32[3,2,224,768]{3,2,1,0:T(8,128)} %copy-done.1) | copy-start | bytes 12386308

commit v5 on v4

--- a/solution.py
+++ b/solution.py
@@ -353,11 +353,12 @@
     cross_state = swap(beside)
     sum_a = (part0[0] + both_up.astype(F32) + raw_down.astype(F32)) * 0.5
     got_a = exchange(sum_a.astype(F16))
-    got_a, both_down, raw_up, far_state, cross_state = lax.optimization_barrier(
-        (got_a, both_down, raw_up, far_state, cross_state)
+    got_a, both_down, raw_up, far_state = lax.optimization_barrier(
+        (got_a, both_down, raw_up, far_state)
     )
     sum_b = (part1[0] + raw_up.astype(F32) + both_down.astype(F32)) * 0.5
     got_b = exchange(sum_b.astype(F16))
+    got_a, cross_state = lax.optimization_barrier((got_a, cross_state))
     same_a = spread(got_a)
 
     at = (mine_new // 2 - x) % NX

time: 147 us -> 147 us (level)
    unnamed x38 -> x34, local copies, waits for them, and re-layouts: 5.33 us -> 3.72 us
  transfers between devices with their start and end apart: 26 -> 26, of which waited for: 11 -> 12; matrix products, arithmetic and copies ran while one was open for 7% -> 7% of each run, Pallas kernels for 9% -> 9%
where the time goes in v5:
time: 147 us
  waiting for transfers between devices  49.9 us (34%)
  starting transfers between devices  30.7 us (21%)
  Pallas kernels  26.3 us (18%)
  blocking collectives  21.1 us (14%)
  other arithmetic  10 us (7%)
  local copies, waits for them, and re-layouts  7.41 us (5%)
    ppermute x6, waiting for transfers between devices, send(): return lax.ppermute(value, ('expert', 'dp'), plane_shift(d, first))  23.9 us
    ppermute x6, waiting for transfers between devices, spread(): return [own] + [lax.ppermute(own, 'expert', x_shift(d)) for d in (1, -1, 2)]  22.9 us
    all_to_all x1, blocking collectives, exchange(): lax.all_to_all(total, ('expert', 'dp'), 0, 0, axis_index_groups=groups, t...  21.1 us
    pallas_call x2, Pallas kernels, partial(): pl.pallas_call(functools.partial(partial_kernel, which), grid_spec=pltpu....  20.5 us
    ppermute x6, starting transfers between devices, send(): return lax.ppermute(value, ('expert', 'dp'), plane_shift(d, first))  11.7 us
    ppermute x6, starting transfers between devices, swap(): return lax.ppermute(value, 'expert', core_swap())  5.48 us
    all_to_all x1, starting transfers between devices, exchange(): lax.all_to_all(total, ('expert', 'dp'), 0, 0, axis_index_groups=groups, t...  5.29 us
    ppermute x6, starting transfers between devices, spread(): return [own] + [lax.ppermute(own, 'expert', x_shift(d)) for d in (1, -1, 2)]  5.15 us
  transfers between devices with their start and end apart: 26, of which 12 were waited for; matrix products, arithmetic and copies ran while one was open for 7% of the time, Pallas kernels for 9%

profile of v5, /device:TPU:15, one launch (start us, length us, event | category | flops | bytes accessed | tf_op | source)
XLA Modules:
  0.0 146.6 jit_solution(9094009760365388629)
XLA Ops:
  0.7 0.8 copy.21
  1.5 10.3 %shard_map.120 = (f32[4,224,768]{2,1,0:T(8,128)}, f32[4,224,768]{2,1,0:T(8,128)}, f32[4,224,768]{2,1,0:T(8,128)}, f32[4,224,768]{2,1,0:T(8,128)}, s32[2,224,768]{2,1,0:T(8,128)}) custom-call(s32[3]{0:T(128)S(1)} %pad_add_fusion.2.here, s32[16,3]{1,0:T(8,128)S(1)} %bitcast.24, bf16[1280,3584]{1,0:T(8,128)(2,1)} %bitcast.29, bf16[1280,768]{1,0:T(8,128)(2,1)} %bitcast.31, ...), custom_call_target="tpu_custom_call" | custom-call | flops 8589934592 | bytes 16777216 | tf_op jit(solution)/shard_map/pallas_call | solution.py:186
  11.8 0.8 collective-permute-start
  12.6 2.0 %convert_element_type.137 = f16[4,224,768]{2,1,0:T(8,128)(2,1)S(1)} convert(f32[4,224,768]{2,1,0:T(8,128)} %get-tuple-element.60) | non-fusion elementwise | flops 688128 | bytes 4128768 | tf_op jit(solution)/shard_map/convert_element_type | solution.py:327
  14.8 0.8 collective-permute-done
  15.6 1.6 %collective-permute-start.1 = (f16[4,224,768]{2,1,0:T(8,128)(2,1)S(1)}, f16[4,224,768]{2,1,0:T(8,128)(2,1)S(1)}, u32[]{:S(2)}, u32[]{:S(2)}) collective-permute-start(f16[4,224,768]{2,1,0:T(8,128)(2,1)S(1)} %convert_element_type.137), channel_id=1, source_target_pairs={{0,4},{1,5},{2,6},{3,7},{4,8},{5,9},{6,10},{7,11},{8,12},{9,13},{1... | collective-permute-start | bytes 4128776 | tf_op jit(solution)/shard_map/ppermute | solution.py:30
  17.2 2.1 %collective-permute-start.2 = (f16[4,224,768]{2,1,0:T(8,128)(2,1)S(1)}, f16[4,224,768]{2,1,0:T(8,128)(2,1)S(1)}, u32[]{:S(2)}, u32[]{:S(2)}) collective-permute-start(f16[4,224,768]{2,1,0:T(8,128)(2,1)S(1)} %convert_element_type.138), channel_id=1, source_target_pairs={{0,12},{1,13},{2,14},{3,15},{4,0},{5,1},{6,2},{7,3},{8,4},{9,5},{1... | collective-permute-start | bytes 4128776 | tf_op jit(solution)/shard_map/ppermute | solution.py:30
  19.6 0.6 collective-permute-start.3
  20.2 10.2 %shard_map.121 = (f32[4,224,768]{2,1,0:T(8,128)}, f32[4,224,768]{2,1,0:T(8,128)}, f32[4,224,768]{2,1,0:T(8,128)}, f32[4,224,768]{2,1,0:T(8,128)}) custom-call(s32[3]{0:T(128)S(1)} %pad_add_fusion.2.here, s32[16,3]{1,0:T(8,128)S(1)} %bitcast.25, bf16[1280,3584]{1,0:T(8,128)(2,1)} %bitcast.30, bf16[1280,768]{1,0:T(8,128)(2,1)} %bitcast.32), custom_call_target="tpu_custom_call" | custom-call | flops 8589934592 | bytes 16777216 | tf_op jit(solution)/shard_map/pallas_call | solution.py:186
  30.4 4.7 %collective-permute-done.1 = f16[4,224,768]{2,1,0:T(8,128)(2,1)S(1)} collective-permute-done((f16[4,224,768]{2,1,0:T(8,128)(2,1)S(1)}, f16[4,224,768]{2,1,0:T(8,128)(2,1)S(1)}, u32[]{:S(2)}, u32[]{:S(2)}) %collective-permute-start.1) | collective-permute-done | bytes 1376288 | tf_op jit(solution)/shard_map/ppermute | solution.py:30
  35.1 0.5 add_convert_fusion.1
  35.6 1.4 collective-permute-start.5
  37.2 2.6 %collective-permute-start.4 = (f16[4,224,768]{2,1,0:T(8,128)(2,1)S(1)}, f16[4,224,768]{2,1,0:T(8,128)(2,1)S(1)}, u32[]{:S(2)}, u32[]{:S(2)}) collective-permute-start(f16[4,224,768]{2,1,0:T(8,128)(2,1)S(1)} %convert_element_type.139), channel_id=1, source_target_pairs={{0,12},{1,13},{2,14},{3,15},{4,0},{5,1},{6,2},{7,3},{8,4},{9,5},{1... | collective-permute-start | bytes 4128776 | tf_op jit(solution)/shard_map/ppermute | solution.py:30
  39.8 14.2 %collective-permute-done.5 = f16[4,224,768]{2,1,0:T(8,128)(2,1)S(1)} collective-permute-done((f16[4,224,768]{2,1,0:T(8,128)(2,1)S(1)}, f16[4,224,768]{2,1,0:T(8,128)(2,1)S(1)}, u32[]{:S(2)}, u32[]{:S(2)}) %collective-permute-start.5) | collective-permute-done | bytes 1376288 | tf_op jit(solution)/shard_map/ppermute | solution.py:30
  54.0 1.0 collective-permute-done.4
  55.0 1.3 collective-permute-start.9
  56.8 3.8 %collective-permute-start.6 = (f16[4,224,768]{2,1,0:T(8,128)(2,1)S(1)}, f16[4,224,768]{2,1,0:T(8,128)(2,1)S(1)}, u32[]{:S(2)}, u32[]{:S(2)}) collective-permute-start(f16[4,224,768]{2,1,0:T(8,128)(2,1)S(1)} %add_convert_fusion), channel_id=1, source_target_pairs={{0,12},{1,13},{2,14},{3,15},{4,0},{5,1},{6,2},{7,3},{8,4},{9,5},{1... | collective-permute-start | bytes 4128776 | tf_op jit(solution)/shard_map/ppermute | solution.py:30
  60.6 1.4 slice_bitcast_fusion
  62.0 0.6 collective-permute-start.8
  62.9 0.6 multiply_convert_fusion.1
  63.5 21.1 %all_to_all.10 = f16[4,224,768]{2,1,0:T(8,128)(2,1)S(1)} all-to-all(f16[4,224,768]{2,1,0:T(8,128)(2,1)S(1)} %multiply_convert_fusion.1), channel_id=1, replica_groups={{0,1,2,3},{4,5,6,7},{8,9,10,11},{12,13,14,15},{16,20,24,28},{17,21,25,2..., dimensions={0} | all-to-all | bytes 2752512 | tf_op jit(solution)/shard_map/all_to_all | solution.py:207
  84.7 4.0 %collective-permute-done.7 = f16[4,224,768]{2,1,0:T(8,128)(2,1)S(1)} collective-permute-done((f16[4,224,768]{2,1,0:T(8,128)(2,1)S(1)}, f16[4,224,768]{2,1,0:T(8,128)(2,1)S(1)}, u32[]{:S(2)}, u32[]{:S(2)}) %collective-permute-start.7) | collective-permute-done | bytes 1376288 | tf_op jit(solution)/shard_map/ppermute | solution.py:30
  88.6 1.7 %multiply_convert_fusion = f16[4,224,768]{2,1,0:T(8,128)(2,1)} fusion(f16[4,224,768]{2,1,0:T(8,128)(2,1)S(1)} %collective-permute-done.6, f32[4,224,768]{2,1,0:T(8,128)S(1)} %copy-done.8, f16[4,224,768]{2,1,0:T(8,128)(2,1)S(1)} %collective-permute-done.7), kind=kLoop, calls=%fused_computation.4 | loop fusion | flops 4128768 | bytes 6881280 | tf_op jit(solution)/shard_map/convert_element_type | solution.py:360
  90.3 5.3 %all-to-all-start.1 = ((f16[4,224,768]{2,1,0:T(8,128)(2,1)}), f16[4,224,768]{2,1,0:T(8,128)(2,1)S(1)}, u32[]{:S(2)}, u32[]{:S(2)}) async-start(f16[4,224,768]{2,1,0:T(8,128)(2,1)} %multiply_convert_fusion), calls=%async_computation.1 | async-start | bytes 2752512 | tf_op jit(solution)/shard_map/all_to_all | solution.py:207
  95.9 2.2 %collective-permute-start.10 = (f16[224,768]{1,0:T(8,128)(2,1)S(1)}, f16[224,768]{1,0:T(8,128)(2,1)S(1)}, u32[]{:S(2)}, u32[]{:S(2)}) collective-permute-start(f16[224,768]{1,0:T(8,128)(2,1)S(1)} %multiply_convert_fusion.3), channel_id=1, source_target_pairs={{0,32},{16,48},{32,64},{48,80},{64,96},{80,112},{96,0},{112,16},{1... | collective-permute-start | bytes 1032200 | tf_op jit(solution)/shard_map/ppermute | solution.py:349
  98.1 1.3 collective-permute-start.12
  99.5 0.6 gather_fusion
  100.4 2.9 %shard_map.122.held = f32[3,2,224,768]{3,2,1,0:T(8,128)S(1)} custom-call(s32[2]{0:T(128)S(1)} %compare_select_fusion.8.pick, s32[2,2,224,768]{3,2,1,0:T(8,128)} %copy-done.6, s32[2,2,224,768]{3,2,1,0:T(8,128)} %collective-permute-done.3.refs_1_, s32[2,2,224,768]{3,2,1,0:T(8,128)} %collective-permute-done.9.refs_2_, ...), custom_call_target="tpu_custom_call" | custom-call | tf_op jit(solution)/shard_map/pallas_call | solution.py:240
  103.2 1.9 %copy-done.1 = f32[3,2,224,768]{3,2,1,0:T(8,128)} copy-done((f32[3,2,224,768]{3,2,1,0:T(8,128)}, f32[3,2,224,768]{3,2,1,0:T(8,128)S(1)}, u32[]{:S(2)}) %copy-start.1) | copy-done | bytes 4128792
  105.2 1.1 all-to-all-done.1
  106.2 6.5 %collective-permute-done.10 = f16[224,768]{1,0:T(8,128)(2,1)S(1)} collective-permute-done((f16[224,768]{1,0:T(8,128)(2,1)S(1)}, f16[224,768]{1,0:T(8,128)(2,1)S(1)}, u32[]{:S(2)}, u32[]{:S(2)}) %collective-permute-start.10) | collective-permute-done | bytes 344096 | tf_op jit(solution)/shard_map/ppermute | solution.py:349
  112.7 3.4 %collective-permute-done.11 = f16[224,768]{1,0:T(8,128)(2,1)S(1)} collective-permute-done((f16[224,768]{1,0:T(8,128)(2,1)S(1)}, f16[224,768]{1,0:T(8,128)(2,1)S(1)}, u32[]{:S(2)}, u32[]{:S(2)}) %collective-permute-start.11) | collective-permute-done | bytes 344096 | tf_op jit(solution)/shard_map/ppermute | solution.py:349
  116.5 1.5 collective-permute-start.19
  118.4 1.0 collective-permute-start.14
  119.5 6.3 %collective-permute-done.18 = f16[224,768]{1,0:T(8,128)(2,1)S(1)} collective-permute-done((f16[224,768]{1,0:T(8,128)(2,1)S(1)}, f16[224,768]{1,0:T(8,128)(2,1)S(1)}, u32[]{:S(2)}, u32[]{:S(2)}) %collective-permute-start.18) | collective-permute-done | bytes 344096 | tf_op jit(solution)/shard_map/ppermute | solution.py:349
  125.8 2.0 %collective-permute-start.16 = (f16[224,768]{1,0:T(8,128)(2,1)S(1)}, f16[224,768]{1,0:T(8,128)(2,1)S(1)}, u32[]{:S(2)}, u32[]{:S(2)}) collective-permute-start(f16[224,768]{1,0:T(8,128)(2,1)S(1)} %collective-permute-done.11), channel_id=1, source_target_pairs={{0,16},{16,0},{32,48},{48,32},{64,80},{80,64},{96,112},{112,96},{1... | collective-permute-start | bytes 1032200 | tf_op jit(solution)/shard_map/ppermute | solution.py:345
  127.7 6.7 %collective-permute-done.19 = f16[224,768]{1,0:T(8,128)(2,1)S(1)} collective-permute-done((f16[224,768]{1,0:T(8,128)(2,1)S(1)}, f16[224,768]{1,0:T(8,128)(2,1)S(1)}, u32[]{:S(2)}, u32[]{:S(2)}) %collective-permute-start.19) | collective-permute-done | bytes 344096 | tf_op jit(solution)/shard_map/ppermute | solution.py:349
  134.4 1.2 collective-permute-start.17
  136.0 0.8 collective-permute-done.17
  137.9 0.5 fusion.20
  138.4 0.5 fusion.13
  139.0 0.5 fusion.6
  139.5 0.5 collective-permute-done.24
  140.0 0.6 fusion.44.grad_1
  140.6 0.6 fusion.36.grad_0
  141.2 0.6 fusion.28.grad_own
  142.1 1.4 copy-done.2
  143.5 3.0 %shard_map.123 = (f32[224,768]{1,0:T(8,128)}, bf16[2,224,768]{2,1,0:T(8,128)(2,1)}, f32[2,224,768]{2,1,0:T(8,128)}, f32[2,224,768]{2,1,0:T(8,128)}) custom-call(f32[224,768]{1,0:T(8,128)S(1)} %fusion.28.grad_own, f32[224,768]{1,0:T(8,128)S(1)} %fusion.36.grad_0, f32[224,768]{1,0:T(8,128)S(1)} %fusion.44.grad_1, f32[224,768]{1,0:T(8,128)S(1)} %bitcast.19, ...), custom_call_target="tpu_custom_call" | custom-call | tf_op jit(solution)/shard_map/pallas_call | solution.py:279
  (81 shorter events, 4.7 us)
Async XLA Ops:
  0.6 99.5 %copy-start = (s32[8,2]{0,1:T(2,128)S(1)}, s32[8,2]{0,1:T(2,128)}, u32[]{:S(2)}) copy-start(s32[8,2]{0,1:T(2,128)} %param.13) | copy-start | bytes 196
  11.8 2.8 %copy-start.13 = (f32[4,224,768]{2,1,0:T(8,128)S(1)}, f32[4,224,768]{2,1,0:T(8,128)}, u32[]{:S(2)}) copy-start(f32[4,224,768]{2,1,0:T(8,128)} %get-tuple-element.61) | copy-start | bytes 8257540
  11.8 3.8 %collective-permute-start = (s32[2,224,768]{2,1,0:T(8,128)}, s32[2,224,768]{2,1,0:T(8,128)S(1)}, u32[]{:S(2)}, u32[]{:S(2)}) collective-permute-start(s32[2,224,768]{2,1,0:T(8,128)} %get-tuple-element.62), channel_id=1, source_target_pairs={{0,16},{16,0},{32,48},{48,32},{64,80},{80,64},{96,112},{112,96},{1... | collective-permute-start | bytes 4128776 | tf_op jit(solution)/shard_map/ppermute | solution.py:326
  14.6 4.7 %copy-start.14 = (s32[2,224,768]{2,1,0:T(8,128)S(1)}, s32[2,224,768]{2,1,0:T(8,128)}, u32[]{:S(2)}) copy-start(s32[2,224,768]{2,1,0:T(8,128)} %get-tuple-element.62) | copy-start | bytes 4128772
  15.6 19.5 %collective-permute-start.1 = (f16[4,224,768]{2,1,0:T(8,128)(2,1)S(1)}, f16[4,224,768]{2,1,0:T(8,128)(2,1)S(1)}, u32[]{:S(2)}, u32[]{:S(2)}) collective-permute-start(f16[4,224,768]{2,1,0:T(8,128)(2,1)S(1)} %convert_element_type.137), channel_id=1, source_target_pairs={{0,4},{1,5},{2,6},{3,7},{4,8},{5,9},{6,10},{7,11},{8,12},{9,13},{1... | collective-permute-start | bytes 4128776 | tf_op jit(solution)/shard_map/ppermute | solution.py:30
  17.2 17.8 %collective-permute-start.2 = (f16[4,224,768]{2,1,0:T(8,128)(2,1)S(1)}, f16[4,224,768]{2,1,0:T(8,128)(2,1)S(1)}, u32[]{:S(2)}, u32[]{:S(2)}) collective-permute-start(f16[4,224,768]{2,1,0:T(8,128)(2,1)S(1)} %convert_element_type.138), channel_id=1, source_target_pairs={{0,12},{1,13},{2,14},{3,15},{4,0},{5,1},{6,2},{7,3},{8,4},{9,5},{1... | collective-permute-start | bytes 4128776 | tf_op jit(solution)/shard_map/ppermute | solution.py:30
  19.6 10.8 %copy-start.6 = (s32[2,2,224,768]{3,2,1,0:T(8,128)}, s32[2,2,224,768]{3,2,1,0:T(8,128)S(1)}, u32[]{:S(2)}) copy-start(s32[2,2,224,768]{3,2,1,0:T(8,128)S(1)} %pad_add_fusion.refs_0_) | copy-start | bytes 8257540
  19.6 35.4 %collective-permute-start.3 = (s32[2,2,224,768]{3,2,1,0:T(8,128)S(1)}, s32[2,2,224,768]{3,2,1,0:T(8,128)}, u32[]{:S(2)}, u32[]{:S(2)}) collective-permute-start(s32[2,2,224,768]{3,2,1,0:T(8,128)S(1)} %pad_add_fusion.refs_0_), channel_id=1, source_target_pairs={{0,32},{16,112},{32,64},{48,16},{64,96},{80,48},{96,0},{112,80},{1... | collective-permute-start | bytes 8257544 | tf_op jit(solution)/shard_map/ppermute | solution.py:39
  20.2 14.9 %copy-start.9 = (f32[4,224,768]{2,1,0:T(8,128)S(1)}, f32[4,224,768]{2,1,0:T(8,128)}, u32[]{:S(2)}) copy-start(f32[4,224,768]{2,1,0:T(8,128)} %get-tuple-element.74) | copy-start | bytes 8257540
  35.1 2.0 %copy-start.12 = (f32[4,224,768]{2,1,0:T(8,128)S(1)}, f32[4,224,768]{2,1,0:T(8,128)}, u32[]{:S(2)}) copy-start(f32[4,224,768]{2,1,0:T(8,128)} %get-tuple-element.73) | copy-start | bytes 8257540
  35.5 20.7 %copy-start.10 = (f32[4,224,768]{2,1,0:T(8,128)S(1)}, f32[4,224,768]{2,1,0:T(8,128)}, u32[]{:S(2)}) copy-start(f32[4,224,768]{2,1,0:T(8,128)} %get-tuple-element.80) | copy-start | bytes 8257540
  35.6 18.4 %collective-permute-start.5 = (f16[4,224,768]{2,1,0:T(8,128)(2,1)S(1)}, f16[4,224,768]{2,1,0:T(8,128)(2,1)S(1)}, u32[]{:S(2)}, u32[]{:S(2)}) collective-permute-start(f16[4,224,768]{2,1,0:T(8,128)(2,1)S(1)} %add_convert_fusion.1), channel_id=1, source_target_pairs={{0,4},{1,5},{2,6},{3,7},{4,8},{5,9},{6,10},{7,11},{8,12},{9,13},{1... | collective-permute-start | bytes 4128776 | tf_op jit(solution)/shard_map/ppermute | solution.py:30
  37.2 17.8 %collective-permute-start.4 = (f16[4,224,768]{2,1,0:T(8,128)(2,1)S(1)}, f16[4,224,768]{2,1,0:T(8,128)(2,1)S(1)}, u32[]{:S(2)}, u32[]{:S(2)}) collective-permute-start(f16[4,224,768]{2,1,0:T(8,128)(2,1)S(1)} %convert_element_type.139), channel_id=1, source_target_pairs={{0,12},{1,13},{2,14},{3,15},{4,0},{5,1},{6,2},{7,3},{8,4},{9,5},{1... | collective-permute-start | bytes 4128776 | tf_op jit(solution)/shard_map/ppermute | solution.py:30
  55.0 40.6 %collective-permute-start.9 = (s32[2,2,224,768]{3,2,1,0:T(8,128)}, s32[2,2,224,768]{3,2,1,0:T(8,128)}, u32[]{:S(2)}, u32[]{:S(2)}) collective-permute-start(s32[2,2,224,768]{3,2,1,0:T(8,128)} %collective-permute-done.3.refs_1_), channel_id=1, source_target_pairs={{0,16},{16,0},{32,48},{48,32},{64,80},{80,64},{96,112},{112,96},{1... | collective-permute-start | bytes 8257544 | tf_op jit(solution)/shard_map/ppermute | solution.py:345
  56.3 6.3 %copy-start.11 = (f32[4,224,768]{2,1,0:T(8,128)S(1)}, f32[4,224,768]{2,1,0:T(8,128)}, u32[]{:S(2)}) copy-start(f32[4,224,768]{2,1,0:T(8,128)} %get-tuple-element.82) | copy-start | bytes 8257540
  56.8 6.2 %copy-start.7 = (f32[4,224,768]{2,1,0:T(8,128)S(1)}, f32[4,224,768]{2,1,0:T(8,128)}, u32[]{:S(2)}) copy-start(f32[4,224,768]{2,1,0:T(8,128)} %get-tuple-element.72) | copy-start | bytes 8257540
  56.8 27.9 %collective-permute-start.6 = (f16[4,224,768]{2,1,0:T(8,128)(2,1)S(1)}, f16[4,224,768]{2,1,0:T(8,128)(2,1)S(1)}, u32[]{:S(2)}, u32[]{:S(2)}) collective-permute-start(f16[4,224,768]{2,1,0:T(8,128)(2,1)S(1)} %add_convert_fusion), channel_id=1, source_target_pairs={{0,12},{1,13},{2,14},{3,15},{4,0},{5,1},{6,2},{7,3},{8,4},{9,5},{1... | collective-permute-start | bytes 4128776 | tf_op jit(solution)/shard_map/ppermute | solution.py:30
  62.0 22.6 %collective-permute-start.8 = (s32[2,224,768]{2,1,0:T(8,128)S(1)}, s32[2,224,768]{2,1,0:T(8,128)}, u32[]{:S(2)}, u32[]{:S(2)}) collective-permute-start(s32[2,224,768]{2,1,0:T(8,128)S(1)} %slice_bitcast_fusion), channel_id=1, source_target_pairs={{0,32},{16,112},{32,64},{48,16},{64,96},{80,48},{96,0},{112,80},{1... | collective-permute-start | bytes 4128776 | tf_op jit(solution)/shard_map/ppermute | solution.py:39
  62.8 25.8 %collective-permute-start.7 = (f16[4,224,768]{2,1,0:T(8,128)(2,1)S(1)}, f16[4,224,768]{2,1,0:T(8,128)(2,1)S(1)}, u32[]{:S(2)}, u32[]{:S(2)}) collective-permute-start(f16[4,224,768]{2,1,0:T(8,128)(2,1)S(1)} %convert_element_type.147), channel_id=1, source_target_pairs={{0,4},{1,5},{2,6},{3,7},{4,8},{5,9},{6,10},{7,11},{8,12},{9,13},{1... | collective-permute-start | bytes 4128776 | tf_op jit(solution)/shard_map/ppermute | solution.py:30
  63.5 25.1 %copy-start.8 = (f32[4,224,768]{2,1,0:T(8,128)S(1)}, f32[4,224,768]{2,1,0:T(8,128)}, u32[]{:S(2)}) copy-start(f32[4,224,768]{2,1,0:T(8,128)} %get-tuple-element.71) | copy-start | bytes 8257540
  88.6 11.7 %collective-permute-start.13 = (s32[2,224,768]{2,1,0:T(8,128)}, s32[2,224,768]{2,1,0:T(8,128)}, u32[]{:S(2)}, u32[]{:S(2)}) collective-permute-start(s32[2,224,768]{2,1,0:T(8,128)} %collective-permute-done.8.refs_3_), channel_id=1, source_target_pairs={{0,16},{16,0},{32,48},{48,32},{64,80},{80,64},{96,112},{112,96},{1... | collective-permute-start | bytes 4128776 | tf_op jit(solution)/shard_map/ppermute | solution.py:345
  90.3 9.1 %copy-start.16 = (s32[4]{0:T(128)S(1)}, s32[4]{0:T(128)}, u32[]{:S(2)}) copy-start(s32[4]{0:T(128)} %constant.106.clone) | copy-start | bytes 52
  90.3 9.1 %copy-start.15 = (s32[8,2]{0,1:T(2,128)S(1)}, s32[8,2]{0,1:T(2,128)}, u32[]{:S(2)}) copy-start(s32[8,2]{0,1:T(2,128)} %param.12) | copy-start | bytes 196
  90.3 15.9 %all-to-all-start.1 = ((f16[4,224,768]{2,1,0:T(8,128)(2,1)}), f16[4,224,768]{2,1,0:T(8,128)(2,1)S(1)}, u32[]{:S(2)}, u32[]{:S(2)}) async-start(f16[4,224,768]{2,1,0:T(8,128)(2,1)} %multiply_convert_fusion), calls=%async_computation.1 | async-start | bytes 2752512 | tf_op jit(solution)/shard_map/all_to_all | solution.py:207
  95.9 16.8 %collective-permute-start.10 = (f16[224,768]{1,0:T(8,128)(2,1)S(1)}, f16[224,768]{1,0:T(8,128)(2,1)S(1)}, u32[]{:S(2)}, u32[]{:S(2)}) collective-permute-start(f16[224,768]{1,0:T(8,128)(2,1)S(1)} %multiply_convert_fusion.3), channel_id=1, source_target_pairs={{0,32},{16,48},{32,64},{48,80},{64,96},{80,112},{96,0},{112,16},{1... | collective-permute-start | bytes 1032200 | tf_op jit(solution)/shard_map/ppermute | solution.py:349
  98.1 18.0 %collective-permute-start.11 = (f16[224,768]{1,0:T(8,128)(2,1)S(1)}, f16[224,768]{1,0:T(8,128)(2,1)S(1)}, u32[]{:S(2)}, u32[]{:S(2)}) collective-permute-start(f16[224,768]{1,0:T(8,128)(2,1)S(1)} %multiply_convert_fusion.3), channel_id=1, source_target_pairs={{0,96},{16,112},{32,0},{48,16},{64,32},{80,48},{96,64},{112,80},{1... | collective-permute-start | bytes 1032200 | tf_op jit(solution)/shard_map/ppermute | solution.py:349
  98.1 18.0 %collective-permute-start.12 = (f16[224,768]{1,0:T(8,128)(2,1)S(1)}, f16[224,768]{1,0:T(8,128)(2,1)S(1)}, u32[]{:S(2)}, u32[]{:S(2)}) collective-permute-start(f16[224,768]{1,0:T(8,128)(2,1)S(1)} %multiply_convert_fusion.3), channel_id=1, source_target_pairs={{0,64},{16,80},{32,96},{48,112},{64,0},{80,16},{96,32},{112,48},{1... | collective-permute-start | bytes 1032200 | tf_op jit(solution)/shard_map/ppermute | solution.py:349
  103.2 1.9 %copy-start.1 = (f32[3,2,224,768]{3,2,1,0:T(8,128)}, f32[3,2,224,768]{3,2,1,0:T(8,128)S(1)}, u32[]{:S(2)}) copy-start(f32[3,2,224,768]{3,2,1,0:T(8,128)S(1)} %shard_map.122.held) | copy-start | bytes 12386308
  116.4 9.4 %collective-permute-start.18 = (f16[224,768]{1,0:T(8,128)(2,1)S(1)}, f16[224,768]{1,0:T(8,128)(2,1)S(1)}, u32[]{:S(2)}, u32[]{:S(2)}) collective-permute-start(f16[224,768]{1,0:T(8,128)(2,1)S(1)} %multiply_convert_fusion.2), channel_id=1, source_target_pairs={{0,32},{16,48},{32,64},{48,80},{64,96},{80,112},{96,0},{112,16},{1... | collective-permute-start | bytes 1032200 | tf_op jit(solution)/shard_map/ppermute | solution.py:349
  116.5 17.9 %collective-permute-start.19 = (f16[224,768]{1,0:T(8,128)(2,1)S(1)}, f16[224,768]{1,0:T(8,128)(2,1)S(1)}, u32[]{:S(2)}, u32[]{:S(2)}) collective-permute-start(f16[224,768]{1,0:T(8,128)(2,1)S(1)} %multiply_convert_fusion.2), channel_id=1, source_target_pairs={{0,96},{16,112},{32,0},{48,16},{64,32},{80,48},{96,64},{112,80},{1... | collective-permute-start | bytes 1032200 | tf_op jit(solution)/shard_map/ppermute | solution.py:349
  118.3 17.7 %collective-permute-start.20 = (f16[224,768]{1,0:T(8,128)(2,1)S(1)}, f16[224,768]{1,0:T(8,128)(2,1)S(1)}, u32[]{:S(2)}, u32[]{:S(2)}) collective-permute-start(f16[224,768]{1,0:T(8,128)(2,1)S(1)} %multiply_convert_fusion.2), channel_id=1, source_target_pairs={{0,64},{16,80},{32,96},{48,112},{64,0},{80,16},{96,32},{112,48},{1... | collective-permute-start | bytes 1032200 | tf_op jit(solution)/shard_map/ppermute | solution.py:349
  118.4 17.6 %collective-permute-start.14 = (f16[224,768]{1,0:T(8,128)(2,1)S(1)}, f16[224,768]{1,0:T(8,128)(2,1)S(1)}, u32[]{:S(2)}, u32[]{:S(2)}) collective-permute-start(f16[224,768]{1,0:T(8,128)(2,1)S(1)} %multiply_convert_fusion.3), channel_id=1, source_target_pairs={{0,16},{16,0},{32,48},{48,32},{64,80},{80,64},{96,112},{112,96},{1... | collective-permute-start | bytes 1032200 | tf_op jit(solution)/shard_map/ppermute | solution.py:345
  119.4 16.6 %collective-permute-start.15 = (f16[224,768]{1,0:T(8,128)(2,1)S(1)}, f16[224,768]{1,0:T(8,128)(2,1)S(1)}, u32[]{:S(2)}, u32[]{:S(2)}) collective-permute-start(f16[224,768]{1,0:T(8,128)(2,1)S(1)} %collective-permute-done.10), channel_id=1, source_target_pairs={{0,16},{16,0},{32,48},{48,32},{64,80},{80,64},{96,112},{112,96},{1... | collective-permute-start | bytes 1032200 | tf_op jit(solution)/shard_map/ppermute | solution.py:345
  125.8 10.3 %collective-permute-start.16 = (f16[224,768]{1,0:T(8,128)(2,1)S(1)}, f16[224,768]{1,0:T(8,128)(2,1)S(1)}, u32[]{:S(2)}, u32[]{:S(2)}) collective-permute-start(f16[224,768]{1,0:T(8,128)(2,1)S(1)} %collective-permute-done.11), channel_id=1, source_target_pairs={{0,16},{16,0},{32,48},{48,32},{64,80},{80,64},{96,112},{112,96},{1... | collective-permute-start | bytes 1032200 | tf_op jit(solution)/shard_map/ppermute | solution.py:345
  134.4 2.5 %collective-permute-start.17 = (f16[224,768]{1,0:T(8,128)(2,1)S(1)}, f16[224,768]{1,0:T(8,128)(2,1)S(1)}, u32[]{:S(2)}, u32[]{:S(2)}) collective-permute-start(f16[224,768]{1,0:T(8,128)(2,1)S(1)} %collective-permute-done.12), channel_id=1, source_target_pairs={{0,16},{16,0},{32,48},{48,32},{64,80},{80,64},{96,112},{112,96},{1... | collective-permute-start | bytes 1032200 | tf_op jit(solution)/shard_map/ppermute | solution.py:345
  136.9 2.6 %collective-permute-start.21 = (f16[224,768]{1,0:T(8,128)(2,1)S(1)}, f16[224,768]{1,0:T(8,128)(2,1)S(1)}, u32[]{:S(2)}, u32[]{:S(2)}) collective-permute-start(f16[224,768]{1,0:T(8,128)(2,1)S(1)} %multiply_convert_fusion.2), channel_id=1, source_target_pairs={{0,16},{16,0},{32,48},{48,32},{64,80},{80,64},{96,112},{112,96},{1... | collective-permute-start | bytes 1032200 | tf_op jit(solution)/shard_map/ppermute | solution.py:382
  137.3 2.3 %collective-permute-start.22 = (f16[224,768]{1,0:T(8,128)(2,1)S(1)}, f16[224,768]{1,0:T(8,128)(2,1)S(1)}, u32[]{:S(2)}, u32[]{:S(2)}) collective-permute-start(f16[224,768]{1,0:T(8,128)(2,1)S(1)} %collective-permute-done.18), channel_id=1, source_target_pairs={{0,16},{16,0},{32,48},{48,32},{64,80},{80,64},{96,112},{112,96},{1... | collective-permute-start | bytes 1032200 | tf_op jit(solution)/shard_map/ppermute | solution.py:382
  137.4 2.1 %collective-permute-start.23 = (f16[224,768]{1,0:T(8,128)(2,1)S(1)}, f16[224,768]{1,0:T(8,128)(2,1)S(1)}, u32[]{:S(2)}, u32[]{:S(2)}) collective-permute-start(f16[224,768]{1,0:T(8,128)(2,1)S(1)} %collective-permute-done.19), channel_id=1, source_target_pairs={{0,16},{16,0},{32,48},{48,32},{64,80},{80,64},{96,112},{112,96},{1... | collective-permute-start | bytes 1032200 | tf_op jit(solution)/shard_map/ppermute | solution.py:382
  137.8 2.2 %collective-permute-start.24 = (f16[224,768]{1,0:T(8,128)(2,1)S(1)}, f16[224,768]{1,0:T(8,128)(2,1)S(1)}, u32[]{:S(2)}, u32[]{:S(2)}) collective-permute-start(f16[224,768]{1,0:T(8,128)(2,1)S(1)} %collective-permute-done.20), channel_id=1, source_target_pairs={{0,16},{16,0},{32,48},{48,32},{64,80},{80,64},{96,112},{112,96},{1... | collective-permute-start | bytes 1032200 | tf_op jit(solution)/shard_map/ppermute | solution.py:382
  140.6 1.2 copy-start.3
  140.6 1.3 copy-start.4
  140.6 1.5 %copy-start.5 = (f32[1,224,768]{2,1,0:T(8,128)S(1)}, f32[1,224,768]{2,1,0:T(8,128)}, u32[]{:S(2)}) copy-start(f32[1,224,768]{2,1,0:T(8,128)} %param.16) | copy-start | bytes 2064388
  141.2 2.3 %copy-start.2 = (f32[3,2,224,768]{3,2,1,0:T(8,128)S(1)}, f32[3,2,224,768]{3,2,1,0:T(8,128)}, u32[]{:S(2)}) copy-start(f32[3,2,224,768]{3,2,1,0:T(8,128)} %copy-done.1) | copy-start | bytes 12386308

commit v6 on v5

--- a/solution.py
+++ b/solution.py
@@ -369,7 +369,8 @@
     got_b, same_a, held = lax.optimization_barrier((got_b, same_a, held))
     same_b = spread(got_b)
     other_a = [swap(v) for v in same_a]
-    other_a, same_b = lax.optimization_barrier((other_a, same_b))
+    swapped = swap(same_b[0])
+    other_a, same_b, swapped = lax.optimization_barrier((other_a, same_b, swapped))
 
     def weighted(same, other, s, t):
         total = 0.0
@@ -379,7 +380,7 @@
 
     grads_a = [weighted(same_a, other_a, 0, t) for t in range(3)]
     grads_a = lax.optimization_barrier(grads_a)
-    other_b = [lax.ppermute(v, "expert", core_swap()) for v in same_b]
+    other_b = [swapped] + [swap(v) for v in same_b[1:]]
     grads = [grads_a[t] + weighted(same_b, other_b, 1, t) for t in range(3)]
     new_master, held_w, held_first, held_second = finish(
         grads, master[0], first_moment[0], second_moment[0], held

time: 147 us -> 147 us (level)
    ppermute x6 -> x10, starting transfers between devices: 5.48 us -> 6.45 us  [swap(): return lax.ppermute(value, 'expert', core_swap())]
  transfers between devices with their start and end apart: 26 -> 26, of which waited for: 12 -> 13; matrix products, arithmetic and copies ran while one was open for 7% -> 7% of each run, Pallas kernels for 9% -> 9%
where the time goes in v6:
time: 147 us
  waiting for transfers between devices  50.1 us (34%)
  starting transfers between devices  30.5 us (21%)
  Pallas kernels  26.3 us (18%)
  blocking collectives  21.1 us (14%)
  other arithmetic  10 us (7%)
  local copies, waits for them, and re-layouts  7.41 us (5%)
    ppermute x6, waiting for transfers between devices, send(): return lax.ppermute(value, ('expert', 'dp'), plane_shift(d, first))  23.9 us
    ppermute x6, waiting for transfers between devices, spread(): return [own] + [lax.ppermute(own, 'expert', x_shift(d)) for d in (1, -1, 2)]  22.9 us
    all_to_all x1, blocking collectives, exchange(): lax.all_to_all(total, ('expert', 'dp'), 0, 0, axis_index_groups=groups, t...  21.1 us
    pallas_call x2, Pallas kernels, partial(): pl.pallas_call(functools.partial(partial_kernel, which), grid_spec=pltpu....  20.5 us
    ppermute x6, starting transfers between devices, send(): return lax.ppermute(value, ('expert', 'dp'), plane_shift(d, first))  11.7 us
    ppermute x10, starting transfers between devices, swap(): return lax.ppermute(value, 'expert', core_swap())  6.45 us
    all_to_all x1, starting transfers between devices, exchange(): lax.all_to_all(total, ('expert', 'dp'), 0, 0, axis_index_groups=groups, t...  5.29 us
    ppermute x6, starting transfers between devices, spread(): return [own] + [lax.ppermute(own, 'expert', x_shift(d)) for d in (1, -1, 2)]  5.07 us
  transfers between devices with their start and end apart: 26, of which 13 were waited for; matrix products, arithmetic and copies ran while one was open for 7% of the time, Pallas kernels for 9%

profile of v6, /device:TPU:15, one launch (start us, length us, event | category | flops | bytes accessed | tf_op | source)
XLA Modules:
  0.0 146.6 jit_solution(4961183975446952017)
XLA Ops:
  0.7 0.8 copy.21
  1.5 10.3 %shard_map.120 = (f32[4,224,768]{2,1,0:T(8,128)}, f32[4,224,768]{2,1,0:T(8,128)}, f32[4,224,768]{2,1,0:T(8,128)}, f32[4,224,768]{2,1,0:T(8,128)}, s32[2,224,768]{2,1,0:T(8,128)}) custom-call(s32[3]{0:T(128)S(1)} %pad_add_fusion.2.here, s32[16,3]{1,0:T(8,128)S(1)} %bitcast.24, bf16[1280,3584]{1,0:T(8,128)(2,1)} %bitcast.29, bf16[1280,768]{1,0:T(8,128)(2,1)} %bitcast.31, ...), custom_call_target="tpu_custom_call" | custom-call | flops 8589934592 | bytes 16777216 | tf_op jit(solution)/shard_map/pallas_call | solution.py:186
  11.8 0.8 collective-permute-start
  12.6 2.0 %convert_element_type.137 = f16[4,224,768]{2,1,0:T(8,128)(2,1)S(1)} convert(f32[4,224,768]{2,1,0:T(8,128)} %get-tuple-element.61) | non-fusion elementwise | flops 688128 | bytes 4128768 | tf_op jit(solution)/shard_map/convert_element_type | solution.py:327
  14.8 0.8 collective-permute-done
  15.6 1.6 %collective-permute-start.1 = (f16[4,224,768]{2,1,0:T(8,128)(2,1)S(1)}, f16[4,224,768]{2,1,0:T(8,128)(2,1)S(1)}, u32[]{:S(2)}, u32[]{:S(2)}) collective-permute-start(f16[4,224,768]{2,1,0:T(8,128)(2,1)S(1)} %convert_element_type.137), channel_id=1, source_target_pairs={{0,4},{1,5},{2,6},{3,7},{4,8},{5,9},{6,10},{7,11},{8,12},{9,13},{1... | collective-permute-start | bytes 4128776 | tf_op jit(solution)/shard_map/ppermute | solution.py:30
  17.2 2.1 %collective-permute-start.2 = (f16[4,224,768]{2,1,0:T(8,128)(2,1)S(1)}, f16[4,224,768]{2,1,0:T(8,128)(2,1)S(1)}, u32[]{:S(2)}, u32[]{:S(2)}) collective-permute-start(f16[4,224,768]{2,1,0:T(8,128)(2,1)S(1)} %convert_element_type.138), channel_id=1, source_target_pairs={{0,12},{1,13},{2,14},{3,15},{4,0},{5,1},{6,2},{7,3},{8,4},{9,5},{1... | collective-permute-start | bytes 4128776 | tf_op jit(solution)/shard_map/ppermute | solution.py:30
  19.6 0.6 collective-permute-start.3
  20.2 10.2 %shard_map.121 = (f32[4,224,768]{2,1,0:T(8,128)}, f32[4,224,768]{2,1,0:T(8,128)}, f32[4,224,768]{2,1,0:T(8,128)}, f32[4,224,768]{2,1,0:T(8,128)}) custom-call(s32[3]{0:T(128)S(1)} %pad_add_fusion.2.here, s32[16,3]{1,0:T(8,128)S(1)} %bitcast.25, bf16[1280,3584]{1,0:T(8,128)(2,1)} %bitcast.30, bf16[1280,768]{1,0:T(8,128)(2,1)} %bitcast.32), custom_call_target="tpu_custom_call" | custom-call | flops 8589934592 | bytes 16777216 | tf_op jit(solution)/shard_map/pallas_call | solution.py:186
  30.4 4.7 %collective-permute-done.1 = f16[4,224,768]{2,1,0:T(8,128)(2,1)S(1)} collective-permute-done((f16[4,224,768]{2,1,0:T(8,128)(2,1)S(1)}, f16[4,224,768]{2,1,0:T(8,128)(2,1)S(1)}, u32[]{:S(2)}, u32[]{:S(2)}) %collective-permute-start.1) | collective-permute-done | bytes 1376288 | tf_op jit(solution)/shard_map/ppermute | solution.py:30
  35.1 0.5 add_convert_fusion.1
  35.6 1.4 collective-permute-start.5
  37.2 2.6 %collective-permute-start.4 = (f16[4,224,768]{2,1,0:T(8,128)(2,1)S(1)}, f16[4,224,768]{2,1,0:T(8,128)(2,1)S(1)}, u32[]{:S(2)}, u32[]{:S(2)}) collective-permute-start(f16[4,224,768]{2,1,0:T(8,128)(2,1)S(1)} %convert_element_type.139), channel_id=1, source_target_pairs={{0,12},{1,13},{2,14},{3,15},{4,0},{5,1},{6,2},{7,3},{8,4},{9,5},{1... | collective-permute-start | bytes 4128776 | tf_op jit(solution)/shard_map/ppermute | solution.py:30
  39.8 14.2 %collective-permute-done.5 = f16[4,224,768]{2,1,0:T(8,128)(2,1)S(1)} collective-permute-done((f16[4,224,768]{2,1,0:T(8,128)(2,1)S(1)}, f16[4,224,768]{2,1,0:T(8,128)(2,1)S(1)}, u32[]{:S(2)}, u32[]{:S(2)}) %collective-permute-start.5) | collective-permute-done | bytes 1376288 | tf_op jit(solution)/shard_map/ppermute | solution.py:30
  54.0 1.0 collective-permute-done.4
  55.0 1.3 collective-permute-start.9
  56.8 3.8 %collective-permute-start.6 = (f16[4,224,768]{2,1,0:T(8,128)(2,1)S(1)}, f16[4,224,768]{2,1,0:T(8,128)(2,1)S(1)}, u32[]{:S(2)}, u32[]{:S(2)}) collective-permute-start(f16[4,224,768]{2,1,0:T(8,128)(2,1)S(1)} %add_convert_fusion), channel_id=1, source_target_pairs={{0,12},{1,13},{2,14},{3,15},{4,0},{5,1},{6,2},{7,3},{8,4},{9,5},{1... | collective-permute-start | bytes 4128776 | tf_op jit(solution)/shard_map/ppermute | solution.py:30
  60.6 1.4 slice_bitcast_fusion
  62.0 0.6 collective-permute-start.8
  62.9 0.6 multiply_convert_fusion.1
  63.5 21.1 %all_to_all.10 = f16[4,224,768]{2,1,0:T(8,128)(2,1)S(1)} all-to-all(f16[4,224,768]{2,1,0:T(8,128)(2,1)S(1)} %multiply_convert_fusion.1), channel_id=1, replica_groups={{0,1,2,3},{4,5,6,7},{8,9,10,11},{12,13,14,15},{16,20,24,28},{17,21,25,2..., dimensions={0} | all-to-all | bytes 2752512 | tf_op jit(solution)/shard_map/all_to_all | solution.py:207
  84.7 4.0 %collective-permute-done.7 = f16[4,224,768]{2,1,0:T(8,128)(2,1)S(1)} collective-permute-done((f16[4,224,768]{2,1,0:T(8,128)(2,1)S(1)}, f16[4,224,768]{2,1,0:T(8,128)(2,1)S(1)}, u32[]{:S(2)}, u32[]{:S(2)}) %collective-permute-start.7) | collective-permute-done | bytes 1376288 | tf_op jit(solution)/shard_map/ppermute | solution.py:30
  88.6 1.7 %multiply_convert_fusion = f16[4,224,768]{2,1,0:T(8,128)(2,1)} fusion(f16[4,224,768]{2,1,0:T(8,128)(2,1)S(1)} %collective-permute-done.6, f32[4,224,768]{2,1,0:T(8,128)S(1)} %copy-done.8, f16[4,224,768]{2,1,0:T(8,128)(2,1)S(1)} %collective-permute-done.7), kind=kLoop, calls=%fused_computation.4 | loop fusion | flops 4128768 | bytes 6881280 | tf_op jit(solution)/shard_map/convert_element_type | solution.py:360
  90.3 5.3 %all-to-all-start.1 = ((f16[4,224,768]{2,1,0:T(8,128)(2,1)}), f16[4,224,768]{2,1,0:T(8,128)(2,1)S(1)}, u32[]{:S(2)}, u32[]{:S(2)}) async-start(f16[4,224,768]{2,1,0:T(8,128)(2,1)} %multiply_convert_fusion), calls=%async_computation.1 | async-start | bytes 2752512 | tf_op jit(solution)/shard_map/all_to_all | solution.py:207
  95.9 2.2 %collective-permute-start.10 = (f16[224,768]{1,0:T(8,128)(2,1)S(1)}, f16[224,768]{1,0:T(8,128)(2,1)S(1)}, u32[]{:S(2)}, u32[]{:S(2)}) collective-permute-start(f16[224,768]{1,0:T(8,128)(2,1)S(1)} %multiply_convert_fusion.3), channel_id=1, source_target_pairs={{0,32},{16,48},{32,64},{48,80},{64,96},{80,112},{96,0},{112,16},{1... | collective-permute-start | bytes 1032200 | tf_op jit(solution)/shard_map/ppermute | solution.py:349
  98.1 1.3 collective-permute-start.12
  99.5 0.6 gather_fusion
  100.4 2.9 %shard_map.122.held = f32[3,2,224,768]{3,2,1,0:T(8,128)S(1)} custom-call(s32[2]{0:T(128)S(1)} %compare_select_fusion.8.pick, s32[2,2,224,768]{3,2,1,0:T(8,128)} %copy-done.6, s32[2,2,224,768]{3,2,1,0:T(8,128)} %collective-permute-done.3.refs_1_, s32[2,2,224,768]{3,2,1,0:T(8,128)} %collective-permute-done.9.refs_2_, ...), custom_call_target="tpu_custom_call" | custom-call | tf_op jit(solution)/shard_map/pallas_call | solution.py:240
  103.2 1.9 %copy-done.1 = f32[3,2,224,768]{3,2,1,0:T(8,128)} copy-done((f32[3,2,224,768]{3,2,1,0:T(8,128)}, f32[3,2,224,768]{3,2,1,0:T(8,128)S(1)}, u32[]{:S(2)}) %copy-start.1) | copy-done | bytes 4128792
  105.2 1.1 all-to-all-done.1
  106.2 6.5 %collective-permute-done.10 = f16[224,768]{1,0:T(8,128)(2,1)S(1)} collective-permute-done((f16[224,768]{1,0:T(8,128)(2,1)S(1)}, f16[224,768]{1,0:T(8,128)(2,1)S(1)}, u32[]{:S(2)}, u32[]{:S(2)}) %collective-permute-start.10) | collective-permute-done | bytes 344096 | tf_op jit(solution)/shard_map/ppermute | solution.py:349
  112.7 3.4 %collective-permute-done.11 = f16[224,768]{1,0:T(8,128)(2,1)S(1)} collective-permute-done((f16[224,768]{1,0:T(8,128)(2,1)S(1)}, f16[224,768]{1,0:T(8,128)(2,1)S(1)}, u32[]{:S(2)}, u32[]{:S(2)}) %collective-permute-start.11) | collective-permute-done | bytes 344096 | tf_op jit(solution)/shard_map/ppermute | solution.py:349
  116.5 1.5 collective-permute-start.19
  118.3 1.1 collective-permute-start.21
  119.5 6.3 %collective-permute-done.18 = f16[224,768]{1,0:T(8,128)(2,1)S(1)} collective-permute-done((f16[224,768]{1,0:T(8,128)(2,1)S(1)}, f16[224,768]{1,0:T(8,128)(2,1)S(1)}, u32[]{:S(2)}, u32[]{:S(2)}) %collective-permute-start.18) | collective-permute-done | bytes 344096 | tf_op jit(solution)/shard_map/ppermute | solution.py:349
  125.8 2.0 %collective-permute-start.15 = (f16[224,768]{1,0:T(8,128)(2,1)S(1)}, f16[224,768]{1,0:T(8,128)(2,1)S(1)}, u32[]{:S(2)}, u32[]{:S(2)}) collective-permute-start(f16[224,768]{1,0:T(8,128)(2,1)S(1)} %collective-permute-done.10), channel_id=1, source_target_pairs={{0,16},{16,0},{32,48},{48,32},{64,80},{80,64},{96,112},{112,96},{1... | collective-permute-start | bytes 1032200 | tf_op jit(solution)/shard_map/ppermute | solution.py:345
  127.7 6.7 %collective-permute-done.19 = f16[224,768]{1,0:T(8,128)(2,1)S(1)} collective-permute-done((f16[224,768]{1,0:T(8,128)(2,1)S(1)}, f16[224,768]{1,0:T(8,128)(2,1)S(1)}, u32[]{:S(2)}, u32[]{:S(2)}) %collective-permute-start.19) | collective-permute-done | bytes 344096 | tf_op jit(solution)/shard_map/ppermute | solution.py:349
  134.4 1.2 collective-permute-start.16
  136.0 0.8 collective-permute-done.16
  136.9 0.5 collective-permute-done.17
  138.3 0.5 fusion.20
  138.8 0.5 fusion.13
  139.3 0.5 fusion.6
  140.0 0.6 fusion.44.grad_1
  140.6 0.6 fusion.36.grad_0
  141.2 0.6 fusion.28.grad_own
  142.1 1.4 copy-done.2
  143.5 3.0 %shard_map.123 = (f32[224,768]{1,0:T(8,128)}, bf16[2,224,768]{2,1,0:T(8,128)(2,1)}, f32[2,224,768]{2,1,0:T(8,128)}, f32[2,224,768]{2,1,0:T(8,128)}) custom-call(f32[224,768]{1,0:T(8,128)S(1)} %fusion.28.grad_own, f32[224,768]{1,0:T(8,128)S(1)} %fusion.36.grad_0, f32[224,768]{1,0:T(8,128)S(1)} %fusion.44.grad_1, f32[224,768]{1,0:T(8,128)S(1)} %bitcast.19, ...), custom_call_target="tpu_custom_call" | custom-call | tf_op jit(solution)/shard_map/pallas_call | solution.py:279
  (81 shorter events, 4.6 us)
Async XLA Ops:
  0.6 99.5 %copy-start = (s32[8,2]{0,1:T(2,128)S(1)}, s32[8,2]{0,1:T(2,128)}, u32[]{:S(2)}) copy-start(s32[8,2]{0,1:T(2,128)} %param.13) | copy-start | bytes 196
  11.8 2.8 %copy-start.13 = (f32[4,224,768]{2,1,0:T(8,128)S(1)}, f32[4,224,768]{2,1,0:T(8,128)}, u32[]{:S(2)}) copy-start(f32[4,224,768]{2,1,0:T(8,128)} %get-tuple-element.62) | copy-start | bytes 8257540
  11.8 3.8 %collective-permute-start = (s32[2,224,768]{2,1,0:T(8,128)}, s32[2,224,768]{2,1,0:T(8,128)S(1)}, u32[]{:S(2)}, u32[]{:S(2)}) collective-permute-start(s32[2,224,768]{2,1,0:T(8,128)} %get-tuple-element.63), channel_id=1, source_target_pairs={{0,16},{16,0},{32,48},{48,32},{64,80},{80,64},{96,112},{112,96},{1... | collective-permute-start | bytes 4128776 | tf_op jit(solution)/shard_map/ppermute | solution.py:326
  14.6 4.7 %copy-start.14 = (s32[2,224,768]{2,1,0:T(8,128)S(1)}, s32[2,224,768]{2,1,0:T(8,128)}, u32[]{:S(2)}) copy-start(s32[2,224,768]{2,1,0:T(8,128)} %get-tuple-element.63) | copy-start | bytes 4128772
  15.6 19.5 %collective-permute-start.1 = (f16[4,224,768]{2,1,0:T(8,128)(2,1)S(1)}, f16[4,224,768]{2,1,0:T(8,128)(2,1)S(1)}, u32[]{:S(2)}, u32[]{:S(2)}) collective-permute-start(f16[4,224,768]{2,1,0:T(8,128)(2,1)S(1)} %convert_element_type.137), channel_id=1, source_target_pairs={{0,4},{1,5},{2,6},{3,7},{4,8},{5,9},{6,10},{7,11},{8,12},{9,13},{1... | collective-permute-start | bytes 4128776 | tf_op jit(solution)/shard_map/ppermute | solution.py:30
  17.2 17.8 %collective-permute-start.2 = (f16[4,224,768]{2,1,0:T(8,128)(2,1)S(1)}, f16[4,224,768]{2,1,0:T(8,128)(2,1)S(1)}, u32[]{:S(2)}, u32[]{:S(2)}) collective-permute-start(f16[4,224,768]{2,1,0:T(8,128)(2,1)S(1)} %convert_element_type.138), channel_id=1, source_target_pairs={{0,12},{1,13},{2,14},{3,15},{4,0},{5,1},{6,2},{7,3},{8,4},{9,5},{1... | collective-permute-start | bytes 4128776 | tf_op jit(solution)/shard_map/ppermute | solution.py:30
  19.6 10.8 %copy-start.6 = (s32[2,2,224,768]{3,2,1,0:T(8,128)}, s32[2,2,224,768]{3,2,1,0:T(8,128)S(1)}, u32[]{:S(2)}) copy-start(s32[2,2,224,768]{3,2,1,0:T(8,128)S(1)} %pad_add_fusion.refs_0_) | copy-start | bytes 8257540
  19.6 35.4 %collective-permute-start.3 = (s32[2,2,224,768]{3,2,1,0:T(8,128)S(1)}, s32[2,2,224,768]{3,2,1,0:T(8,128)}, u32[]{:S(2)}, u32[]{:S(2)}) collective-permute-start(s32[2,2,224,768]{3,2,1,0:T(8,128)S(1)} %pad_add_fusion.refs_0_), channel_id=1, source_target_pairs={{0,32},{16,112},{32,64},{48,16},{64,96},{80,48},{96,0},{112,80},{1... | collective-permute-start | bytes 8257544 | tf_op jit(solution)/shard_map/ppermute | solution.py:39
  20.2 14.9 %copy-start.9 = (f32[4,224,768]{2,1,0:T(8,128)S(1)}, f32[4,224,768]{2,1,0:T(8,128)}, u32[]{:S(2)}) copy-start(f32[4,224,768]{2,1,0:T(8,128)} %get-tuple-element.75) | copy-start | bytes 8257540
  35.1 2.0 %copy-start.12 = (f32[4,224,768]{2,1,0:T(8,128)S(1)}, f32[4,224,768]{2,1,0:T(8,128)}, u32[]{:S(2)}) copy-start(f32[4,224,768]{2,1,0:T(8,128)} %get-tuple-element.74) | copy-start | bytes 8257540
  35.5 20.7 %copy-start.10 = (f32[4,224,768]{2,1,0:T(8,128)S(1)}, f32[4,224,768]{2,1,0:T(8,128)}, u32[]{:S(2)}) copy-start(f32[4,224,768]{2,1,0:T(8,128)} %get-tuple-element.81) | copy-start | bytes 8257540
  35.6 18.4 %collective-permute-start.5 = (f16[4,224,768]{2,1,0:T(8,128)(2,1)S(1)}, f16[4,224,768]{2,1,0:T(8,128)(2,1)S(1)}, u32[]{:S(2)}, u32[]{:S(2)}) collective-permute-start(f16[4,224,768]{2,1,0:T(8,128)(2,1)S(1)} %add_convert_fusion.1), channel_id=1, source_target_pairs={{0,4},{1,5},{2,6},{3,7},{4,8},{5,9},{6,10},{7,11},{8,12},{9,13},{1... | collective-permute-start | bytes 4128776 | tf_op jit(solution)/shard_map/ppermute | solution.py:30
  37.2 17.8 %collective-permute-start.4 = (f16[4,224,768]{2,1,0:T(8,128)(2,1)S(1)}, f16[4,224,768]{2,1,0:T(8,128)(2,1)S(1)}, u32[]{:S(2)}, u32[]{:S(2)}) collective-permute-start(f16[4,224,768]{2,1,0:T(8,128)(2,1)S(1)} %convert_element_type.139), channel_id=1, source_target_pairs={{0,12},{1,13},{2,14},{3,15},{4,0},{5,1},{6,2},{7,3},{8,4},{9,5},{1... | collective-permute-start | bytes 4128776 | tf_op jit(solution)/shard_map/ppermute | solution.py:30
  55.0 40.6 %collective-permute-start.9 = (s32[2,2,224,768]{3,2,1,0:T(8,128)}, s32[2,2,224,768]{3,2,1,0:T(8,128)}, u32[]{:S(2)}, u32[]{:S(2)}) collective-permute-start(s32[2,2,224,768]{3,2,1,0:T(8,128)} %collective-permute-done.3.refs_1_), channel_id=1, source_target_pairs={{0,16},{16,0},{32,48},{48,32},{64,80},{80,64},{96,112},{112,96},{1... | collective-permute-start | bytes 8257544 | tf_op jit(solution)/shard_map/ppermute | solution.py:345
  56.3 6.3 %copy-start.11 = (f32[4,224,768]{2,1,0:T(8,128)S(1)}, f32[4,224,768]{2,1,0:T(8,128)}, u32[]{:S(2)}) copy-start(f32[4,224,768]{2,1,0:T(8,128)} %get-tuple-element.83) | copy-start | bytes 8257540
  56.8 6.2 %copy-start.7 = (f32[4,224,768]{2,1,0:T(8,128)S(1)}, f32[4,224,768]{2,1,0:T(8,128)}, u32[]{:S(2)}) copy-start(f32[4,224,768]{2,1,0:T(8,128)} %get-tuple-element.73) | copy-start | bytes 8257540
  56.8 27.9 %collective-permute-start.6 = (f16[4,224,768]{2,1,0:T(8,128)(2,1)S(1)}, f16[4,224,768]{2,1,0:T(8,128)(2,1)S(1)}, u32[]{:S(2)}, u32[]{:S(2)}) collective-permute-start(f16[4,224,768]{2,1,0:T(8,128)(2,1)S(1)} %add_convert_fusion), channel_id=1, source_target_pairs={{0,12},{1,13},{2,14},{3,15},{4,0},{5,1},{6,2},{7,3},{8,4},{9,5},{1... | collective-permute-start | bytes 4128776 | tf_op jit(solution)/shard_map/ppermute | solution.py:30
  62.0 22.6 %collective-permute-start.8 = (s32[2,224,768]{2,1,0:T(8,128)S(1)}, s32[2,224,768]{2,1,0:T(8,128)}, u32[]{:S(2)}, u32[]{:S(2)}) collective-permute-start(s32[2,224,768]{2,1,0:T(8,128)S(1)} %slice_bitcast_fusion), channel_id=1, source_target_pairs={{0,32},{16,112},{32,64},{48,16},{64,96},{80,48},{96,0},{112,80},{1... | collective-permute-start | bytes 4128776 | tf_op jit(solution)/shard_map/ppermute | solution.py:39
  62.8 25.8 %collective-permute-start.7 = (f16[4,224,768]{2,1,0:T(8,128)(2,1)S(1)}, f16[4,224,768]{2,1,0:T(8,128)(2,1)S(1)}, u32[]{:S(2)}, u32[]{:S(2)}) collective-permute-start(f16[4,224,768]{2,1,0:T(8,128)(2,1)S(1)} %convert_element_type.147), channel_id=1, source_target_pairs={{0,4},{1,5},{2,6},{3,7},{4,8},{5,9},{6,10},{7,11},{8,12},{9,13},{1... | collective-permute-start | bytes 4128776 | tf_op jit(solution)/shard_map/ppermute | solution.py:30
  63.5 25.1 %copy-start.8 = (f32[4,224,768]{2,1,0:T(8,128)S(1)}, f32[4,224,768]{2,1,0:T(8,128)}, u32[]{:S(2)}) copy-start(f32[4,224,768]{2,1,0:T(8,128)} %get-tuple-element.72) | copy-start | bytes 8257540
  88.6 11.7 %collective-permute-start.13 = (s32[2,224,768]{2,1,0:T(8,128)}, s32[2,224,768]{2,1,0:T(8,128)}, u32[]{:S(2)}, u32[]{:S(2)}) collective-permute-start(s32[2,224,768]{2,1,0:T(8,128)} %collective-permute-done.8.refs_3_), channel_id=1, source_target_pairs={{0,16},{16,0},{32,48},{48,32},{64,80},{80,64},{96,112},{112,96},{1... | collective-permute-start | bytes 4128776 | tf_op jit(solution)/shard_map/ppermute | solution.py:345
  90.3 9.1 %copy-start.16 = (s32[4]{0:T(128)S(1)}, s32[4]{0:T(128)}, u32[]{:S(2)}) copy-start(s32[4]{0:T(128)} %constant.106.clone) | copy-start | bytes 52
  90.3 9.1 %copy-start.15 = (s32[8,2]{0,1:T(2,128)S(1)}, s32[8,2]{0,1:T(2,128)}, u32[]{:S(2)}) copy-start(s32[8,2]{0,1:T(2,128)} %param.12) | copy-start | bytes 196
  90.3 15.9 %all-to-all-start.1 = ((f16[4,224,768]{2,1,0:T(8,128)(2,1)}), f16[4,224,768]{2,1,0:T(8,128)(2,1)S(1)}, u32[]{:S(2)}, u32[]{:S(2)}) async-start(f16[4,224,768]{2,1,0:T(8,128)(2,1)} %multiply_convert_fusion), calls=%async_computation.1 | async-start | bytes 2752512 | tf_op jit(solution)/shard_map/all_to_all | solution.py:207
  95.9 16.8 %collective-permute-start.10 = (f16[224,768]{1,0:T(8,128)(2,1)S(1)}, f16[224,768]{1,0:T(8,128)(2,1)S(1)}, u32[]{:S(2)}, u32[]{:S(2)}) collective-permute-start(f16[224,768]{1,0:T(8,128)(2,1)S(1)} %multiply_convert_fusion.3), channel_id=1, source_target_pairs={{0,32},{16,48},{32,64},{48,80},{64,96},{80,112},{96,0},{112,16},{1... | collective-permute-start | bytes 1032200 | tf_op jit(solution)/shard_map/ppermute | solution.py:349
  98.1 18.0 %collective-permute-start.11 = (f16[224,768]{1,0:T(8,128)(2,1)S(1)}, f16[224,768]{1,0:T(8,128)(2,1)S(1)}, u32[]{:S(2)}, u32[]{:S(2)}) collective-permute-start(f16[224,768]{1,0:T(8,128)(2,1)S(1)} %multiply_convert_fusion.3), channel_id=1, source_target_pairs={{0,96},{16,112},{32,0},{48,16},{64,32},{80,48},{96,64},{112,80},{1... | collective-permute-start | bytes 1032200 | tf_op jit(solution)/shard_map/ppermute | solution.py:349
  98.1 18.0 %collective-permute-start.12 = (f16[224,768]{1,0:T(8,128)(2,1)S(1)}, f16[224,768]{1,0:T(8,128)(2,1)S(1)}, u32[]{:S(2)}, u32[]{:S(2)}) collective-permute-start(f16[224,768]{1,0:T(8,128)(2,1)S(1)} %multiply_convert_fusion.3), channel_id=1, source_target_pairs={{0,64},{16,80},{32,96},{48,112},{64,0},{80,16},{96,32},{112,48},{1... | collective-permute-start | bytes 1032200 | tf_op jit(solution)/shard_map/ppermute | solution.py:349
  103.2 1.9 %copy-start.1 = (f32[3,2,224,768]{3,2,1,0:T(8,128)}, f32[3,2,224,768]{3,2,1,0:T(8,128)S(1)}, u32[]{:S(2)}) copy-start(f32[3,2,224,768]{3,2,1,0:T(8,128)S(1)} %shard_map.122.held) | copy-start | bytes 12386308
  116.4 9.4 %collective-permute-start.18 = (f16[224,768]{1,0:T(8,128)(2,1)S(1)}, f16[224,768]{1,0:T(8,128)(2,1)S(1)}, u32[]{:S(2)}, u32[]{:S(2)}) collective-permute-start(f16[224,768]{1,0:T(8,128)(2,1)S(1)} %multiply_convert_fusion.2), channel_id=1, source_target_pairs={{0,32},{16,48},{32,64},{48,80},{64,96},{80,112},{96,0},{112,16},{1... | collective-permute-start | bytes 1032200 | tf_op jit(solution)/shard_map/ppermute | solution.py:349
  116.5 17.9 %collective-permute-start.19 = (f16[224,768]{1,0:T(8,128)(2,1)S(1)}, f16[224,768]{1,0:T(8,128)(2,1)S(1)}, u32[]{:S(2)}, u32[]{:S(2)}) collective-permute-start(f16[224,768]{1,0:T(8,128)(2,1)S(1)} %multiply_convert_fusion.2), channel_id=1, source_target_pairs={{0,96},{16,112},{32,0},{48,16},{64,32},{80,48},{96,64},{112,80},{1... | collective-permute-start | bytes 1032200 | tf_op jit(solution)/shard_map/ppermute | solution.py:349
  117.9 17.7 %collective-permute-start.20 = (f16[224,768]{1,0:T(8,128)(2,1)S(1)}, f16[224,768]{1,0:T(8,128)(2,1)S(1)}, u32[]{:S(2)}, u32[]{:S(2)}) collective-permute-start(f16[224,768]{1,0:T(8,128)(2,1)S(1)} %multiply_convert_fusion.2), channel_id=1, source_target_pairs={{0,64},{16,80},{32,96},{48,112},{64,0},{80,16},{96,32},{112,48},{1... | collective-permute-start | bytes 1032200 | tf_op jit(solution)/shard_map/ppermute | solution.py:349
  118.3 17.7 %collective-permute-start.21 = (f16[224,768]{1,0:T(8,128)(2,1)S(1)}, f16[224,768]{1,0:T(8,128)(2,1)S(1)}, u32[]{:S(2)}, u32[]{:S(2)}) collective-permute-start(f16[224,768]{1,0:T(8,128)(2,1)S(1)} %multiply_convert_fusion.2), channel_id=1, source_target_pairs={{0,16},{16,0},{32,48},{48,32},{64,80},{80,64},{96,112},{112,96},{1... | collective-permute-start | bytes 1032200 | tf_op jit(solution)/shard_map/ppermute | solution.py:345
  119.4 16.6 %collective-permute-start.14 = (f16[224,768]{1,0:T(8,128)(2,1)S(1)}, f16[224,768]{1,0:T(8,128)(2,1)S(1)}, u32[]{:S(2)}, u32[]{:S(2)}) collective-permute-start(f16[224,768]{1,0:T(8,128)(2,1)S(1)} %multiply_convert_fusion.3), channel_id=1, source_target_pairs={{0,16},{16,0},{32,48},{48,32},{64,80},{80,64},{96,112},{112,96},{1... | collective-permute-start | bytes 1032200 | tf_op jit(solution)/shard_map/ppermute | solution.py:345
  125.8 10.3 %collective-permute-start.15 = (f16[224,768]{1,0:T(8,128)(2,1)S(1)}, f16[224,768]{1,0:T(8,128)(2,1)S(1)}, u32[]{:S(2)}, u32[]{:S(2)}) collective-permute-start(f16[224,768]{1,0:T(8,128)(2,1)S(1)} %collective-permute-done.10), channel_id=1, source_target_pairs={{0,16},{16,0},{32,48},{48,32},{64,80},{80,64},{96,112},{112,96},{1... | collective-permute-start | bytes 1032200 | tf_op jit(solution)/shard_map/ppermute | solution.py:345
  134.4 2.5 %collective-permute-start.16 = (f16[224,768]{1,0:T(8,128)(2,1)S(1)}, f16[224,768]{1,0:T(8,128)(2,1)S(1)}, u32[]{:S(2)}, u32[]{:S(2)}) collective-permute-start(f16[224,768]{1,0:T(8,128)(2,1)S(1)} %collective-permute-done.11), channel_id=1, source_target_pairs={{0,16},{16,0},{32,48},{48,32},{64,80},{80,64},{96,112},{112,96},{1... | collective-permute-start | bytes 1032200 | tf_op jit(solution)/shard_map/ppermute | solution.py:345
  135.6 1.8 %collective-permute-start.17 = (f16[224,768]{1,0:T(8,128)(2,1)S(1)}, f16[224,768]{1,0:T(8,128)(2,1)S(1)}, u32[]{:S(2)}, u32[]{:S(2)}) collective-permute-start(f16[224,768]{1,0:T(8,128)(2,1)S(1)} %collective-permute-done.12), channel_id=1, source_target_pairs={{0,16},{16,0},{32,48},{48,32},{64,80},{80,64},{96,112},{112,96},{1... | collective-permute-start | bytes 1032200 | tf_op jit(solution)/shard_map/ppermute | solution.py:345
  137.4 2.5 %collective-permute-start.22 = (f16[224,768]{1,0:T(8,128)(2,1)S(1)}, f16[224,768]{1,0:T(8,128)(2,1)S(1)}, u32[]{:S(2)}, u32[]{:S(2)}) collective-permute-start(f16[224,768]{1,0:T(8,128)(2,1)S(1)} %collective-permute-done.18), channel_id=1, source_target_pairs={{0,16},{16,0},{32,48},{48,32},{64,80},{80,64},{96,112},{112,96},{1... | collective-permute-start | bytes 1032200 | tf_op jit(solution)/shard_map/ppermute | solution.py:345
  137.7 2.1 %collective-permute-start.23 = (f16[224,768]{1,0:T(8,128)(2,1)S(1)}, f16[224,768]{1,0:T(8,128)(2,1)S(1)}, u32[]{:S(2)}, u32[]{:S(2)}) collective-permute-start(f16[224,768]{1,0:T(8,128)(2,1)S(1)} %collective-permute-done.19), channel_id=1, source_target_pairs={{0,16},{16,0},{32,48},{48,32},{64,80},{80,64},{96,112},{112,96},{1... | collective-permute-start | bytes 1032200 | tf_op jit(solution)/shard_map/ppermute | solution.py:345
  137.9 2.1 %collective-permute-start.24 = (f16[224,768]{1,0:T(8,128)(2,1)S(1)}, f16[224,768]{1,0:T(8,128)(2,1)S(1)}, u32[]{:S(2)}, u32[]{:S(2)}) collective-permute-start(f16[224,768]{1,0:T(8,128)(2,1)S(1)} %collective-permute-done.20), channel_id=1, source_target_pairs={{0,16},{16,0},{32,48},{48,32},{64,80},{80,64},{96,112},{112,96},{1... | collective-permute-start | bytes 1032200 | tf_op jit(solution)/shard_map/ppermute | solution.py:345
  140.6 1.2 copy-start.3
  140.6 1.3 copy-start.4
  140.6 1.5 %copy-start.5 = (f32[1,224,768]{2,1,0:T(8,128)S(1)}, f32[1,224,768]{2,1,0:T(8,128)}, u32[]{:S(2)}) copy-start(f32[1,224,768]{2,1,0:T(8,128)} %param.16) | copy-start | bytes 2064388
  141.2 2.3 %copy-start.2 = (f32[3,2,224,768]{3,2,1,0:T(8,128)S(1)}, f32[3,2,224,768]{3,2,1,0:T(8,128)}, u32[]{:S(2)}) copy-start(f32[3,2,224,768]{3,2,1,0:T(8,128)} %copy-done.1) | copy-start | bytes 12386308
